TPU v7x, 32 devices: a whole 2x2x4 slice. The times are simulated.
32 devices in a mesh: elec: 8 (over y, x, core), drop: 4 (over z).
Axes of the slice: x: 2, y: 2, z: 4, core: 2. Of those that a mesh axis runs over, the one named last changes fastest.
Arguments:
- elec_pos: float32 [3, 4096], P(None, 'elec'), may hold values from -3 to 3
- drop_vert: float32 [3, 4096], P(None, 'drop'), may hold values from -4 to 4
- drop_conn: int32 [3, 8192], P(None, 'drop'), may hold values from 0 to 4095, as said below
- elec_rhs: float32 [128, 4096], P(None, 'elec'), may hold values from -6 to 6
- drop_rhs: float32 [128, 8192], P(None, 'drop'), may hold values from -6 to 6
- elec_inv: float32 [32, 128, 128], P('elec')
- drop_inv: float32 [64, 128, 128], P('drop')
Outputs:
- charge_elec: float32 [128, 4096], P(None, 'elec')
- charge_drop: float32 [128, 8192], P(None, 'drop')
Inputs may be any that keep to these rules, and one draw needn't show every extreme that they name: `drop_conn`: panel p's three vertices all lie in vertex block p // 2048, that is among vertices (1024) * (p // 2048) to 1024 * (p // 2048 + 1) - 1; every vertex is the first vertex of exactly two panels of its block.
All inputs are finite; a program needn't handle non-finite values.
Results may differ from a plain program's by a relative error of at most 0.0001.
Values sent between devices are 32-bit elements; how exact they have to be, the bound alone decides.
No kernel may reach another device: no remote copies, remote signals or barrier semaphores. Data moves between devices by JAX's collectives and lax.ppermute only.
A program may use at most 64 MiB of HBM per device.

v0:
```python
import math

import jax
import jax.numpy as jnp
from jax import lax
from jax.sharding import PartitionSpec as P

ITERS = 2


HIGH = lax.Precision.HIGHEST


def constants(total_drop):
    screen = 1.0
    soften = 0.001
    couple = 1.0 / (3.0 * math.sqrt(total_drop))
    return (screen, soften, couple)


def centroids(drop_vert, conn):
    corners = jnp.take(drop_vert, conn, axis=1)
    return (corners[:, 0] + corners[:, 1] + corners[:, 2]) / 3.0


def kernel_tile(position, centres, screen, soften, couple):
    delta_x = position[0][:, None] - centres[0][None, :]
    delta_y = position[1][:, None] - centres[1][None, :]
    delta_z = position[2][:, None] - centres[2][None, :]
    distance = jnp.sqrt(delta_x * delta_x + delta_y * delta_y + delta_z * delta_z + soften)
    return couple * jnp.exp(-screen * distance) / distance


def block_solve(inverse, values):
    rhs_rows, columns = values.shape
    block_count, block_size, _ = inverse.shape
    shaped = values.reshape(rhs_rows, block_count, block_size)
    solved = jnp.einsum("bjk,rbk->rbj", inverse, shaped, precision=HIGH)
    return solved.reshape(rhs_rows, columns)


def on_device(elec_pos, drop_vert, drop_conn, elec_rhs, drop_rhs, elec_inv, drop_inv):
    drop_devices = lax.axis_size("drop")
    rhs_count, elec_local = elec_rhs.shape
    drop_local = drop_rhs.shape[1]
    screen, soften, couple = constants(drop_local * drop_devices)
    half_block = drop_vert.shape[1]
    local_conn = drop_conn - lax.axis_index("drop") * half_block
    centres = centroids(drop_vert, local_conn)
    block_rows = math.gcd(elec_local, 512)
    block_count = elec_local // block_rows
    elec_blocks = jnp.moveaxis(elec_pos.reshape(3, block_count, block_rows), 1, 0)

    def kernel_at(position):
        return kernel_tile(position, centres, screen, soften, couple)

    def to_elec_of(charge_drop, kernel):
        return lax.dot_general(charge_drop, kernel, (((1,), (1,)), ((), ())), precision=HIGH)

    charge_elec = block_solve(elec_inv, elec_rhs)
    charge_drop = block_solve(drop_inv, drop_rhs)
    for iteration in range(ITERS):
        charge_blocks = jnp.moveaxis(charge_elec.reshape(rhs_count, block_count, block_rows), 1, 0)
        start_sum = jnp.zeros((rhs_count, drop_local), jnp.float32)
        pieces = lax.map(lambda position: to_elec_of(charge_drop, kernel_at(position)), elec_blocks)

        def add_block(summed, inputs):
            position, charge_part = inputs
            return (summed + jnp.dot(charge_part, kernel_at(position), precision=HIGH), None)

        part_drop, _ = lax.scan(add_block, start_sum, (elec_blocks, charge_blocks))
        part_elec = jnp.moveaxis(pieces, 0, 1).reshape(rhs_count, elec_local)
        part_elec, part_drop = (part_elec, part_drop)
        field_elec = lax.psum(part_elec, "drop")
        field_drop = lax.psum(part_drop, "elec")
        charge_elec = block_solve(elec_inv, elec_rhs - field_elec)
        charge_drop = block_solve(drop_inv, drop_rhs - field_drop)
    return (charge_elec, charge_drop)


def solution(mesh):
    placed = (
        P(None, "elec"),
        P(None, "drop"),
        P(None, "drop"),
        P(None, "elec"),
        P(None, "drop"),
        P("elec", None, None),
        P("drop", None, None),
    )
    return jax.shard_map(
        on_device,
        mesh=mesh,
        in_specs=placed,
        out_specs=(P(None, "elec"), P(None, "drop")),
        check_vma=False,
    )
```

profile of v0, /device:TPU:0, one launch (start us, length us, event | category | flops | bytes accessed | tf_op | source)
XLA Modules:
  0.0 208.2 jit_solution(7794309949813763590)
XLA Ops:
  7.2 0.0 copy-start
  7.2 0.0 copy-start.4
  7.2 0.0 copy-start.1
  7.2 0.0 all-reduce.7.cloned.1.call-start
  7.2 0.9 compare_and_fusion
  8.2 0.9 copy.19
  9.2 20.9 %gather_fusion = f32[6144,3]{1,0:T(8,128)} fusion(f32[3,1024]{0,1:T(8,128)S(1)} %copy.19, s32[6144]{0:T(1024)S(1)} %broadcast_clamp_fusion), kind=kCustom, calls=%fused_computation | custom fusion | bytes 172032 | tf_op jit(solution)/shard_map/jit(_take)/gather | solution.py:22
  30.1 2.7 %copy.20 = f32[3,2048,3]{1,0,2:T(4,128)S(1)} copy(f32[3,2048,3]{2,1,0:T(8,128)} %bitcast.76) | data formatting | bytes 147456 | tf_op jit(solution)/shard_map/jit(_take)/gather | solution.py:22
  32.8 0.1 fusion.22
  32.8 0.0 copy-done.4
  32.9 0.0 copy-done
  32.9 0.0 copy-done.1
  32.9 2.3 %fusion.7 = f32[16,128,128]{1,2,0:T(8,128)S(1)} fusion(f32[16,128,128]{2,1,0:T(8,128)S(1)} %copy-done, f32[128,2048]{1,0:T(8,128)S(1)} %copy-done.1), kind=kOutput, calls=%fused_computation.9 | convolution fusion | flops 402653184 | bytes 3145728 | tf_op jit(solution)/shard_map/bjk,rbk->rbj/dot_general | solution.py:38
  35.2 0.0 copy-start.2
  35.2 0.0 copy-start.3
  35.2 8.5 %fusion.1 = f32[128,512]{1,0:T(8,128)} fusion(f32[128,2048]{0,1:T(8,128)S(1)} %bitcast.78, f32[2048]{0:T(1024)S(1)} %bitcast.86, f32[512]{0:T(512)S(1)} %bitcast.98, f32[2048]{0:T(1024)S(1)} %bitcast.90, f32[512]{0:T(512)S(1)} %bitcast.102, f32[2048]{0:T(1024)S(1)} %bitcast.82, f32[512]{0:T(512)S(1)} %bitcast.94), kind=kOutput, calls=%fused_computation.3 | convolution fusion | flops 1623195648 | bytes 1341440 | tf_op jit(solution)/shard_map/while/body/eval_jaxpr/dot_general | solution.py:58
  43.7 0.0 all-reduce.7.cloned.1.call-update
  43.7 0.2 all-reduce.9.cloned.1.call-start
  44.0 0.0 copy-done.2
  44.0 0.0 copy-done.3
  44.0 0.7 fusion.19
  44.6 6.8 %fusion.3 = f32[128,2048]{1,0:T(8,128)} fusion(f32[128,512]{0,1:T(8,128)S(1)} %bitcast.80, f32[2048]{0:T(1024)S(1)} %bitcast.87, f32[512]{0:T(512)S(1)} %bitcast.99, f32[2048]{0:T(1024)S(1)} %bitcast.91, f32[512]{0:T(512)S(1)} %bitcast.103, f32[2048]{0:T(1024)S(1)} %bitcast.83, f32[512]{0:T(512)S(1)} %bitcast.95), kind=kOutput, calls=%fused_computation.5 | convolution fusion | flops 1623195648 | bytes 1341440 | tf_op jit(solution)/shard_map/while/body/eval_jaxpr/dot_general | solution.py:69
  51.5 30.4 %all-reduce.7.cloned.1.call-done = f32[128,512]{1,0:T(8,128)} async-done(((f32[128,512]{1,0:T(8,128)}), f32[128,512]{1,0:T(8,128)}) %all-reduce.7.cloned.1.call-update) | async-done | bytes 262160 | tf_op jit(solution)/shard_map/psum | solution.py:74
  81.9 1.6 fusion.13
  83.5 7.1 %fusion = f32[128,2048]{1,0:T(8,128)} fusion(f32[128,512]{0,1:T(8,128)S(1)} %bitcast.81, f32[2048]{0:T(1024)S(1)} %bitcast.88, f32[512]{0:T(512)S(1)} %bitcast.100, f32[2048]{0:T(1024)S(1)} %bitcast.92, f32[512]{0:T(512)S(1)} %bitcast.104, f32[2048]{0:T(1024)S(1)} %bitcast.84, f32[512]{0:T(512)S(1)} %bitcast.96), kind=kOutput, calls=%fused_computation.2 | convolution fusion | flops 1623195648 | bytes 1341440 | tf_op jit(solution)/shard_map/while/body/eval_jaxpr/dot_general | solution.py:69
  90.5 0.0 all-reduce.9.cloned.1.call-update
  90.6 0.0 all-reduce.5.cloned.1.call-start
  90.6 61.4 %all-reduce.9.cloned.1.call-done = (f32[128,2048]{1,0:T(8,128)}, f32[128,2048]{1,0:T(8,128)}) async-done(((f32[128,2048]{1,0:T(8,128)}, f32[128,2048]{1,0:T(8,128)}), (f32[128,2048]{1,0:T(8,128)}, f32[128,2048]{1,0:T(8,128)})) %all-reduce.9.cloned.1.call-update) | async-done | bytes 2097168 | tf_op jit(solution)/shard_map/psum | solution.py:75
  152.0 1.7 subtract_bitcast_fusion
  153.7 2.3 %fusion.10 = f32[16,128,128]{1,2,0:T(8,128)S(1)} fusion(f32[16,128,128]{2,1,0:T(8,128)S(1)} %copy-done, f32[16,16,8,128]{3,2,1,0:T(8,128)S(1)} %get-tuple-element.61), kind=kOutput, calls=%fused_computation.12 | convolution fusion | flops 402653184 | bytes 3145728 | tf_op jit(solution)/shard_map/bjk,rbk->rbj/dot_general | solution.py:38
  156.0 8.4 %fusion.2 = f32[128,512]{1,0:T(8,128)} fusion(f32[128,2048]{0,1:T(8,128)S(1)} %bitcast.77, f32[2048]{0:T(1024)S(1)} %bitcast.89, f32[512]{0:T(512)S(1)} %bitcast.101, f32[2048]{0:T(1024)S(1)} %bitcast.93, f32[512]{0:T(512)S(1)} %bitcast.105, f32[2048]{0:T(1024)S(1)} %bitcast.85, f32[512]{0:T(512)S(1)} %bitcast.97), kind=kOutput, calls=%fused_computation.4 | convolution fusion | flops 1623195648 | bytes 1341440 | tf_op jit(solution)/shard_map/while/body/eval_jaxpr/dot_general | solution.py:58
  164.4 0.0 all-reduce.5.cloned.1.call-update
  164.5 2.3 %fusion.4 = f32[16,128,128]{1,2,0:T(8,128)S(1)} fusion(f32[16,128,128]{2,1,0:T(8,128)S(1)} %copy-done, f32[16,16,8,128]{3,2,1,0:T(8,128)S(1)} %get-tuple-element.60), kind=kOutput, calls=%fused_computation.6 | convolution fusion | flops 402653184 | bytes 3145728 | tf_op jit(solution)/shard_map/bjk,rbk->rbj/dot_general | solution.py:38
  166.8 1.3 copy.27
  168.1 31.1 %all-reduce.5.cloned.1.call-done = f32[128,512]{1,0:T(8,128)} async-done(((f32[128,512]{1,0:T(8,128)}), f32[128,512]{1,0:T(8,128)}) %all-reduce.5.cloned.1.call-update) | async-done | bytes 262160 | tf_op jit(solution)/shard_map/psum | solution.py:74
  199.1 1.7 fusion.16
  200.8 0.8 copy.26
  (5 shorter events, 0.1 us)
Async XLA Ops:
  7.2 25.7 %copy-start = (f32[16,128,128]{2,1,0:T(8,128)S(1)}, f32[16,128,128]{2,1,0:T(8,128)}, u32[]{:S(2)}) copy-start(f32[16,128,128]{2,1,0:T(8,128)} %param.13) | copy-start | bytes 3145732
  7.2 25.7 %copy-start.4 = (f32[3,512]{1,0:T(4,128)S(1)}, f32[3,512]{1,0:T(4,128)}, u32[]{:S(2)}) copy-start(f32[3,512]{1,0:T(4,128)} %param.7) | copy-start | bytes 18436
  7.2 25.7 %copy-start.1 = (f32[128,2048]{1,0:T(8,128)S(1)}, f32[128,2048]{1,0:T(8,128)}, u32[]{:S(2)}) copy-start(f32[128,2048]{1,0:T(8,128)} %param.11) | copy-start | bytes 3145732
  7.2 74.7 %all-reduce.7.cloned.1.call-start = ((), (), s32[]{:S(2)}) async-start(), calls=%async_computation.1 | async-start | bytes 524288 | tf_op jit(solution)/shard_map/psum | solution.py:74
  35.2 8.8 %copy-start.2 = (f32[4,128,128]{2,1,0:T(8,128)S(1)}, f32[4,128,128]{2,1,0:T(8,128)}, u32[]{:S(2)}) copy-start(f32[4,128,128]{2,1,0:T(8,128)} %param.12) | copy-start | bytes 786436
  35.2 8.8 %copy-start.3 = (f32[128,512]{1,0:T(8,128)S(1)}, f32[128,512]{1,0:T(8,128)}, u32[]{:S(2)}) copy-start(f32[128,512]{1,0:T(8,128)} %param.10) | copy-start | bytes 786436
  43.7 108.3 %all-reduce.9.cloned.1.call-start = ((), (), s32[]{:S(2)}) async-start(), calls=%async_computation.2 | async-start | bytes 4194304 | tf_op jit(solution)/shard_map/psum | solution.py:75
  90.6 108.6 %all-reduce.5.cloned.1.call-start = ((), (), s32[]{:S(2)}) async-start(), calls=%async_computation | async-start | bytes 524288 | tf_op jit(solution)/shard_map/psum | solution.py:74
Sparse Core Ops, SparseCore 0:
  43.8 37.9 all-reduce.6
  90.7 61.2 all-reduce.8
  164.6 34.5 all-reduce.4
where the time goes:
time: 208 us
  waiting for transfers between devices  123 us (59%)
  matrix products  41.6 us (20%)
  local copies, waits for them, and re-layouts  26.7 us (13%)
  between operations  13.9 us (7%)
  other arithmetic  2.73 us (1%)
    psum x2, waiting for transfers between devices, on_device(): field_elec = lax.psum(part_elec, 'drop')  61.5 us
    psum x1, waiting for transfers between devices, on_device(): field_drop = lax.psum(part_drop, 'elec')  61.4 us
    gather x2, local copies, waits for them, and re-layouts, centroids(): corners = jnp.take(drop_vert, conn, axis=1)  23.6 us
    dot_general x2, matrix products, to_elec_of(): lax.dot_general(charge_drop, kernel, (((1,), (1,)), ((), ())), precision=...  16.9 us
    dot_general x2, matrix products, add_block(): jnp.dot(charge_part, kernel_at(position), precision=HIGH)  13.9 us
    dot_general x6, matrix products, block_solve(): solved = jnp.einsum('bjk,rbk->rbj', inverse, shaped, precision=HIGH)  10.9 us
  transfers between devices with their start and end apart: 3, of which 3 were waited for; matrix products, arithmetic and copies ran while one was open for 5% of the time, Pallas kernels for 0%

commit v1 on v0

v1 whole, which is shorter than its diff:
```python
import math

import jax
import jax.numpy as jnp
from jax import lax
from jax.experimental import pallas as pl
from jax.experimental.pallas import tpu as pltpu
from jax.sharding import PartitionSpec as P

SOFTEN = 0.001
SCREEN = 1.0
LANES = 128
CHUNK = 256
VMEM = pl.BlockSpec(memory_space=pltpu.VMEM)
SMEM = pl.BlockSpec(memory_space=pltpu.SMEM)
PARAMS = pltpu.CompilerParams(vmem_limit_bytes=40 * 2**20)
ROWS_IN = ((1,), (0,))
ROWS_OUT = ((1,), (1,))


def couple_of(total_drop):
    return 1.0 / (3.0 * math.sqrt(total_drop))


def split(value):
    high = value.astype(jnp.bfloat16)
    low = (value - high.astype(jnp.float32)).astype(jnp.bfloat16)
    return high, low


def stacked(value):
    high, low = split(value)
    return high, jnp.concatenate([high, low], axis=0)


def product(charge, weights, contract):
    high, both = charge
    weight_high, weight_low = weights
    dims = (contract, ((), ()))
    first = lax.dot_general(both, weight_high, dims, preferred_element_type=jnp.float32)
    second = lax.dot_general(high, weight_low, dims, preferred_element_type=jnp.float32)
    rows = high.shape[0]
    return first[:rows] + (first[rows:] + second)


def solve_block(inverse, values):
    return product(stacked(values), split(inverse), ROWS_OUT)


def gather_row(vert_ref, index):
    tiles = vert_ref.shape[1] // LANES
    lane, tile = index % LANES, index // LANES
    found = []
    for axis in range(3):
        total = jnp.zeros(index.shape, jnp.float32)
        for at in range(tiles):
            table = jnp.broadcast_to(vert_ref[axis : axis + 1, at * LANES : (at + 1) * LANES], index.shape)
            total = jnp.where(tile == at, jnp.take_along_axis(table, lane, axis=1), total)
        found.append(total)
    return found


def first_kernel(couple, core_ref, pos_ref, vert_ref, conn_ref, erhs_ref, drhs_ref, einv_ref, dinv_ref,
                 high_ref, low_ref, elec_ref, keep_ref, send_ref, place, centre, wide, held_d, both_d, field):
    elec, drop = high_ref.shape
    rows = erhs_ref.shape[0]
    half = drop // 2
    half_block = vert_ref.shape[1]
    for at in range(drop // LANES):
        cols = slice(at * LANES, (at + 1) * LANES)
        corners = gather_row(vert_ref, conn_ref[:, cols] % half_block)
        for axis in range(3):
            g = corners[axis]
            centre[axis : axis + 1, cols] = (g[0:1] + g[1:2] + g[2:3]) / 3.0
    place[...] = jnp.zeros_like(place)
    place[0:3, :] = pos_ref[...]
    upright = place[...].T
    for axis in range(3):
        wide[axis] = jnp.broadcast_to(upright[:, axis : axis + 1], (elec, LANES))
    pieces = []
    for at in range(elec // LANES):
        pieces.append(solve_block(einv_ref[at], erhs_ref[:, at * LANES : (at + 1) * LANES]))
    charge_elec = stacked(jnp.concatenate(pieces, axis=1))
    for at in range(drop // LANES):
        cols = slice(at * LANES, (at + 1) * LANES)
        solved = solve_block(dinv_ref[at], drhs_ref[:, cols])
        high, both = stacked(solved)
        both_d[:, cols] = both
    total = jnp.zeros((rows, elec), jnp.float32)
    for at in range(drop // CHUNK):
        cols = slice(at * CHUNK, (at + 1) * CHUNK)
        tiles = []
        for lane in range(at * CHUNK, (at + 1) * CHUNK, LANES):
            here = slice(lane, lane + LANES)
            dx = wide[0] - centre[0:1, here]
            dy = wide[1] - centre[1:2, here]
            dz = wide[2] - centre[2:3, here]
            square = dx * dx + dy * dy + dz * dz + SOFTEN
            inverse = lax.rsqrt(square)
            tiles.append(jnp.exp((square * inverse) * -SCREEN) * inverse)
        weights = split(jnp.concatenate(tiles, axis=1))
        high_ref[:, cols], low_ref[:, cols] = weights
        both = both_d[:, cols]
        total = total + product((both[:rows], both), weights, ROWS_OUT)
        field[:, cols] = product(charge_elec, weights, ROWS_IN) * couple
    elec_ref[...] = total * couple
    mine = pl.multiple_of(core_ref[0] * half, half)
    other = pl.multiple_of((1 - core_ref[0]) * half, half)
    keep_ref[...] = field[:, pl.ds(mine, half)]
    send_ref[...] = field[:, pl.ds(other, half)]


def first(core, couple, elec_pos, drop_vert, drop_conn, elec_rhs, drop_rhs, elec_inv, drop_inv):
    rows, elec = elec_rhs.shape
    drop = drop_rhs.shape[1]
    return pl.pallas_call(
        lambda *refs: first_kernel(couple, *refs),
        out_shape=[
            jax.ShapeDtypeStruct((elec, drop), jnp.bfloat16),
            jax.ShapeDtypeStruct((elec, drop), jnp.bfloat16),
            jax.ShapeDtypeStruct((rows, elec), jnp.float32),
            jax.ShapeDtypeStruct((rows, drop // 2), jnp.float32),
            jax.ShapeDtypeStruct((rows, drop // 2), jnp.float32),
        ],
        in_specs=[SMEM] + [VMEM] * 7,
        out_specs=[VMEM] * 5,
        scratch_shapes=[
            pltpu.VMEM((LANES, elec), jnp.float32),
            pltpu.VMEM((8, drop), jnp.float32),
            pltpu.VMEM((3, elec, LANES), jnp.float32),
            pltpu.VMEM((8, LANES), jnp.float32),
            pltpu.VMEM((2 * rows, drop), jnp.bfloat16),
            pltpu.VMEM((rows, drop), jnp.float32),
        ],
        compiler_params=PARAMS,
        name="coupling_and_first_fields",
    )(core, elec_pos, drop_vert, drop_conn, elec_rhs, drop_rhs, elec_inv, drop_inv)


def drop_solve_kernel(core_ref, rhs_ref, inv_ref, left_ref, right_ref, out_ref):
    for at in range(out_ref.shape[1] // LANES):
        cols = slice(at * LANES, (at + 1) * LANES)
        out_ref[:, cols] = solve_block(inv_ref[at], rhs_ref[:, cols] - (left_ref[:, cols] + right_ref[:, cols]))


def drop_solve(core, drop_rhs, drop_inv, left, right):
    rows, half = left.shape
    whole = pl.BlockSpec((rows, half), lambda i, core: (0, 0))
    return pl.pallas_call(
        drop_solve_kernel,
        out_shape=jax.ShapeDtypeStruct((rows, half), jnp.float32),
        grid_spec=pltpu.PrefetchScalarGridSpec(
            num_scalar_prefetch=1,
            grid=(1,),
            in_specs=[
                pl.BlockSpec((rows, half), lambda i, core: (0, core[0])),
                pl.BlockSpec((half // LANES, LANES, LANES), lambda i, core: (core[0], 0, 0)),
                whole,
                whole,
            ],
            out_specs=whole,
        ),
        compiler_params=PARAMS,
        name="drop_charges",
    )(core, drop_rhs, drop_inv, left, right)


def elec_charge(rhs_ref, inv_ref, left_ref, right_ref):
    pieces = []
    for at in range(rhs_ref.shape[1] // LANES):
        cols = slice(at * LANES, (at + 1) * LANES)
        pieces.append(solve_block(inv_ref[at], rhs_ref[:, cols] - (left_ref[:, cols] + right_ref[:, cols])))
    return jnp.concatenate(pieces, axis=1)


def elec_solve_kernel(rhs_ref, inv_ref, left_ref, right_ref, out_ref):
    out_ref[...] = elec_charge(rhs_ref, inv_ref, left_ref, right_ref)


def elec_solve(elec_rhs, elec_inv, left, right):
    return pl.pallas_call(
        elec_solve_kernel,
        out_shape=jax.ShapeDtypeStruct(left.shape, jnp.float32),
        in_specs=[VMEM] * 4,
        out_specs=VMEM,
        compiler_params=PARAMS,
        name="elec_charges",
    )(elec_rhs, elec_inv, left, right)


def to_drop_kernel(couple, core_ref, rhs_ref, inv_ref, left_ref, right_ref, high_ref, low_ref, keep_ref, send_ref):
    half = keep_ref.shape[1]
    charge = stacked(elec_charge(rhs_ref, inv_ref, left_ref, right_ref))
    for place, out_ref in ((1 - core_ref[0], send_ref), (core_ref[0], keep_ref)):
        for at in range(half // CHUNK):
            cols = pl.ds(pl.multiple_of(place * half + at * CHUNK, CHUNK), CHUNK)
            here = slice(at * CHUNK, (at + 1) * CHUNK)
            out_ref[:, here] = product(charge, (high_ref[:, cols], low_ref[:, cols]), ROWS_IN) * couple


def to_drop(core, couple, elec_rhs, elec_inv, left, right, high, low):
    rows = elec_rhs.shape[0]
    half = high.shape[1] // 2
    return pl.pallas_call(
        lambda *refs: to_drop_kernel(couple, *refs),
        out_shape=[jax.ShapeDtypeStruct((rows, half), jnp.float32)] * 2,
        in_specs=[SMEM] + [VMEM] * 6,
        out_specs=[VMEM] * 2,
        compiler_params=PARAMS,
        name="elec_charges_to_drop_field",
    )(core, elec_rhs, elec_inv, left, right, high, low)


def to_elec_kernel(couple, core_ref, own_ref, other_ref, high_ref, low_ref, out_ref):
    half = own_ref.shape[1]
    total = jnp.zeros(out_ref.shape, jnp.float32)
    for place, charge_ref in ((core_ref[0], own_ref), (1 - core_ref[0], other_ref)):
        for at in range(half // CHUNK):
            cols = pl.ds(pl.multiple_of(place * half + at * CHUNK, CHUNK), CHUNK)
            here = slice(at * CHUNK, (at + 1) * CHUNK)
            total = total + product(stacked(charge_ref[:, here]), (high_ref[:, cols], low_ref[:, cols]), ROWS_OUT)
    out_ref[...] = total * couple


def to_elec(core, couple, own, other, high, low):
    return pl.pallas_call(
        lambda *refs: to_elec_kernel(couple, *refs),
        out_shape=jax.ShapeDtypeStruct((own.shape[0], high.shape[0]), jnp.float32),
        in_specs=[SMEM] + [VMEM] * 4,
        out_specs=VMEM,
        compiler_params=PARAMS,
        name="drop_charges_to_elec_field",
    )(core, own, other, high, low)


def join_kernel(core_ref, own_ref, other_ref, out_ref):
    half = own_ref.shape[1]
    out_ref[:, pl.ds(pl.multiple_of(core_ref[0] * half, half), half)] = own_ref[...]
    out_ref[:, pl.ds(pl.multiple_of((1 - core_ref[0]) * half, half), half)] = other_ref[...]


def join(core, own, other):
    rows, half = own.shape
    return pl.pallas_call(
        join_kernel,
        out_shape=jax.ShapeDtypeStruct((rows, 2 * half), jnp.float32),
        in_specs=[SMEM] + [VMEM] * 2,
        out_specs=VMEM,
        compiler_params=PARAMS,
        name="join_halves",
    )(core, own, other)


def exchanges(elec_devices, drop_devices):
    def pairs(partner):
        out = []
        for elec in range(elec_devices):
            for drop in range(drop_devices):
                to_elec, to_drop = partner(elec, drop)
                out.append((elec * drop_devices + drop, to_elec * drop_devices + to_drop))
        return out

    def ordered(bits, step, core):
        return bits[step] if core == 0 else bits[len(bits) - 1 - step]

    chip_bits = range(1, elec_devices.bit_length() - 1)
    drop_bits = range(drop_devices.bit_length() - 1)
    core = pairs(lambda e, d: (e ^ 1, d))
    plane = [
        pairs(lambda e, d, s=s: (e ^ (1 << ordered(chip_bits, s, e & 1)), d)) for s in range(len(chip_bits))
    ]
    line = [
        pairs(lambda e, d, s=s: (e, d ^ (1 << ordered(drop_bits, s, e & 1)))) for s in range(len(drop_bits))
    ]
    return core, plane, line


def solution(mesh):
    elec_devices, drop_devices = mesh.shape["elec"], mesh.shape["drop"]
    core_pairs, plane_pairs, line_pairs = exchanges(elec_devices, drop_devices)

    def swap(value, pairs):
        return lax.ppermute(value, ("elec", "drop"), pairs)

    def summed(value, steps):
        for pairs in steps[:-1]:
            value = value + swap(value, pairs)
        return value, swap(value, steps[-1])

    def on_device(elec_pos, drop_vert, drop_conn, elec_rhs, drop_rhs, elec_inv, drop_inv):
        couple = couple_of(drop_rhs.shape[1] * drop_devices)
        core = (lax.axis_index("elec") % 2).astype(jnp.int32).reshape(1)
        high, low, elec_1, keep_1, send_1 = first(
            core, couple, elec_pos, drop_vert, drop_conn, elec_rhs, drop_rhs, elec_inv, drop_inv
        )
        drop_1 = summed(keep_1 + swap(send_1, core_pairs), plane_pairs)
        elec_1 = summed(elec_1, line_pairs)
        keep_2, send_2 = to_drop(core, couple, elec_rhs, elec_inv, *elec_1, high, low)
        own_1 = drop_solve(core, drop_rhs, drop_inv, *drop_1)
        other_1 = swap(own_1, core_pairs)
        elec_2 = to_elec(core, couple, own_1, other_1, high, low)
        drop_2 = summed(keep_2 + swap(send_2, core_pairs), plane_pairs)
        elec_2 = summed(elec_2, line_pairs)
        own_2 = drop_solve(core, drop_rhs, drop_inv, *drop_2)
        charge_drop = join(core, own_2, swap(own_2, core_pairs))
        charge_elec = elec_solve(elec_rhs, elec_inv, *elec_2)
        return (charge_elec, charge_drop)

    placed = (
        P(None, "elec"),
        P(None, "drop"),
        P(None, "drop"),
        P(None, "elec"),
        P(None, "drop"),
        P("elec", None, None),
        P("drop", None, None),
    )
    return jax.shard_map(
        on_device,
        mesh=mesh,
        in_specs=placed,
        out_specs=(P(None, "elec"), P(None, "drop")),
        check_vma=False,
    )
```

time: 208 us -> 74.2 us (0.36)
  waiting for transfers between devices: 123 us -> 40.9 us
  matrix products: 41.6 us -> 0 us
  local copies, waits for them, and re-layouts: 26.7 us -> 6.53 us
  starting transfers between devices: 0.3 us -> 15 us
  between operations: 13.9 us -> 0.78 us
  Pallas kernels: 0 us -> 10.2 us
  other arithmetic: 2.73 us -> 0.32 us
    psum x3 -> x0, waiting for transfers between devices: 123 us -> none  [the longest x2 61.5 us: on_device(): field_elec = lax.psum(part_elec, 'drop')]
    dot_general x10 -> x0, matrix products: 41.6 us -> none  [the longest x2 16.9 us: to_elec_of(): lax.dot_general(charge_drop, kernel, (((1,), (1,)), ((), ())), precision=...]
    ppermute x0 -> x12, waiting for transfers between devices: none -> 40.9 us  [swap(): return lax.ppermute(value, ('elec', 'drop'), pairs)]
    gather x2 -> x0, local copies, waits for them, and re-layouts: 23.6 us -> none  [centroids(): corners = jnp.take(drop_vert, conn, axis=1)]
    ppermute x0 -> x12, starting transfers between devices: none -> 15 us  [swap(): return lax.ppermute(value, ('elec', 'drop'), pairs)]
    pallas_call x0 -> x7, Pallas kernels: none -> 10.2 us  [the longest x1 4.7 us: first(): pl.pallas_call(lambda *refs: first_kernel(couple, *refs), out_shape=[jax....]
    unnamed x13 -> x20, local copies, waits for them, and re-layouts: 3.11 us -> 6.53 us
  transfers between devices with their start and end apart: 3 -> 12, of which waited for: 3 -> 8; matrix products, arithmetic and copies ran while one was open for 5% -> 0% of each run, Pallas kernels for 0% -> 6%
where the time goes in v1:
time: 74.2 us; the launch traced here: 73.8 us
  waiting for transfers between devices  40.9 us (55%)
  starting transfers between devices  15 us (20%)
  Pallas kernels  10.2 us (14%)
  local copies, waits for them, and re-layouts  6.53 us (9%)
  between operations  0.78 us (1%)
    ppermute x12, waiting for transfers between devices, swap(): return lax.ppermute(value, ('elec', 'drop'), pairs)  40.9 us
    ppermute x12, starting transfers between devices, swap(): return lax.ppermute(value, ('elec', 'drop'), pairs)  15 us
    unnamed x20, local copies, waits for them, and re-layouts  6.53 us
    pallas_call x1, Pallas kernels, first(): pl.pallas_call(lambda *refs: first_kernel(couple, *refs), out_shape=[jax....  4.7 us
  transfers between devices with their start and end apart: 12, of which 8 were waited for; matrix products, arithmetic and copies ran while one was open for 0% of the time, Pallas kernels for 6%

profile of v1, /device:TPU:0, one launch (start us, length us, event | category | flops | bytes accessed | tf_op | source)
XLA Modules:
  0.0 73.8 jit_solution(3963643344338092655)
XLA Ops:
  0.6 0.0 copy-start
  0.7 1.2 %copy-done = f32[128,2048]{1,0:T(8,128)S(1)} copy-done((f32[128,2048]{1,0:T(8,128)S(1)}, f32[128,2048]{1,0:T(8,128)}, u32[]{:S(2)}) %copy-start) | copy-done | bytes 1048600
  1.9 0.0 copy-start.2
  1.9 1.2 %copy-done.2 = f32[16,128,128]{2,1,0:T(8,128)S(1)} copy-done((f32[16,128,128]{2,1,0:T(8,128)S(1)}, f32[16,128,128]{2,1,0:T(8,128)}, u32[]{:S(2)}) %copy-start.2) | copy-done | bytes 1048600
  3.1 0.0 copy-start.4
  3.1 0.9 %copy-done.4 = f32[128,512]{1,0:T(8,128)S(1)} copy-done((f32[128,512]{1,0:T(8,128)S(1)}, f32[128,512]{1,0:T(8,128)}, u32[]{:S(2)}) %copy-start.4) | copy-done | bytes 262168
  4.0 0.0 copy-start.6
  4.0 0.9 %copy-done.6 = f32[4,128,128]{2,1,0:T(8,128)S(1)} copy-done((f32[4,128,128]{2,1,0:T(8,128)S(1)}, f32[4,128,128]{2,1,0:T(8,128)}, u32[]{:S(2)}) %copy-start.6) | copy-done | bytes 262168
  5.0 0.0 copy-start.7
  5.0 0.8 %copy-done.7 = s32[3,2048]{1,0:T(4,128)S(1)} copy-done((s32[3,2048]{1,0:T(4,128)S(1)}, s32[3,2048]{1,0:T(4,128)}, u32[]{:S(2)}) %copy-start.7) | copy-done | bytes 24600
  5.8 0.0 copy-start.8
  5.8 0.7 copy-done.8
  6.5 0.0 copy-start.9
  6.5 0.7 copy-done.9
  7.2 0.0 copy-start.5
  7.2 4.7 %coupling_and_first_fields.1 = (bf16[512,2048]{1,0:T(8,128)(2,1)S(1)}, bf16[512,2048]{1,0:T(8,128)(2,1)S(1)}, f32[128,512]{1,0:T(8,128)S(1)}, f32[128,1024]{1,0:T(8,128)S(1)}, f32[128,1024]{1,0:T(8,128)S(1)}) custom-call(s32[1]{0:T(128)} %bitcast.refs_0_.core_ref, f32[3,512]{1,0:T(4,128)S(1)} %copy-done.9, f32[3,1024]{1,0:T(4,128)S(1)} %copy-done.8, ...), custom_call_target="tpu_custom_call" | custom-call | tf_op jit(solution)/shard_map/coupling_and_first_fields/pallas_call | solution.py:116
  11.9 0.5 collective-permute-start
  12.4 2.7 %collective-permute-start.6 = (f32[128,512]{1,0:T(8,128)S(1)}, f32[128,512]{1,0:T(8,128)S(1)}, u32[]{:S(2)}, u32[]{:S(2)}) collective-permute-start(f32[128,512]{1,0:T(8,128)S(1)} %get-tuple-element.13), channel_id=1, source_target_pairs={{0,1},{1,0},{2,3},{3,2},{4,6},{5,7},{6,4},{7,5},{8,9},{9,8},{10,11... | collective-permute-start | bytes 786440 | tf_op jit(solution)/shard_map/ppermute | solution.py:283
  15.0 6.8 %collective-permute-done.6 = f32[128,512]{1,0:T(8,128)S(1)} collective-permute-done((f32[128,512]{1,0:T(8,128)S(1)}, f32[128,512]{1,0:T(8,128)S(1)}, u32[]{:S(2)}, u32[]{:S(2)}) %collective-permute-start.6) | collective-permute-done | bytes 262176 | tf_op jit(solution)/shard_map/ppermute | solution.py:283
  21.9 2.8 %collective-permute-start.7 = (f32[128,512]{1,0:T(8,128)S(1)}, f32[128,512]{1,0:T(8,128)S(1)}, u32[]{:S(2)}, u32[]{:S(2)}) collective-permute-start(f32[128,512]{1,0:T(8,128)S(1)} %add.26.refs_3_), channel_id=1, source_target_pairs={{0,2},{1,3},{2,0},{3,1},{4,5},{5,4},{6,7},{7,6},{8,10},{9,11},{10,... | collective-permute-start | bytes 786440 | tf_op jit(solution)/shard_map/ppermute | solution.py:283
  24.7 0.0 collective-permute-done
  24.7 0.1 add.23
  24.8 1.6 %collective-permute-start.1 = (f32[128,1024]{1,0:T(8,128)S(1)}, f32[128,1024]{1,0:T(8,128)S(1)}, u32[]{:S(2)}, u32[]{:S(2)}) collective-permute-start(f32[128,1024]{1,0:T(8,128)S(1)} %add.23), channel_id=1, source_target_pairs={{0,8},{1,9},{2,10},{3,11},{4,20},{5,21},{6,22},{7,23},{8,0},{9,1},... | collective-permute-start | bytes 1572872 | tf_op jit(solution)/shard_map/ppermute | solution.py:283
  26.3 4.4 %collective-permute-done.7.refs_4_ = f32[128,512]{1,0:T(8,128)S(1)} collective-permute-done((f32[128,512]{1,0:T(8,128)S(1)}, f32[128,512]{1,0:T(8,128)S(1)}, u32[]{:S(2)}, u32[]{:S(2)}) %collective-permute-start.7) | collective-permute-done | bytes 262176 | tf_op jit(solution)/shard_map/ppermute | solution.py:283
  30.7 0.0 copy-done.5
  30.7 1.2 %elec_charges_to_drop_field.1 = (f32[128,1024]{1,0:T(8,128)S(1)}, f32[128,1024]{1,0:T(8,128)S(1)}) custom-call(s32[1]{0:T(128)} %bitcast.refs_0_.core_ref, f32[128,512]{1,0:T(8,128)S(1)} %copy-done.5, f32[4,128,128]{2,1,0:T(8,128)S(1)} %copy-done.6, f32[128,512]{1,0:T(8,128)S(1)} %add.26.refs_3_, f32[128,512]{1,0:T(8,128)S(1)} %collective-permute-done.7.refs_4_, ...), custom_call_target="tpu_custom_call" | custom-call | tf_op jit(solution)/shard_map/elec_charges_to_drop_field/pallas_call | solution.py:204
  31.9 0.0 copy-start.1
  31.9 0.0 copy-start.3
  31.9 0.1 collective-permute-start.8
  32.1 1.9 %collective-permute-done.1 = f32[128,1024]{1,0:T(8,128)S(1)} collective-permute-done((f32[128,1024]{1,0:T(8,128)S(1)}, f32[128,1024]{1,0:T(8,128)S(1)}, u32[]{:S(2)}, u32[]{:S(2)}) %collective-permute-start.1) | collective-permute-done | bytes 524320 | tf_op jit(solution)/shard_map/ppermute | solution.py:283
  34.0 0.1 add.24.left_ref
  34.1 1.6 %collective-permute-start.2 = (f32[128,1024]{1,0:T(8,128)S(1)}, f32[128,1024]{1,0:T(8,128)S(1)}, u32[]{:S(2)}, u32[]{:S(2)}) collective-permute-start(f32[128,1024]{1,0:T(8,128)S(1)} %add.24.left_ref), channel_id=1, source_target_pairs={{0,16},{1,17},{2,18},{3,19},{4,12},{5,13},{6,14},{7,15},{8,24},{9,... | collective-permute-start | bytes 1572872 | tf_op jit(solution)/shard_map/ppermute | solution.py:283
  35.7 0.0 collective-permute-done.8
  35.7 0.1 add.27
  35.7 1.6 %collective-permute-start.9 = (f32[128,1024]{1,0:T(8,128)S(1)}, f32[128,1024]{1,0:T(8,128)S(1)}, u32[]{:S(2)}, u32[]{:S(2)}) collective-permute-start(f32[128,1024]{1,0:T(8,128)S(1)} %add.27), channel_id=1, source_target_pairs={{0,8},{1,9},{2,10},{3,11},{4,20},{5,21},{6,22},{7,23},{8,0},{9,1},... | collective-permute-start | bytes 1572872 | tf_op jit(solution)/shard_map/ppermute | solution.py:283
  37.3 11.3 %collective-permute-done.2.right_ref = f32[128,1024]{1,0:T(8,128)S(1)} collective-permute-done((f32[128,1024]{1,0:T(8,128)S(1)}, f32[128,1024]{1,0:T(8,128)S(1)}, u32[]{:S(2)}, u32[]{:S(2)}) %collective-permute-start.2) | collective-permute-done | bytes 524320 | tf_op jit(solution)/shard_map/ppermute | solution.py:283
  48.6 0.0 copy-done.1
  48.6 0.0 copy-done.3
  48.7 0.5 drop_charges.2.refs_1_
  49.1 0.1 collective-permute-start.3
  49.2 0.0 collective-permute-done.9
  49.2 0.1 add.28.left_ref
  49.3 1.4 %collective-permute-start.10 = (f32[128,1024]{1,0:T(8,128)S(1)}, f32[128,1024]{1,0:T(8,128)S(1)}, u32[]{:S(2)}, u32[]{:S(2)}) collective-permute-start(f32[128,1024]{1,0:T(8,128)S(1)} %add.28.left_ref), channel_id=1, source_target_pairs={{0,16},{1,17},{2,18},{3,19},{4,12},{5,13},{6,14},{7,15},{8,24},{9,... | collective-permute-start | bytes 1572872 | tf_op jit(solution)/shard_map/ppermute | solution.py:283
  50.7 0.4 collective-permute-done.3.refs_2_
  51.1 1.4 %drop_charges_to_elec_field.1 = f32[128,512]{1,0:T(8,128)S(1)} custom-call(s32[1]{0:T(128)} %bitcast.refs_0_.core_ref, f32[128,1024]{1,0:T(8,128)S(1)} %drop_charges.2.refs_1_, f32[128,1024]{1,0:T(8,128)S(1)} %collective-permute-done.3.refs_2_, bf16[512,2048]{1,0:T(8,128)(2,1)S(1)} %get-tuple-element.11.refs_3_.refs_5_, ...), custom_call_target="tpu_custom_call" | custom-call | tf_op jit(solution)/shard_map/drop_charges_to_elec_field/pallas_call | solution.py:226
  52.5 2.2 %collective-permute-start.4 = (f32[128,512]{1,0:T(8,128)S(1)}, f32[128,512]{1,0:T(8,128)S(1)}, u32[]{:S(2)}, u32[]{:S(2)}) collective-permute-start(f32[128,512]{1,0:T(8,128)S(1)} %drop_charges_to_elec_field.1), channel_id=1, source_target_pairs={{0,1},{1,0},{2,3},{3,2},{4,6},{5,7},{6,4},{7,5},{8,9},{9,8},{10,11... | collective-permute-start | bytes 786440 | tf_op jit(solution)/shard_map/ppermute | solution.py:283
  54.7 3.8 %collective-permute-done.10.right_ref = f32[128,1024]{1,0:T(8,128)S(1)} collective-permute-done((f32[128,1024]{1,0:T(8,128)S(1)}, f32[128,1024]{1,0:T(8,128)S(1)}, u32[]{:S(2)}, u32[]{:S(2)}) %collective-permute-start.10) | collective-permute-done | bytes 524320 | tf_op jit(solution)/shard_map/ppermute | solution.py:283
  58.5 0.5 drop_charges.3.own_ref
  59.0 0.1 collective-permute-start.11
  59.1 2.7 %collective-permute-done.4 = f32[128,512]{1,0:T(8,128)S(1)} collective-permute-done((f32[128,512]{1,0:T(8,128)S(1)}, f32[128,512]{1,0:T(8,128)S(1)}, u32[]{:S(2)}, u32[]{:S(2)}) %collective-permute-start.4) | collective-permute-done | bytes 262176 | tf_op jit(solution)/shard_map/ppermute | solution.py:283
  61.8 0.5 collective-permute-start.5
  62.3 9.4 %collective-permute-done.5.right_ref = f32[128,512]{1,0:T(8,128)S(1)} collective-permute-done((f32[128,512]{1,0:T(8,128)S(1)}, f32[128,512]{1,0:T(8,128)S(1)}, u32[]{:S(2)}, u32[]{:S(2)}) %collective-permute-start.5) | collective-permute-done | bytes 262176 | tf_op jit(solution)/shard_map/ppermute | solution.py:283
  71.7 1.0 %elec_charges.1 = f32[128,512]{1,0:T(8,128)} custom-call(f32[128,512]{1,0:T(8,128)S(1)} %copy-done.5, f32[4,128,128]{2,1,0:T(8,128)S(1)} %copy-done.6, f32[128,512]{1,0:T(8,128)S(1)} %add.25.left_ref, f32[128,512]{1,0:T(8,128)S(1)} %collective-permute-done.5.right_ref), custom_call_target="tpu_custom_call" | custom-call | tf_op jit(solution)/shard_map/elec_charges/pallas_call | solution.py:181
  72.8 0.0 collective-permute-done.11.other_ref
  72.8 1.0 %join_halves.1 = f32[128,2048]{1,0:T(8,128)} custom-call(s32[1]{0:T(128)} %bitcast.refs_0_.core_ref, f32[128,1024]{1,0:T(8,128)S(1)} %drop_charges.3.own_ref, f32[128,1024]{1,0:T(8,128)S(1)} %collective-permute-done.11.other_ref), custom_call_target="tpu_custom_call" | custom-call | tf_op jit(solution)/shard_map/join_halves/pallas_call | solution.py:244
  (2 shorter events, 0.1 us)
Async XLA Ops:
  0.6 1.2 %copy-start = (f32[128,2048]{1,0:T(8,128)S(1)}, f32[128,2048]{1,0:T(8,128)}, u32[]{:S(2)}) copy-start(f32[128,2048]{1,0:T(8,128)} %rhs_ref.5) | copy-start | bytes 3145732
  1.9 1.2 %copy-start.2 = (f32[16,128,128]{2,1,0:T(8,128)S(1)}, f32[16,128,128]{2,1,0:T(8,128)}, u32[]{:S(2)}) copy-start(f32[16,128,128]{2,1,0:T(8,128)} %inv_ref.5) | copy-start | bytes 3145732
  3.1 0.9 %copy-start.4 = (f32[128,512]{1,0:T(8,128)S(1)}, f32[128,512]{1,0:T(8,128)}, u32[]{:S(2)}) copy-start(f32[128,512]{1,0:T(8,128)} %refs_1_.3) | copy-start | bytes 786436
  4.0 0.9 %copy-start.6 = (f32[4,128,128]{2,1,0:T(8,128)S(1)}, f32[4,128,128]{2,1,0:T(8,128)}, u32[]{:S(2)}) copy-start(f32[4,128,128]{2,1,0:T(8,128)} %refs_2_.3) | copy-start | bytes 786436
  5.0 0.8 %copy-start.7 = (s32[3,2048]{1,0:T(4,128)S(1)}, s32[3,2048]{1,0:T(4,128)}, u32[]{:S(2)}) copy-start(s32[3,2048]{1,0:T(4,128)} %refs_3_.1) | copy-start | bytes 73732
  5.8 0.7 copy-start.8
  6.5 0.7 copy-start.9
  7.2 23.6 %copy-start.5 = (f32[128,512]{1,0:T(8,128)S(1)}, f32[128,512]{1,0:T(8,128)}, u32[]{:S(2)}) copy-start(f32[128,512]{1,0:T(8,128)} %refs_1_.3) | copy-start | bytes 786436
  11.9 12.8 %collective-permute-start = (f32[128,1024]{1,0:T(8,128)S(1)}, f32[128,1024]{1,0:T(8,128)S(1)}, u32[]{:S(2)}, u32[]{:S(2)}) collective-permute-start(f32[128,1024]{1,0:T(8,128)S(1)} %get-tuple-element.10), channel_id=1, source_target_pairs={{0,4},{1,5},{2,6},{3,7},{4,0},{5,1},{6,2},{7,3},{8,12},{9,13},{10,... | collective-permute-start | bytes 1572872 | tf_op jit(solution)/shard_map/ppermute | solution.py:283
  12.4 9.4 %collective-permute-start.6 = (f32[128,512]{1,0:T(8,128)S(1)}, f32[128,512]{1,0:T(8,128)S(1)}, u32[]{:S(2)}, u32[]{:S(2)}) collective-permute-start(f32[128,512]{1,0:T(8,128)S(1)} %get-tuple-element.13), channel_id=1, source_target_pairs={{0,1},{1,0},{2,3},{3,2},{4,6},{5,7},{6,4},{7,5},{8,9},{9,8},{10,11... | collective-permute-start | bytes 786440 | tf_op jit(solution)/shard_map/ppermute | solution.py:283
  21.9 8.9 %collective-permute-start.7 = (f32[128,512]{1,0:T(8,128)S(1)}, f32[128,512]{1,0:T(8,128)S(1)}, u32[]{:S(2)}, u32[]{:S(2)}) collective-permute-start(f32[128,512]{1,0:T(8,128)S(1)} %add.26.refs_3_), channel_id=1, source_target_pairs={{0,2},{1,3},{2,0},{3,1},{4,5},{5,4},{6,7},{7,6},{8,10},{9,11},{10,... | collective-permute-start | bytes 786440 | tf_op jit(solution)/shard_map/ppermute | solution.py:283
  24.8 9.2 %collective-permute-start.1 = (f32[128,1024]{1,0:T(8,128)S(1)}, f32[128,1024]{1,0:T(8,128)S(1)}, u32[]{:S(2)}, u32[]{:S(2)}) collective-permute-start(f32[128,1024]{1,0:T(8,128)S(1)} %add.23), channel_id=1, source_target_pairs={{0,8},{1,9},{2,10},{3,11},{4,20},{5,21},{6,22},{7,23},{8,0},{9,1},... | collective-permute-start | bytes 1572872 | tf_op jit(solution)/shard_map/ppermute | solution.py:283
  31.9 16.7 %copy-start.1 = (f32[128,2048]{1,0:T(8,128)S(1)}, f32[128,2048]{1,0:T(8,128)}, u32[]{:S(2)}) copy-start(f32[128,2048]{1,0:T(8,128)} %rhs_ref.5) | copy-start | bytes 3145732
  31.9 16.7 %copy-start.3 = (f32[16,128,128]{2,1,0:T(8,128)S(1)}, f32[16,128,128]{2,1,0:T(8,128)}, u32[]{:S(2)}) copy-start(f32[16,128,128]{2,1,0:T(8,128)} %inv_ref.5) | copy-start | bytes 3145732
  31.9 3.7 %collective-permute-start.8 = (f32[128,1024]{1,0:T(8,128)S(1)}, f32[128,1024]{1,0:T(8,128)S(1)}, u32[]{:S(2)}, u32[]{:S(2)}) collective-permute-start(f32[128,1024]{1,0:T(8,128)S(1)} %get-tuple-element.15), channel_id=1, source_target_pairs={{0,4},{1,5},{2,6},{3,7},{4,0},{5,1},{6,2},{7,3},{8,12},{9,13},{10,... | collective-permute-start | bytes 1572872 | tf_op jit(solution)/shard_map/ppermute | solution.py:283
  34.1 14.6 %collective-permute-start.2 = (f32[128,1024]{1,0:T(8,128)S(1)}, f32[128,1024]{1,0:T(8,128)S(1)}, u32[]{:S(2)}, u32[]{:S(2)}) collective-permute-start(f32[128,1024]{1,0:T(8,128)S(1)} %add.24.left_ref), channel_id=1, source_target_pairs={{0,16},{1,17},{2,18},{3,19},{4,12},{5,13},{6,14},{7,15},{8,24},{9,... | collective-permute-start | bytes 1572872 | tf_op jit(solution)/shard_map/ppermute | solution.py:283
  35.7 13.5 %collective-permute-start.9 = (f32[128,1024]{1,0:T(8,128)S(1)}, f32[128,1024]{1,0:T(8,128)S(1)}, u32[]{:S(2)}, u32[]{:S(2)}) collective-permute-start(f32[128,1024]{1,0:T(8,128)S(1)} %add.27), channel_id=1, source_target_pairs={{0,8},{1,9},{2,10},{3,11},{4,20},{5,21},{6,22},{7,23},{8,0},{9,1},... | collective-permute-start | bytes 1572872 | tf_op jit(solution)/shard_map/ppermute | solution.py:283
  49.1 2.0 %collective-permute-start.3 = (f32[128,1024]{1,0:T(8,128)S(1)}, f32[128,1024]{1,0:T(8,128)S(1)}, u32[]{:S(2)}, u32[]{:S(2)}) collective-permute-start(f32[128,1024]{1,0:T(8,128)S(1)} %drop_charges.2.refs_1_), channel_id=1, source_target_pairs={{0,4},{1,5},{2,6},{3,7},{4,0},{5,1},{6,2},{7,3},{8,12},{9,13},{10,... | collective-permute-start | bytes 1572872 | tf_op jit(solution)/shard_map/ppermute | solution.py:283
  49.3 9.2 %collective-permute-start.10 = (f32[128,1024]{1,0:T(8,128)S(1)}, f32[128,1024]{1,0:T(8,128)S(1)}, u32[]{:S(2)}, u32[]{:S(2)}) collective-permute-start(f32[128,1024]{1,0:T(8,128)S(1)} %add.28.left_ref), channel_id=1, source_target_pairs={{0,16},{1,17},{2,18},{3,19},{4,12},{5,13},{6,14},{7,15},{8,24},{9,... | collective-permute-start | bytes 1572872 | tf_op jit(solution)/shard_map/ppermute | solution.py:283
  52.5 9.3 %collective-permute-start.4 = (f32[128,512]{1,0:T(8,128)S(1)}, f32[128,512]{1,0:T(8,128)S(1)}, u32[]{:S(2)}, u32[]{:S(2)}) collective-permute-start(f32[128,512]{1,0:T(8,128)S(1)} %drop_charges_to_elec_field.1), channel_id=1, source_target_pairs={{0,1},{1,0},{2,3},{3,2},{4,6},{5,7},{6,4},{7,5},{8,9},{9,8},{10,11... | collective-permute-start | bytes 786440 | tf_op jit(solution)/shard_map/ppermute | solution.py:283
  59.0 13.8 %collective-permute-start.11 = (f32[128,1024]{1,0:T(8,128)S(1)}, f32[128,1024]{1,0:T(8,128)S(1)}, u32[]{:S(2)}, u32[]{:S(2)}) collective-permute-start(f32[128,1024]{1,0:T(8,128)S(1)} %drop_charges.3.own_ref), channel_id=1, source_target_pairs={{0,4},{1,5},{2,6},{3,7},{4,0},{5,1},{6,2},{7,3},{8,12},{9,13},{10,... | collective-permute-start | bytes 1572872 | tf_op jit(solution)/shard_map/ppermute | solution.py:283
  61.8 9.9 %collective-permute-start.5 = (f32[128,512]{1,0:T(8,128)S(1)}, f32[128,512]{1,0:T(8,128)S(1)}, u32[]{:S(2)}, u32[]{:S(2)}) collective-permute-start(f32[128,512]{1,0:T(8,128)S(1)} %add.25.left_ref), channel_id=1, source_target_pairs={{0,2},{1,3},{2,0},{3,1},{4,5},{5,4},{6,7},{7,6},{8,10},{9,11},{10,... | collective-permute-start | bytes 786440 | tf_op jit(solution)/shard_map/ppermute | solution.py:283

commit v2 on v0

v2 whole, which is shorter than its diff:
```python
import functools
import math

import jax
import jax.numpy as jnp
from jax import lax
from jax.experimental import pallas as pl
from jax.experimental.pallas import tpu as pltpu
from jax.sharding import PartitionSpec as P

SOFTEN = 0.001
SCREEN = 1.0
LANES = 128
CHUNK = 256
VMEM = pl.BlockSpec(memory_space=pltpu.VMEM)
SMEM = pl.BlockSpec(memory_space=pltpu.SMEM)
HBM = pl.BlockSpec(memory_space=pltpu.HBM)
ROWS_IN = ((1,), (0,))
ROWS_OUT = ((1,), (1,))


def couple_of(total_drop):
    return 1.0 / (3.0 * math.sqrt(total_drop))


def split(value):
    high = value.astype(jnp.bfloat16)
    low = (value - high.astype(jnp.float32)).astype(jnp.bfloat16)
    return high, low


def stacked(value):
    return jnp.concatenate(split(value), axis=0)


def product(both, weights, contract):
    weight_high, weight_low = weights
    rows = both.shape[0] // 2
    dims = (contract, ((), ()))
    first = lax.dot_general(both, weight_high, dims, preferred_element_type=jnp.float32)
    second = lax.dot_general(both[:rows], weight_low, dims, preferred_element_type=jnp.float32)
    return first[:rows] + (first[rows:] + second)


def solve_block(inverse, values):
    return product(stacked(values), split(inverse), ROWS_OUT)


def solve(inv_ref, values):
    pieces = []
    for at in range(values.shape[1] // LANES):
        pieces.append(solve_block(inv_ref[at], values[:, at * LANES : (at + 1) * LANES]))
    return jnp.concatenate(pieces, axis=1)


def gather(vert_ref, index):
    lane, tile = index % LANES, index // LANES
    found = []
    for axis in range(3):
        total = jnp.zeros(index.shape, jnp.float32)
        for at in range(vert_ref.shape[1] // LANES):
            table = jnp.broadcast_to(vert_ref[axis : axis + 1, at * LANES : (at + 1) * LANES], index.shape)
            total = jnp.where(tile == at, jnp.take_along_axis(table, lane, axis=1), total)
        found.append(total)
    return found


def fill_centres(vert_ref, conn_ref, centre):
    half_block = vert_ref.shape[1]
    for at in range(conn_ref.shape[1] // LANES):
        cols = slice(at * LANES, (at + 1) * LANES)
        corners = gather(vert_ref, conn_ref[:, cols] % half_block)
        for axis in range(3):
            g = corners[axis]
            centre[axis : axis + 1, cols] = (g[0:1] + g[1:2] + g[2:3]) / 3.0


def coupling_chunk(wide, centre, start):
    tiles = []
    for lane in range(start, start + CHUNK, LANES):
        here = slice(lane, lane + LANES)
        dx = wide[0] - centre[0:1, here]
        dy = wide[1] - centre[1:2, here]
        dz = wide[2] - centre[2:3, here]
        square = dx * dx + dy * dy + dz * dz + SOFTEN
        inverse = lax.rsqrt(square)
        tiles.append(jnp.exp((square * inverse) * -SCREEN) * inverse)
    return split(jnp.concatenate(tiles, axis=1))


def columns(place, width):
    return pl.ds(pl.multiple_of(place * width, width), width)


def first_kernel(couple, core_ref, pos_hbm, vert_hbm, conn_hbm, erhs_hbm, einv_hbm, drhs_hbm, dinv_hbm,
                 ohigh_ref, olow_ref, high_ref, low_ref, send_ref, keep_ref, elec_ref, erhs, einv, drhs, dinv,
                 pos, vert, conn, place, wide, centre, sems):
    elec, half = high_ref.shape
    blocks = half // LANES
    moves = ((conn_hbm, conn), (vert_hbm, vert), (pos_hbm, pos), (erhs_hbm, erhs), (einv_hbm, einv),
             (drhs_hbm, drhs), (dinv_hbm, dinv))
    copies = [pltpu.make_async_copy(here, there, sems.at[at]) for at, (here, there) in enumerate(moves)]
    for copy in copies:
        copy.start()
    for copy in copies[:3]:
        copy.wait()
    place[...] = jnp.zeros_like(place)
    place[0:3, :] = pos[...]
    upright = place[...].T
    for axis in range(3):
        wide[axis] = jnp.broadcast_to(upright[:, axis : axis + 1], (elec, LANES))
    fill_centres(vert, conn, centre)
    for copy in copies[3:]:
        copy.wait()
    both = stacked(solve(einv, erhs[...]))
    total = jnp.zeros(elec_ref.shape, jnp.float32)
    for place_at, parts, field_ref in (
        (1 - core_ref[0], (ohigh_ref, olow_ref), send_ref),
        (core_ref[0], (high_ref, low_ref), keep_ref),
    ):
        here = columns(place_at, half)
        centres = centre[:, here]
        charge = stacked(solve(dinv.at[pl.ds(place_at * blocks, blocks)], drhs[:, here]))
        for start in range(0, half, CHUNK):
            cols = slice(start, start + CHUNK)
            weights = coupling_chunk(wide, centres, start)
            parts[0][:, cols], parts[1][:, cols] = weights
            field_ref[:, cols] = product(both, weights, ROWS_IN) * couple
            total = total + product(charge[:, cols], weights, ROWS_OUT)
    elec_ref[...] = total * couple


def add_pairs_kernel(a_ref, b_ref, c_ref, d_ref, ab_ref, cd_ref):
    ab_ref[...] = a_ref[...] + b_ref[...]
    cd_ref[...] = c_ref[...] + d_ref[...]


def to_drop_kernel(couple, rhs_ref, inv_ref, field_ref, high_ref, low_ref, send_ref, both_ref):
    both = stacked(solve(inv_ref, rhs_ref[...] - field_ref[...]))
    both_ref[...] = both
    for start in range(0, high_ref.shape[1], CHUNK):
        cols = slice(start, start + CHUNK)
        send_ref[:, cols] = product(both, (high_ref[:, cols], low_ref[:, cols]), ROWS_IN) * couple


def halves_kernel(couple, core_ref, both_ref, rhs_ref, inv_ref, field_ref, high_ref, low_ref, keep_ref, elec_ref):
    half = high_ref.shape[1]
    blocks = half // LANES
    keep_ref[...] = product(both_ref[...], (high_ref[...], low_ref[...]), ROWS_IN) * couple
    values = rhs_ref[:, columns(core_ref[0], half)] - field_ref[...]
    charge = solve(inv_ref.at[pl.ds(core_ref[0] * blocks, blocks)], values)
    elec_ref[...] = product(stacked(charge), (high_ref[...], low_ref[...]), ROWS_OUT)


def to_elec_kernel(couple, core_ref, rhs_ref, inv_ref, field_ref, part_ref, high_ref, low_ref, keep_ref, send_ref,
                   elec_ref, sum_ref):
    half = high_ref.shape[1]
    blocks = half // LANES
    other = 1 - core_ref[0]
    sum_ref[...] = keep_ref[...] + send_ref[...]
    values = rhs_ref[:, columns(other, half)] - field_ref[...]
    charge = solve(inv_ref.at[pl.ds(other * blocks, blocks)], values)
    elec_ref[...] = (part_ref[...] + product(stacked(charge), (high_ref[...], low_ref[...]), ROWS_OUT)) * couple


def elec_kernel(rhs_ref, inv_ref, field_ref, out_ref):
    out_ref[...] = solve(inv_ref, rhs_ref[...] - field_ref[...])


def drop_kernel(core_ref, rhs_ref, inv_ref, own_ref, other_ref, out_ref):
    half = own_ref.shape[1]
    blocks = half // LANES
    for place, field_ref in ((core_ref[0], own_ref), (1 - core_ref[0], other_ref)):
        cols = columns(place, half)
        out_ref[:, cols] = solve(inv_ref.at[pl.ds(place * blocks, blocks)], rhs_ref[:, cols] - field_ref[...])


def run(kernel, name, micros, operands, specs, outs, scratch=()):
    return pl.pallas_call(
        kernel,
        out_shape=[jax.ShapeDtypeStruct(shape, dtype) for shape, dtype in outs],
        in_specs=specs,
        out_specs=[VMEM] * len(outs),
        scratch_shapes=list(scratch),
        compiler_params=pltpu.CompilerParams(vmem_limit_bytes=32 * 2**20),
        cost_estimate=pl.CostEstimate(flops=0, bytes_accessed=int(micros * 3.3e6), transcendentals=0),
        name=name,
    )(*operands)


def exchanges(elec_devices, drop_devices):
    def pairs(partner):
        out = []
        for elec in range(elec_devices):
            for drop in range(drop_devices):
                to_elec, to_drop = partner(elec, drop)
                out.append((elec * drop_devices + drop, to_elec * drop_devices + to_drop))
        return out

    def ordered(bits, step, core):
        return bits[step] if core == 0 else bits[len(bits) - 1 - step]

    chip_bits = range(1, elec_devices.bit_length() - 1)
    drop_bits = range(drop_devices.bit_length() - 1)
    core = pairs(lambda e, d: (e ^ 1, d))
    plane = [
        pairs(lambda e, d, s=s: (e ^ (1 << ordered(chip_bits, s, e & 1)), d)) for s in range(len(chip_bits))
    ]
    line = [
        pairs(lambda e, d, s=s: (e, d ^ (1 << ordered(drop_bits, s, e & 1)))) for s in range(len(drop_bits))
    ]
    return core, plane, line


def solution(mesh):
    elec_devices, drop_devices = mesh.shape["elec"], mesh.shape["drop"]
    core_pairs, plane_pairs, line_pairs = exchanges(elec_devices, drop_devices)

    def swap(value, pairs):
        return lax.ppermute(value, ("elec", "drop"), pairs)

    def sums(line, plane):
        for at in range(max(len(line_pairs), len(plane_pairs))):
            line_got = swap(line, line_pairs[at]) if at < len(line_pairs) else jnp.zeros_like(line)
            plane_got = swap(plane, plane_pairs[at]) if at < len(plane_pairs) else jnp.zeros_like(plane)
            line, plane = run(
                add_pairs_kernel, "add_pairs", 0.1,
                (line, line_got, plane, plane_got),
                [VMEM] * 4,
                [(line.shape, jnp.float32), (plane.shape, jnp.float32)],
            )
        return line, plane

    def on_device(elec_pos, drop_vert, drop_conn, elec_rhs, drop_rhs, elec_inv, drop_inv):
        f32, bf16 = jnp.float32, jnp.bfloat16
        rows, elec = elec_rhs.shape
        drop = drop_rhs.shape[1]
        half = drop // 2
        couple = couple_of(drop * drop_devices)
        core = (lax.axis_index("elec") % 2).astype(jnp.int32).reshape(1)

        inputs = (elec_pos, drop_vert, drop_conn, elec_rhs, elec_inv, drop_rhs, drop_inv)
        outs = [((elec, half), bf16)] * 4 + [((rows, half), f32)] * 2 + [((rows, elec), f32)]
        outs += [(value.shape, f32) for value in inputs[3:]]
        other_high, other_low, own_high, own_low, send, keep, line, elec_rhs, elec_inv, drop_rhs, drop_inv = run(
            functools.partial(first_kernel, couple), "coupling_and_first_fields", 5.0,
            (core, *(pltpu.with_memory_space_constraint(value, pltpu.HBM) for value in inputs)),
            [SMEM] + [HBM] * 7,
            outs,
            [pltpu.VMEM(value.shape, value.dtype) for value in inputs[:3]]
            + [pltpu.VMEM((LANES, elec), f32), pltpu.VMEM((3, elec, LANES), f32), pltpu.VMEM((8, drop), f32),
               pltpu.SemaphoreType.DMA((7,))],
        )
        got = swap(send, core_pairs)
        line, plane = sums(line, keep + got)

        plane_got = swap(plane, core_pairs)
        send, both = run(
            functools.partial(to_drop_kernel, couple), "elec_charges_to_drop_field", 0.8,
            (elec_rhs, elec_inv, line, other_high, other_low),
            [VMEM] * 5,
            [((rows, half), f32), ((2 * rows, elec), bf16)],
        )
        got = swap(send, core_pairs)
        keep, part = run(
            functools.partial(halves_kernel, couple), "fields_of_own_half", 2.0,
            (core, both, drop_rhs, drop_inv, plane, own_high, own_low),
            [SMEM] + [VMEM] * 6,
            [((rows, half), f32), ((rows, elec), f32)],
        )
        line, plane = run(
            functools.partial(to_elec_kernel, couple), "field_of_other_half", 1.4,
            (core, drop_rhs, drop_inv, plane_got, part, other_high, other_low, keep, got),
            [SMEM] + [VMEM] * 8,
            [((rows, elec), f32), ((rows, half), f32)],
        )
        line, plane = sums(line, plane)

        plane_got = swap(plane, core_pairs)
        charge_elec, = run(
            elec_kernel, "elec_charges", 1.0, (elec_rhs, elec_inv, line), [VMEM] * 3, [((rows, elec), f32)]
        )
        charge_drop, = run(
            drop_kernel, "drop_charges", 1.8, (core, drop_rhs, drop_inv, plane, plane_got), [SMEM] + [VMEM] * 4,
            [((rows, drop), f32)],
        )
        return (charge_elec, charge_drop)

    placed = (
        P(None, "elec"),
        P(None, "drop"),
        P(None, "drop"),
        P(None, "elec"),
        P(None, "drop"),
        P("elec", None, None),
        P("drop", None, None),
    )
    return jax.shard_map(
        on_device,
        mesh=mesh,
        in_specs=placed,
        out_specs=(P(None, "elec"), P(None, "drop")),
        check_vma=False,
    )
```

time: 208 us -> 61.3 us (0.29)
  waiting for transfers between devices: 123 us -> 31.9 us
  matrix products: 41.6 us -> 0 us
  local copies, waits for them, and re-layouts: 26.7 us -> 0 us
  starting transfers between devices: 0.3 us -> 15.8 us
  between operations: 13.9 us -> 0.73 us
  Pallas kernels: 0 us -> 12.7 us
  other arithmetic: 2.73 us -> 0.07 us
    psum x3 -> x0, waiting for transfers between devices: 123 us -> none  [the longest x2 61.5 us: on_device(): field_elec = lax.psum(part_elec, 'drop')]
    dot_general x10 -> x0, matrix products: 41.6 us -> none  [the longest x2 16.9 us: to_elec_of(): lax.dot_general(charge_drop, kernel, (((1,), (1,)), ((), ())), precision=...]
    ppermute x0 -> x12, waiting for transfers between devices: none -> 31.9 us  [swap(): return lax.ppermute(value, ('elec', 'drop'), pairs)]
    gather x2 -> x0, local copies, waits for them, and re-layouts: 23.6 us -> none  [centroids(): corners = jnp.take(drop_vert, conn, axis=1)]
    ppermute x0 -> x12, starting transfers between devices: none -> 15.8 us  [swap(): return lax.ppermute(value, ('elec', 'drop'), pairs)]
    pallas_call x0 -> x10, Pallas kernels: none -> 12.7 us  [run(): pl.pallas_call(kernel, out_shape=[jax.ShapeDtypeStruct(shape, dtype) for...]
    unnamed x13 -> x0, local copies, waits for them, and re-layouts: 3.11 us -> none
  transfers between devices with their start and end apart: 3 -> 12, of which waited for: 3 -> 8; matrix products, arithmetic and copies ran while one was open for 5% -> 0% of each run, Pallas kernels for 0% -> 4%
where the time goes in v2:
time: 61.3 us; the launch traced here: 61.2 us
  waiting for transfers between devices  31.9 us (52%)
  starting transfers between devices  15.8 us (26%)
  Pallas kernels  12.7 us (21%)
  between operations  0.73 us (1%)
    ppermute x12, waiting for transfers between devices, swap(): return lax.ppermute(value, ('elec', 'drop'), pairs)  31.9 us
    ppermute x12, starting transfers between devices, swap(): return lax.ppermute(value, ('elec', 'drop'), pairs)  15.8 us
    pallas_call x10, Pallas kernels, run(): pl.pallas_call(kernel, out_shape=[jax.ShapeDtypeStruct(shape, dtype) for...  12.7 us
  transfers between devices with their start and end apart: 12, of which 8 were waited for; matrix products, arithmetic and copies ran while one was open for 0% of the time, Pallas kernels for 4%

profile of v2, /device:TPU:0, one launch (start us, length us, event | category | flops | bytes accessed | tf_op | source)
XLA Modules:
  0.0 61.2 jit_solution(5781628177831280890)
XLA Ops:
  0.6 6.0 %coupling_and_first_fields.1 = (bf16[512,1024]{1,0:T(8,128)(2,1)S(1)}, bf16[512,1024]{1,0:T(8,128)(2,1)S(1)}, bf16[512,1024]{1,0:T(8,128)(2,1)S(1)}, bf16[512,10...) custom-call(s32[1]{0:T(128)} %bitcast.core_ref, ...), custom_call_target="tpu_custom_call" | custom-call | bytes 16500000 | tf_op jit(solution)/shard_map/coupling_and_first_fields/pallas_call | solution.py:179
  6.7 0.5 collective-permute-start.1
  7.2 1.5 %collective-permute-done.1 = f32[128,1024]{1,0:T(8,128)S(1)} collective-permute-done((f32[128,1024]{1,0:T(8,128)S(1)}, f32[128,1024]{1,0:T(8,128)S(1)}, u32[]{:S(2)}, u32[]{:S(2)}) %collective-permute-start.1) | collective-permute-done | bytes 524320 | tf_op jit(solution)/shard_map/ppermute | solution.py:220
  8.7 0.1 add.8.c_ref
  8.8 2.9 %collective-permute-start.2 = (f32[128,1024]{1,0:T(8,128)S(1)}, f32[128,1024]{1,0:T(8,128)S(1)}, u32[]{:S(2)}, u32[]{:S(2)}) collective-permute-start(f32[128,1024]{1,0:T(8,128)S(1)} %add.8.c_ref), channel_id=1, source_target_pairs={{0,8},{1,9},{2,10},{3,11},{4,20},{5,21},{6,22},{7,23},{8,0},{9,1},... | collective-permute-start | bytes 1572872 | tf_op jit(solution)/shard_map/ppermute | solution.py:220
  11.7 1.6 %collective-permute-start = (f32[128,512]{1,0:T(8,128)S(1)}, f32[128,512]{1,0:T(8,128)S(1)}, u32[]{:S(2)}, u32[]{:S(2)}) collective-permute-start(f32[128,512]{1,0:T(8,128)S(1)} %get-tuple-element.31.a_ref), channel_id=1, source_target_pairs={{0,1},{1,0},{2,3},{3,2},{4,6},{5,7},{6,4},{7,5},{8,9},{9,8},{10,11... | collective-permute-start | bytes 786440 | tf_op jit(solution)/shard_map/ppermute | solution.py:220
  13.3 7.3 %collective-permute-done.b_ref = f32[128,512]{1,0:T(8,128)S(1)} collective-permute-done((f32[128,512]{1,0:T(8,128)S(1)}, f32[128,512]{1,0:T(8,128)S(1)}, u32[]{:S(2)}, u32[]{:S(2)}) %collective-permute-start) | collective-permute-done | bytes 262176 | tf_op jit(solution)/shard_map/ppermute | solution.py:220
  20.6 0.0 collective-permute-done.2.d_ref
  20.6 0.1 add_pairs.4
  20.7 0.4 collective-permute-start.4
  21.1 3.1 %collective-permute-start.3 = (f32[128,512]{1,0:T(8,128)S(1)}, f32[128,512]{1,0:T(8,128)S(1)}, u32[]{:S(2)}, u32[]{:S(2)}) collective-permute-start(f32[128,512]{1,0:T(8,128)S(1)} %get-tuple-element.34.a_ref), channel_id=1, source_target_pairs={{0,2},{1,3},{2,0},{3,1},{4,5},{5,4},{6,7},{7,6},{8,10},{9,11},{10,... | collective-permute-start | bytes 786440 | tf_op jit(solution)/shard_map/ppermute | solution.py:220
  24.2 5.3 %collective-permute-done.3.b_ref = f32[128,512]{1,0:T(8,128)S(1)} collective-permute-done((f32[128,512]{1,0:T(8,128)S(1)}, f32[128,512]{1,0:T(8,128)S(1)}, u32[]{:S(2)}, u32[]{:S(2)}) %collective-permute-start.3) | collective-permute-done | bytes 262176 | tf_op jit(solution)/shard_map/ppermute | solution.py:220
  29.5 0.5 collective-permute-done.4.d_ref
  29.9 0.1 add_pairs.5
  30.0 0.8 %elec_charges_to_drop_field.1 = (f32[128,1024]{1,0:T(8,128)S(1)}, bf16[256,512]{1,0:T(8,128)(2,1)S(1)}) custom-call(f32[128,512]{1,0:T(8,128)S(1)} %get-tuple-element.27.rhs_ref, f32[4,128,128]{2,1,0:T(8,128)S(1)} %get-tuple-element.28.inv_ref, f32[128,512]{1,0:T(8,128)S(1)} %get-tuple-element.37.field_ref, ...), custom_call_target="tpu_custom_call" | custom-call | bytes 2640000 | tf_op jit(solution)/shard_map/elec_charges_to_drop_field/pallas_call | solution.py:179
  30.8 0.1 collective-permute-start.6
  30.9 0.5 collective-permute-start.5
  31.4 1.6 %fields_of_own_half.1 = (f32[128,1024]{1,0:T(8,128)S(1)}, f32[128,512]{1,0:T(8,128)S(1)}) custom-call(s32[1]{0:T(128)} %bitcast.core_ref, bf16[256,512]{1,0:T(8,128)(2,1)S(1)} %get-tuple-element.40.both_ref, f32[128,2048]{1,0:T(8,128)S(1)} %get-tuple-element.29.rhs_ref, f32[16,128,128]{2,1,0:T(8,128)S(1)} %get-tuple-element.30.inv_ref, ...), custom_call_target="tpu_custom_call" | custom-call | bytes 6600000 | tf_op jit(solution)/shard_map/fields_of_own_half/pallas_call | solution.py:179
  32.9 0.0 collective-permute-done.6.send_ref
  33.0 0.6 collective-permute-done.5.field_ref
  33.5 1.2 %field_of_other_half.1 = (f32[128,512]{1,0:T(8,128)S(1)}, f32[128,1024]{1,0:T(8,128)S(1)}) custom-call(s32[1]{0:T(128)} %bitcast.core_ref, f32[128,2048]{1,0:T(8,128)S(1)} %get-tuple-element.29.rhs_ref, f32[16,128,128]{2,1,0:T(8,128)S(1)} %get-tuple-element.30.inv_ref, f32[128,1024]{1,0:T(8,128)S(1)} %collective-permute-done.5.field_ref, ...), custom_call_target="tpu_custom_call" | custom-call | bytes 4620000 | tf_op jit(solution)/shard_map/field_of_other_half/pallas_call | solution.py:179
  34.7 3.0 %collective-permute-start.8 = (f32[128,1024]{1,0:T(8,128)S(1)}, f32[128,1024]{1,0:T(8,128)S(1)}, u32[]{:S(2)}, u32[]{:S(2)}) collective-permute-start(f32[128,1024]{1,0:T(8,128)S(1)} %get-tuple-element.47.c_ref), channel_id=1, source_target_pairs={{0,8},{1,9},{2,10},{3,11},{4,20},{5,21},{6,22},{7,23},{8,0},{9,1},... | collective-permute-start | bytes 1572872 | tf_op jit(solution)/shard_map/ppermute | solution.py:220
  37.7 0.8 %collective-permute-start.7 = (f32[128,512]{1,0:T(8,128)S(1)}, f32[128,512]{1,0:T(8,128)S(1)}, u32[]{:S(2)}, u32[]{:S(2)}) collective-permute-start(f32[128,512]{1,0:T(8,128)S(1)} %get-tuple-element.46.a_ref), channel_id=1, source_target_pairs={{0,1},{1,0},{2,3},{3,2},{4,6},{5,7},{6,4},{7,5},{8,9},{9,8},{10,11... | collective-permute-start | bytes 786440 | tf_op jit(solution)/shard_map/ppermute | solution.py:220
  38.4 7.9 %collective-permute-done.7.b_ref = f32[128,512]{1,0:T(8,128)S(1)} collective-permute-done((f32[128,512]{1,0:T(8,128)S(1)}, f32[128,512]{1,0:T(8,128)S(1)}, u32[]{:S(2)}, u32[]{:S(2)}) %collective-permute-start.7) | collective-permute-done | bytes 262176 | tf_op jit(solution)/shard_map/ppermute | solution.py:220
  46.3 0.0 collective-permute-done.8.d_ref
  46.3 0.1 add_pairs.6
  46.4 0.8 %collective-permute-start.10 = (f32[128,1024]{1,0:T(8,128)S(1)}, f32[128,1024]{1,0:T(8,128)S(1)}, u32[]{:S(2)}, u32[]{:S(2)}) collective-permute-start(f32[128,1024]{1,0:T(8,128)S(1)} %get-tuple-element.49.c_ref), channel_id=1, source_target_pairs={{0,16},{1,17},{2,18},{3,19},{4,12},{5,13},{6,14},{7,15},{8,24},{9,... | collective-permute-start | bytes 1572872 | tf_op jit(solution)/shard_map/ppermute | solution.py:220
  47.2 2.1 %collective-permute-start.9 = (f32[128,512]{1,0:T(8,128)S(1)}, f32[128,512]{1,0:T(8,128)S(1)}, u32[]{:S(2)}, u32[]{:S(2)}) collective-permute-start(f32[128,512]{1,0:T(8,128)S(1)} %get-tuple-element.48.a_ref), channel_id=1, source_target_pairs={{0,2},{1,3},{2,0},{3,1},{4,5},{5,4},{6,7},{7,6},{8,10},{9,11},{10,... | collective-permute-start | bytes 786440 | tf_op jit(solution)/shard_map/ppermute | solution.py:220
  49.4 7.9 %collective-permute-done.9.b_ref = f32[128,512]{1,0:T(8,128)S(1)} collective-permute-done((f32[128,512]{1,0:T(8,128)S(1)}, f32[128,512]{1,0:T(8,128)S(1)}, u32[]{:S(2)}, u32[]{:S(2)}) %collective-permute-start.9) | collective-permute-done | bytes 262176 | tf_op jit(solution)/shard_map/ppermute | solution.py:220
  57.3 0.0 collective-permute-done.10.d_ref
  57.3 0.1 add_pairs.7
  57.4 0.1 collective-permute-start.11
  57.5 1.0 %elec_charges.1 = f32[128,512]{1,0:T(8,128)} custom-call(f32[128,512]{1,0:T(8,128)S(1)} %get-tuple-element.27.rhs_ref, f32[4,128,128]{2,1,0:T(8,128)S(1)} %get-tuple-element.28.inv_ref, f32[128,512]{1,0:T(8,128)S(1)} %get-tuple-element.50.field_ref), custom_call_target="tpu_custom_call" | custom-call | bytes 3300000 | tf_op jit(solution)/shard_map/elec_charges/pallas_call | solution.py:179
  58.5 0.9 %collective-permute-done.11.other_ref = f32[128,1024]{1,0:T(8,128)S(1)} collective-permute-done((f32[128,1024]{1,0:T(8,128)S(1)}, f32[128,1024]{1,0:T(8,128)S(1)}, u32[]{:S(2)}, u32[]{:S(2)}) %collective-permute-start.11) | collective-permute-done | bytes 524320 | tf_op jit(solution)/shard_map/ppermute | solution.py:220
  59.4 1.8 %drop_charges.1 = f32[128,2048]{1,0:T(8,128)} custom-call(s32[1]{0:T(128)} %bitcast.core_ref, f32[128,2048]{1,0:T(8,128)S(1)} %get-tuple-element.29.rhs_ref, f32[16,128,128]{2,1,0:T(8,128)S(1)} %get-tuple-element.30.inv_ref, f32[128,1024]{1,0:T(8,128)S(1)} %get-tuple-element.51.own_ref, f32[128,1024]{1,0:T(8,128)S(1)} %collective-permute-done.11.other_ref), custom_call_target="tpu_custom_call" | custom-call | bytes 5940000 | tf_op jit(solution)/shard_map/drop_charges/pallas_call | solution.py:179
Async XLA Ops:
  6.7 2.1 %collective-permute-start.1 = (f32[128,1024]{1,0:T(8,128)S(1)}, f32[128,1024]{1,0:T(8,128)S(1)}, u32[]{:S(2)}, u32[]{:S(2)}) collective-permute-start(f32[128,1024]{1,0:T(8,128)S(1)} %get-tuple-element.33), channel_id=1, source_target_pairs={{0,4},{1,5},{2,6},{3,7},{4,0},{5,1},{6,2},{7,3},{8,12},{9,13},{10,... | collective-permute-start | bytes 1572872 | tf_op jit(solution)/shard_map/ppermute | solution.py:220
  8.8 11.8 %collective-permute-start.2 = (f32[128,1024]{1,0:T(8,128)S(1)}, f32[128,1024]{1,0:T(8,128)S(1)}, u32[]{:S(2)}, u32[]{:S(2)}) collective-permute-start(f32[128,1024]{1,0:T(8,128)S(1)} %add.8.c_ref), channel_id=1, source_target_pairs={{0,8},{1,9},{2,10},{3,11},{4,20},{5,21},{6,22},{7,23},{8,0},{9,1},... | collective-permute-start | bytes 1572872 | tf_op jit(solution)/shard_map/ppermute | solution.py:220
  11.7 8.9 %collective-permute-start = (f32[128,512]{1,0:T(8,128)S(1)}, f32[128,512]{1,0:T(8,128)S(1)}, u32[]{:S(2)}, u32[]{:S(2)}) collective-permute-start(f32[128,512]{1,0:T(8,128)S(1)} %get-tuple-element.31.a_ref), channel_id=1, source_target_pairs={{0,1},{1,0},{2,3},{3,2},{4,6},{5,7},{6,4},{7,5},{8,9},{9,8},{10,11... | collective-permute-start | bytes 786440 | tf_op jit(solution)/shard_map/ppermute | solution.py:220
  20.7 9.2 %collective-permute-start.4 = (f32[128,1024]{1,0:T(8,128)S(1)}, f32[128,1024]{1,0:T(8,128)S(1)}, u32[]{:S(2)}, u32[]{:S(2)}) collective-permute-start(f32[128,1024]{1,0:T(8,128)S(1)} %get-tuple-element.35.c_ref), channel_id=1, source_target_pairs={{0,16},{1,17},{2,18},{3,19},{4,12},{5,13},{6,14},{7,15},{8,24},{9,... | collective-permute-start | bytes 1572872 | tf_op jit(solution)/shard_map/ppermute | solution.py:220
  21.1 8.4 %collective-permute-start.3 = (f32[128,512]{1,0:T(8,128)S(1)}, f32[128,512]{1,0:T(8,128)S(1)}, u32[]{:S(2)}, u32[]{:S(2)}) collective-permute-start(f32[128,512]{1,0:T(8,128)S(1)} %get-tuple-element.34.a_ref), channel_id=1, source_target_pairs={{0,2},{1,3},{2,0},{3,1},{4,5},{5,4},{6,7},{7,6},{8,10},{9,11},{10,... | collective-permute-start | bytes 786440 | tf_op jit(solution)/shard_map/ppermute | solution.py:220
  30.8 2.1 %collective-permute-start.6 = (f32[128,1024]{1,0:T(8,128)S(1)}, f32[128,1024]{1,0:T(8,128)S(1)}, u32[]{:S(2)}, u32[]{:S(2)}) collective-permute-start(f32[128,1024]{1,0:T(8,128)S(1)} %get-tuple-element.45), channel_id=1, source_target_pairs={{0,4},{1,5},{2,6},{3,7},{4,0},{5,1},{6,2},{7,3},{8,12},{9,13},{10,... | collective-permute-start | bytes 1572872 | tf_op jit(solution)/shard_map/ppermute | solution.py:220
  30.9 2.6 %collective-permute-start.5 = (f32[128,1024]{1,0:T(8,128)S(1)}, f32[128,1024]{1,0:T(8,128)S(1)}, u32[]{:S(2)}, u32[]{:S(2)}) collective-permute-start(f32[128,1024]{1,0:T(8,128)S(1)} %get-tuple-element.36.field_ref), channel_id=1, source_target_pairs={{0,4},{1,5},{2,6},{3,7},{4,0},{5,1},{6,2},{7,3},{8,12},{9,13},{10,... | collective-permute-start | bytes 1572872 | tf_op jit(solution)/shard_map/ppermute | solution.py:220
  34.7 11.6 %collective-permute-start.8 = (f32[128,1024]{1,0:T(8,128)S(1)}, f32[128,1024]{1,0:T(8,128)S(1)}, u32[]{:S(2)}, u32[]{:S(2)}) collective-permute-start(f32[128,1024]{1,0:T(8,128)S(1)} %get-tuple-element.47.c_ref), channel_id=1, source_target_pairs={{0,8},{1,9},{2,10},{3,11},{4,20},{5,21},{6,22},{7,23},{8,0},{9,1},... | collective-permute-start | bytes 1572872 | tf_op jit(solution)/shard_map/ppermute | solution.py:220
  37.7 8.7 %collective-permute-start.7 = (f32[128,512]{1,0:T(8,128)S(1)}, f32[128,512]{1,0:T(8,128)S(1)}, u32[]{:S(2)}, u32[]{:S(2)}) collective-permute-start(f32[128,512]{1,0:T(8,128)S(1)} %get-tuple-element.46.a_ref), channel_id=1, source_target_pairs={{0,1},{1,0},{2,3},{3,2},{4,6},{5,7},{6,4},{7,5},{8,9},{9,8},{10,11... | collective-permute-start | bytes 786440 | tf_op jit(solution)/shard_map/ppermute | solution.py:220
  46.4 10.9 %collective-permute-start.10 = (f32[128,1024]{1,0:T(8,128)S(1)}, f32[128,1024]{1,0:T(8,128)S(1)}, u32[]{:S(2)}, u32[]{:S(2)}) collective-permute-start(f32[128,1024]{1,0:T(8,128)S(1)} %get-tuple-element.49.c_ref), channel_id=1, source_target_pairs={{0,16},{1,17},{2,18},{3,19},{4,12},{5,13},{6,14},{7,15},{8,24},{9,... | collective-permute-start | bytes 1572872 | tf_op jit(solution)/shard_map/ppermute | solution.py:220
  47.2 10.1 %collective-permute-start.9 = (f32[128,512]{1,0:T(8,128)S(1)}, f32[128,512]{1,0:T(8,128)S(1)}, u32[]{:S(2)}, u32[]{:S(2)}) collective-permute-start(f32[128,512]{1,0:T(8,128)S(1)} %get-tuple-element.48.a_ref), channel_id=1, source_target_pairs={{0,2},{1,3},{2,0},{3,1},{4,5},{5,4},{6,7},{7,6},{8,10},{9,11},{10,... | collective-permute-start | bytes 786440 | tf_op jit(solution)/shard_map/ppermute | solution.py:220
  57.4 2.0 %collective-permute-start.11 = (f32[128,1024]{1,0:T(8,128)S(1)}, f32[128,1024]{1,0:T(8,128)S(1)}, u32[]{:S(2)}, u32[]{:S(2)}) collective-permute-start(f32[128,1024]{1,0:T(8,128)S(1)} %get-tuple-element.51.own_ref), channel_id=1, source_target_pairs={{0,4},{1,5},{2,6},{3,7},{4,0},{5,1},{6,2},{7,3},{8,12},{9,13},{10,... | collective-permute-start | bytes 1572872 | tf_op jit(solution)/shard_map/ppermute | solution.py:220

commit v3 on v2

v3 whole, which is shorter than its diff:
```python
import functools
import math

import jax
import jax.numpy as jnp
from jax import lax
from jax.experimental import pallas as pl
from jax.experimental.pallas import tpu as pltpu
from jax.sharding import PartitionSpec as P

SOFTEN = 0.001
SCREEN = 1.0
LANES = 128
CHUNK = 256
VMEM = pl.BlockSpec(memory_space=pltpu.VMEM)
SMEM = pl.BlockSpec(memory_space=pltpu.SMEM)
ANY = pl.BlockSpec(memory_space=pl.ANY)
HBM = pl.BlockSpec(memory_space=pltpu.HBM)
ROWS_IN = ((1,), (0,))
ROWS_OUT = ((1,), (1,))


def couple_of(total_drop):
    return 1.0 / (3.0 * math.sqrt(total_drop))


def split(value):
    high = value.astype(jnp.bfloat16)
    low = (value - high.astype(jnp.float32)).astype(jnp.bfloat16)
    return high, low


def stacked(value):
    return jnp.concatenate(split(value), axis=0)


def product(both, weights, contract):
    weight_high, weight_low = weights
    rows = both.shape[0] // 2
    dims = (contract, ((), ()))
    first = lax.dot_general(both, weight_high, dims, preferred_element_type=jnp.float32)
    second = lax.dot_general(both[:rows], weight_low, dims, preferred_element_type=jnp.float32)
    return first[:rows] + (first[rows:] + second)


def solve_block(inverse, values):
    return product(stacked(values), split(inverse), ROWS_OUT)


def solve(inv_ref, values):
    pieces = []
    for at in range(values.shape[1] // LANES):
        pieces.append(solve_block(inv_ref[at], values[:, at * LANES : (at + 1) * LANES]))
    return jnp.concatenate(pieces, axis=1)


def gather(vert_ref, index):
    lane, tile = index % LANES, index // LANES
    found = []
    for axis in range(3):
        total = jnp.zeros(index.shape, jnp.float32)
        for at in range(vert_ref.shape[1] // LANES):
            table = jnp.broadcast_to(vert_ref[axis : axis + 1, at * LANES : (at + 1) * LANES], index.shape)
            total = jnp.where(tile == at, jnp.take_along_axis(table, lane, axis=1), total)
        found.append(total)
    return found


def fill_centres(vert_ref, conn_ref, centre):
    half_block = vert_ref.shape[1]
    for at in range(conn_ref.shape[1] // LANES):
        cols = slice(at * LANES, (at + 1) * LANES)
        corners = gather(vert_ref, conn_ref[:, cols] % half_block)
        for axis in range(3):
            g = corners[axis]
            centre[axis : axis + 1, cols] = (g[0:1] + g[1:2] + g[2:3]) / 3.0


def coupling_chunk(wide, centre, start):
    tiles = []
    for lane in range(start, start + CHUNK, LANES):
        here = slice(lane, lane + LANES)
        dx = wide[0] - centre[0:1, here]
        dy = wide[1] - centre[1:2, here]
        dz = wide[2] - centre[2:3, here]
        square = dx * dx + dy * dy + dz * dz + SOFTEN
        inverse = lax.rsqrt(square)
        tiles.append(jnp.exp((square * inverse) * -SCREEN) * inverse)
    return split(jnp.concatenate(tiles, axis=1))


def columns(place, width):
    return pl.ds(pl.multiple_of(place * width, width), width)


def spread(pos, wide):
    upright = jnp.concatenate([pos, jnp.zeros((LANES - pos.shape[0], pos.shape[1]), jnp.float32)], axis=0).T
    for axis in range(3):
        wide[axis] = jnp.broadcast_to(upright[:, axis : axis + 1], (pos.shape[1], LANES))


def first_kernel(couple, core_ref, pos_hbm, vert_hbm, conn_hbm, erhs_hbm, einv_hbm, drhs_hbm, dinv_hbm,
                 high_ref, low_ref, send_ref, wide_ref, centre_ref, elec_ref, own_ref, other_ref,
                 erhs, einv, drhs, dinv, pos, vert, conn, centre, sems):
    half = high_ref.shape[1]
    blocks = half // LANES
    moves = ((conn_hbm, conn), (vert_hbm, vert), (pos_hbm, pos), (erhs_hbm, erhs), (einv_hbm, einv),
             (drhs_hbm, drhs), (dinv_hbm, dinv))
    copies = [pltpu.make_async_copy(here, there, sems.at[at]) for at, (here, there) in enumerate(moves)]
    for copy in copies:
        copy.start()
    for copy in copies[:3]:
        copy.wait()
    spread(pos[...], wide_ref)
    fill_centres(vert, conn, centre)
    for copy in copies[3:]:
        copy.wait()
    both = stacked(solve(einv, erhs[...]))
    elec_ref[...] = both
    own, other = core_ref[0], 1 - core_ref[0]
    centre_ref[...] = centre[:, columns(own, half)]
    centres = centre[:, columns(other, half)]
    for start in range(0, half, CHUNK):
        cols = slice(start, start + CHUNK)
        weights = coupling_chunk(wide_ref, centres, start)
        high_ref[:, cols], low_ref[:, cols] = weights
        send_ref[:, cols] = product(both, weights, ROWS_IN) * couple
        for place, out_ref in ((own, own_ref), (other, other_ref)):
            block = place * blocks + start // LANES
            here = pl.ds(pl.multiple_of(place * half + start, CHUNK), CHUNK)
            out_ref[:, cols] = stacked(solve(dinv.at[pl.ds(block, CHUNK // LANES)], drhs[:, here]))


def second_kernel(couple, wide_ref, centre_ref, both_ref, own_ref, other_ref, ohigh_ref, olow_ref,
                  high_ref, low_ref, keep_ref, elec_ref):
    total = jnp.zeros(elec_ref.shape, jnp.float32)
    for start in range(0, high_ref.shape[1], CHUNK):
        cols = slice(start, start + CHUNK)
        weights = coupling_chunk(wide_ref, centre_ref, start)
        high_ref[:, cols], low_ref[:, cols] = weights
        keep_ref[:, cols] = product(both_ref[...], weights, ROWS_IN) * couple
        total = total + product(other_ref[:, cols], (ohigh_ref[:, cols], olow_ref[:, cols]), ROWS_OUT)
        total = total + product(own_ref[:, cols], weights, ROWS_OUT)
    elec_ref[...] = total * couple


def drop_charge(place, rhs_ref, inv_ref, field):
    half = field.shape[1]
    blocks = half // LANES
    return solve(inv_ref.at[pl.ds(place * blocks, blocks)], rhs_ref[:, columns(place, half)] - field)


def add_kernel(a_ref, b_ref, *rest):
    rest[-1][...] = a_ref[...] + b_ref[...]


def add_pairs_kernel(a_ref, b_ref, c_ref, d_ref, ab_ref, cd_ref):
    ab_ref[...] = a_ref[...] + b_ref[...]
    cd_ref[...] = c_ref[...] + d_ref[...]


def middle_kernel(couple, line_ref, line_got_ref, plane_ref, plane_got_ref, rhs_ref, inv_ref, high_ref, low_ref,
                  two_ref, both_ref):
    two_ref[0] = plane_ref[...] + plane_got_ref[...]
    both = stacked(solve(inv_ref, rhs_ref[...] - (line_ref[...] + line_got_ref[...])))
    both_ref[...] = both
    two_ref[1] = product(both, (high_ref[...], low_ref[...]), ROWS_IN) * couple


def own_kernel(couple, core_ref, both_ref, rhs_ref, inv_ref, two_ref, high_ref, low_ref, keep_ref, elec_ref):
    weights = high_ref[...], low_ref[...]
    keep_ref[...] = product(both_ref[...], weights, ROWS_IN) * couple
    charge = drop_charge(core_ref[0], rhs_ref, inv_ref, two_ref[0])
    elec_ref[...] = product(stacked(charge), weights, ROWS_OUT)


def plane_kernel(keep_ref, two_ref, out_ref):
    out_ref[...] = keep_ref[...] + two_ref[1]


def other_kernel(couple, core_ref, rhs_ref, inv_ref, two_ref, share_ref, high_ref, low_ref, elec_ref):
    charge = drop_charge(1 - core_ref[0], rhs_ref, inv_ref, two_ref[0])
    elec_ref[...] = (share_ref[...] + product(stacked(charge), (high_ref[...], low_ref[...]), ROWS_OUT)) * couple


def charges_kernel(core_ref, erhs_ref, einv_ref, line_ref, drhs_ref, dinv_ref, plane_ref, elec_hbm, drop_hbm,
                   elec, half, sems):
    elec[...] = solve(einv_ref, erhs_ref[...] - line_ref[...])
    elec_copy = pltpu.make_async_copy(elec, elec_hbm, sems.at[0])
    elec_copy.start()
    half[...] = drop_charge(core_ref[0], drhs_ref, dinv_ref, plane_ref[...])
    drop_copy = pltpu.make_async_copy(half, drop_hbm.at[:, columns(core_ref[0], half.shape[1])], sems.at[1])
    drop_copy.start()
    elec_copy.wait()
    drop_copy.wait()


def rest_kernel(core_ref, rhs_ref, inv_ref, field_ref, _, drop_hbm, half, sems):
    width = half.shape[1] // 2
    blocks = width // LANES
    copies = []
    for at in range(2):
        place = (1 - core_ref[0]) * 2 + at
        here = slice(at * width, (at + 1) * width)
        values = rhs_ref[:, columns(place, width)] - field_ref[:, here]
        half[:, here] = solve(inv_ref.at[pl.ds(place * blocks, blocks)], values)
        copies.append(pltpu.make_async_copy(half.at[:, here], drop_hbm.at[:, columns(place, width)], sems.at[at]))
        copies[-1].start()
    for copy in copies:
        copy.wait()


def run(kernel, name, micros, operands, specs, outs, scratch=(), out_spec=VMEM, aliases=()):
    return pl.pallas_call(
        kernel,
        out_shape=[jax.ShapeDtypeStruct(shape, dtype) for shape, dtype in outs],
        in_specs=specs,
        out_specs=[out_spec] * len(outs),
        input_output_aliases=dict(aliases),
        scratch_shapes=list(scratch),
        compiler_params=pltpu.CompilerParams(vmem_limit_bytes=32 * 2**20),
        cost_estimate=pl.CostEstimate(flops=0, bytes_accessed=int(micros * 3.3e6), transcendentals=0),
        name=name,
    )(*operands)


def add(left, right, *after):
    return run(
        add_kernel, "add", 0.1, (left, right, *after), [VMEM] * 2 + [ANY] * len(after), [(left.shape, jnp.float32)]
    )[0]


def exchanges(elec_devices, drop_devices):
    def pairs(partner):
        out = []
        for elec in range(elec_devices):
            for drop in range(drop_devices):
                to_elec, to_drop = partner(elec, drop)
                out.append((elec * drop_devices + drop, to_elec * drop_devices + to_drop))
        return out

    def ordered(bits, step, core):
        return bits[step] if core == 0 else bits[len(bits) - 1 - step]

    chip_bits = range(1, elec_devices.bit_length() - 1)
    drop_bits = range(drop_devices.bit_length() - 1)
    core = pairs(lambda e, d: (e ^ 1, d))
    plane = [
        pairs(lambda e, d, s=s: (e ^ (1 << ordered(chip_bits, s, e & 1)), d)) for s in range(len(chip_bits))
    ]
    line = [
        pairs(lambda e, d, s=s: (e, d ^ (1 << ordered(drop_bits, s, e & 1)))) for s in range(len(drop_bits))
    ]
    return core, plane, line


def solution(mesh):
    elec_devices, drop_devices = mesh.shape["elec"], mesh.shape["drop"]
    core_pairs, plane_pairs, line_pairs = exchanges(elec_devices, drop_devices)

    def swap(value, pairs):
        return lax.ppermute(value, ("elec", "drop"), pairs)

    def sums(line, plane):
        for at in range(max(len(line_pairs), len(plane_pairs)) - 1):
            line_got = swap(line, line_pairs[at]) if at < len(line_pairs) - 1 else jnp.zeros_like(line)
            plane_got = swap(plane, plane_pairs[at]) if at < len(plane_pairs) - 1 else jnp.zeros_like(plane)
            plane = add(plane, plane_got)
            line = add(line, line_got, plane)
        return line, swap(line, line_pairs[-1]), plane, swap(plane, plane_pairs[-1])

    def on_device(elec_pos, drop_vert, drop_conn, elec_rhs, drop_rhs, elec_inv, drop_inv):
        f32, bf16 = jnp.float32, jnp.bfloat16
        rows, elec = elec_rhs.shape
        drop = drop_rhs.shape[1]
        half = drop // 2
        couple = couple_of(drop * drop_devices)
        core = (lax.axis_index("elec") % 2).astype(jnp.int32).reshape(1)

        inputs = (elec_pos, drop_vert, drop_conn, elec_rhs, elec_inv, drop_rhs, drop_inv)
        outs = [((elec, half), bf16)] * 2 + [((rows, half), f32), ((3, elec, LANES), f32), ((8, half), f32)]
        outs += [((2 * rows, elec), bf16)] + [((2 * rows, half), bf16)] * 2 + [(value.shape, f32) for value in inputs[3:]]
        (other_high, other_low, send, wide, centre, both, own_charge, other_charge,
         elec_rhs, elec_inv, drop_rhs, drop_inv) = run(
            functools.partial(first_kernel, couple), "coupling_other_half", 4.0,
            (core, *(pltpu.with_memory_space_constraint(value, pltpu.HBM) for value in inputs)),
            [SMEM] + [HBM] * 7,
            outs,
            [pltpu.VMEM(value.shape, value.dtype) for value in inputs[:3]]
            + [pltpu.VMEM((8, drop), f32), pltpu.SemaphoreType.DMA((7,))],
        )
        got = swap(send, core_pairs)
        own_high, own_low, keep, line = run(
            functools.partial(second_kernel, couple), "coupling_own_half", 2.0,
            (wide, centre, both, own_charge, other_charge, other_high, other_low),
            [VMEM] * 7,
            [((elec, half), bf16)] * 2 + [((rows, half), f32), ((rows, elec), f32)],
        )
        parts = sums(line, add(keep, got, line))

        two, both = run(
            functools.partial(middle_kernel, couple), "elec_charges_to_drop_field", 0.8,
            (*parts, elec_rhs, elec_inv, other_high, other_low),
            [VMEM] * 8,
            [((2, rows, half), f32), ((2 * rows, elec), bf16)],
        )
        two_got = swap(two, core_pairs)
        keep, share = run(
            functools.partial(own_kernel, couple), "fields_of_own_half", 1.5,
            (core, both, drop_rhs, drop_inv, two, own_high, own_low),
            [SMEM] + [VMEM] * 6,
            [((rows, half), f32), ((rows, elec), f32)],
        )
        plane, = run(plane_kernel, "add", 0.1, (keep, two_got), [VMEM] * 2, [((rows, half), f32)])
        line, = run(
            functools.partial(other_kernel, couple), "elec_field_of_other_half", 1.0,
            (core, drop_rhs, drop_inv, two_got, share, other_high, other_low),
            [SMEM] + [VMEM] * 6,
            [((rows, elec), f32)],
        )
        parts = sums(line, plane)

        line, plane = run(
            add_pairs_kernel, "add_pairs", 0.1, parts, [VMEM] * 4, [((rows, elec), f32), ((rows, half), f32)]
        )
        plane_got = swap(plane, core_pairs)
        outs = [((rows, elec), f32), ((rows, drop), f32)]
        charge_elec, charge_drop = run(
            charges_kernel, "charges_of_own_half", 1.3,
            (core, elec_rhs, elec_inv, line, drop_rhs, drop_inv, plane),
            [SMEM] + [VMEM] * 6,
            outs,
            [pltpu.VMEM((rows, elec), f32), pltpu.VMEM((rows, half), f32), pltpu.SemaphoreType.DMA((2,))],
            out_spec=HBM,
        )
        charge_drop, = run(
            rest_kernel, "charges_of_other_half", 1.0,
            (core, drop_rhs, drop_inv, plane_got, charge_drop),
            [SMEM] + [VMEM] * 3 + [HBM],
            outs[1:],
            [pltpu.VMEM((rows, half), f32), pltpu.SemaphoreType.DMA((2,))],
            out_spec=HBM,
            aliases={4: 0},
        )
        return (charge_elec, charge_drop)

    placed = (
        P(None, "elec"),
        P(None, "drop"),
        P(None, "drop"),
        P(None, "elec"),
        P(None, "drop"),
        P("elec", None, None),
        P("drop", None, None),
    )
    return jax.shard_map(
        on_device,
        mesh=mesh,
        in_specs=placed,
        out_specs=(P(None, "elec"), P(None, "drop")),
        check_vma=False,
    )
```

time: 61.3 us -> 57.7 us (0.941)
  waiting for transfers between devices: 31.9 us -> 29.1 us
  starting transfers between devices: 15.8 us -> 14.6 us
    ppermute x12 -> x11, waiting for transfers between devices: 31.9 us -> 29.1 us  [swap(): return lax.ppermute(value, ('elec', 'drop'), pairs)]
    ppermute x12 -> x11, starting transfers between devices: 15.8 us -> 14.6 us  [swap(): return lax.ppermute(value, ('elec', 'drop'), pairs)]
    pallas_call x10 -> x14, Pallas kernels: 12.7 us -> 13 us  [run(): pl.pallas_call(kernel, out_shape=[jax.ShapeDtypeStruct(shape, dtype) for...]
  transfers between devices with their start and end apart: 12 -> 11, of which waited for: 8 -> 7; matrix products, arithmetic and copies ran while one was open for 0% -> 0% of each run, Pallas kernels for 4% -> 12%
where the time goes in v3:
time: 57.7 us; the launch traced here: 57.5 us
  waiting for transfers between devices  29.1 us (50%)
  starting transfers between devices  14.6 us (25%)
  Pallas kernels  13 us (23%)
  between operations  0.76 us (1%)
    ppermute x11, waiting for transfers between devices, swap(): return lax.ppermute(value, ('elec', 'drop'), pairs)  29.1 us
    ppermute x11, starting transfers between devices, swap(): return lax.ppermute(value, ('elec', 'drop'), pairs)  14.6 us
    pallas_call x14, Pallas kernels, run(): pl.pallas_call(kernel, out_shape=[jax.ShapeDtypeStruct(shape, dtype) for...  13 us
  transfers between devices with their start and end apart: 11, of which 7 were waited for; matrix products, arithmetic and copies ran while one was open for 0% of the time, Pallas kernels for 12%

profile of v3, /device:TPU:0, one launch (start us, length us, event | category | flops | bytes accessed | tf_op | source)
XLA Modules:
  0.0 57.5 jit_solution(4798996956906576571)
XLA Ops:
  0.6 4.1 %coupling_other_half.1 = (bf16[512,1024]{1,0:T(8,128)(2,1)S(1)}, bf16[512,1024]{1,0:T(8,128)(2,1)S(1)}, f32[128,1024]{1,0:T(8,128)S(1)}, f32[3,512,128]{2,1,0:T(...) custom-call(s32[1]{0:T(128)} %bitcast.core_ref, ...), custom_call_target="tpu_custom_call" | custom-call | bytes 13200000 | tf_op jit(solution)/shard_map/coupling_other_half/pallas_call | solution.py:214
  4.7 0.5 collective-permute-start.1
  5.2 2.4 %coupling_own_half.1 = (bf16[512,1024]{1,0:T(8,128)(2,1)S(1)}, bf16[512,1024]{1,0:T(8,128)(2,1)S(1)}, f32[128,1024]{1,0:T(8,128)S(1)}, f32[128,512]{1,0:T(8,128)S(1)}) custom-call(f32[3,512,128]{2,1,0:T(8,128)S(1)} %get-tuple-element.30.wide_ref, f32[8,1024]{1,0:T(8,128)S(1)} %get-tuple-element.31.centre_ref, ...), custom_call_target="tpu_custom_call" | custom-call | bytes 6600000 | tf_op jit(solution)/shard_map/coupling_own_half/pallas_call | solution.py:214
  7.6 0.0 collective-permute-done.1.b_ref
  7.7 0.1 add.11.a_ref
  7.7 2.6 %collective-permute-start.2 = (f32[128,1024]{1,0:T(8,128)S(1)}, f32[128,1024]{1,0:T(8,128)S(1)}, u32[]{:S(2)}, u32[]{:S(2)}) collective-permute-start(f32[128,1024]{1,0:T(8,128)S(1)} %add.11.a_ref), channel_id=1, source_target_pairs={{0,8},{1,9},{2,10},{3,11},{4,20},{5,21},{6,22},{7,23},{8,0},{9,1},... | collective-permute-start | bytes 1572872 | tf_op jit(solution)/shard_map/ppermute | solution.py:262
  10.3 1.6 %collective-permute-start = (f32[128,512]{1,0:T(8,128)S(1)}, f32[128,512]{1,0:T(8,128)S(1)}, u32[]{:S(2)}, u32[]{:S(2)}) collective-permute-start(f32[128,512]{1,0:T(8,128)S(1)} %get-tuple-element.37.rest_0_.a_ref), channel_id=1, source_target_pairs={{0,1},{1,0},{2,3},{3,2},{4,6},{5,7},{6,4},{7,5},{8,9},{9,8},{10,11... | collective-permute-start | bytes 786440 | tf_op jit(solution)/shard_map/ppermute | solution.py:262
  11.9 5.6 %collective-permute-done.2.b_ref = f32[128,1024]{1,0:T(8,128)S(1)} collective-permute-done((f32[128,1024]{1,0:T(8,128)S(1)}, f32[128,1024]{1,0:T(8,128)S(1)}, u32[]{:S(2)}, u32[]{:S(2)}) %collective-permute-start.2) | collective-permute-done | bytes 524320 | tf_op jit(solution)/shard_map/ppermute | solution.py:262
  17.4 0.1 add.12.rest_0_.plane_ref
  17.5 2.1 %collective-permute-start.4 = (f32[128,1024]{1,0:T(8,128)S(1)}, f32[128,1024]{1,0:T(8,128)S(1)}, u32[]{:S(2)}, u32[]{:S(2)}) collective-permute-start(f32[128,1024]{1,0:T(8,128)S(1)} %add.12.rest_0_.plane_ref), channel_id=1, source_target_pairs={{0,16},{1,17},{2,18},{3,19},{4,12},{5,13},{6,14},{7,15},{8,24},{9,... | collective-permute-start | bytes 1572872 | tf_op jit(solution)/shard_map/ppermute | solution.py:262
  19.6 0.0 collective-permute-done.b_ref
  19.7 2.7 %collective-permute-start.3 = (f32[128,512]{1,0:T(8,128)S(1)}, f32[128,512]{1,0:T(8,128)S(1)}, u32[]{:S(2)}, u32[]{:S(2)}) collective-permute-start(f32[128,512]{1,0:T(8,128)S(1)} %add.13.line_ref), channel_id=1, source_target_pairs={{0,2},{1,3},{2,0},{3,1},{4,5},{5,4},{6,7},{7,6},{8,10},{9,11},{10,... | collective-permute-start | bytes 786440 | tf_op jit(solution)/shard_map/ppermute | solution.py:262
  22.3 7.5 %collective-permute-done.3.line_got_ref = f32[128,512]{1,0:T(8,128)S(1)} collective-permute-done((f32[128,512]{1,0:T(8,128)S(1)}, f32[128,512]{1,0:T(8,128)S(1)}, u32[]{:S(2)}, u32[]{:S(2)}) %collective-permute-start.3) | collective-permute-done | bytes 262176 | tf_op jit(solution)/shard_map/ppermute | solution.py:262
  29.9 0.0 collective-permute-done.4.plane_got_ref
  29.9 0.9 %elec_charges_to_drop_field.1 = (f32[2,128,1024]{2,1,0:T(8,128)S(1)}, bf16[256,512]{1,0:T(8,128)(2,1)S(1)}) custom-call(f32[128,512]{1,0:T(8,128)S(1)} %add.13.line_ref, f32[128,512]{1,0:T(8,128)S(1)} %collective-permute-done.3.line_got_ref, f32[128,1024]{1,0:T(8,128)S(1)} %add.12.rest_0_.plane_ref, f32[128,1024]{1,0:T(8,128)S(1)} %collective-permute-done.4.plane_got_ref, ...), custom_call_target="tpu_custom_call" | custom-call | bytes 2640000 | tf_op jit(solution)/shard_map/elec_charges_to_drop_field/pallas_call | solution.py:214
  30.7 0.1 collective-permute-start.5
  30.8 1.5 %fields_of_own_half.1 = (f32[128,1024]{1,0:T(8,128)S(1)}, f32[128,512]{1,0:T(8,128)S(1)}) custom-call(s32[1]{0:T(128)} %bitcast.core_ref, bf16[256,512]{1,0:T(8,128)(2,1)S(1)} %get-tuple-element.41.both_ref, f32[128,2048]{1,0:T(8,128)S(1)} %get-tuple-element.28.rhs_ref.drhs_ref, f32[16,128,128]{2,1,0:T(8,128)S(1)} %get-tuple-element.29.inv_ref.dinv_ref, ...), custom_call_target="tpu_custom_call" | custom-call | bytes 4950000 | tf_op jit(solution)/shard_map/fields_of_own_half/pallas_call | solution.py:214
  32.3 1.1 %collective-permute-done.5.two_ref = f32[2,128,1024]{2,1,0:T(8,128)S(1)} collective-permute-done((f32[2,128,1024]{2,1,0:T(8,128)S(1)}, f32[2,128,1024]{2,1,0:T(8,128)S(1)}, u32[]{:S(2)}, u32[]{:S(2)}) %collective-permute-start.5) | collective-permute-done | bytes 1048608 | tf_op jit(solution)/shard_map/ppermute | solution.py:262
  33.4 0.1 add.14.a_ref
  33.5 1.5 %collective-permute-start.7 = (f32[128,1024]{1,0:T(8,128)S(1)}, f32[128,1024]{1,0:T(8,128)S(1)}, u32[]{:S(2)}, u32[]{:S(2)}) collective-permute-start(f32[128,1024]{1,0:T(8,128)S(1)} %add.14.a_ref), channel_id=1, source_target_pairs={{0,8},{1,9},{2,10},{3,11},{4,20},{5,21},{6,22},{7,23},{8,0},{9,1},... | collective-permute-start | bytes 1572872 | tf_op jit(solution)/shard_map/ppermute | solution.py:262
  35.1 1.1 %elec_field_of_other_half.1.a_ref = f32[128,512]{1,0:T(8,128)S(1)} custom-call(s32[1]{0:T(128)} %bitcast.core_ref, f32[128,2048]{1,0:T(8,128)S(1)} %get-tuple-element.28.rhs_ref.drhs_ref, f32[16,128,128]{2,1,0:T(8,128)S(1)} %get-tuple-element.29.inv_ref.dinv_ref, f32[2,128,1024]{2,1,0:T(8,128)S(1)} %collective-permute-done.5.two_ref, ...), custom_call_target="tpu_custom_call" | custom-call | bytes 3300000 | tf_op jit(solution)/shard_map/elec_field_of_other_half/pallas_call | solution.py:214
  36.2 0.8 %collective-permute-start.6 = (f32[128,512]{1,0:T(8,128)S(1)}, f32[128,512]{1,0:T(8,128)S(1)}, u32[]{:S(2)}, u32[]{:S(2)}) collective-permute-start(f32[128,512]{1,0:T(8,128)S(1)} %elec_field_of_other_half.1.a_ref), channel_id=1, source_target_pairs={{0,1},{1,0},{2,3},{3,2},{4,6},{5,7},{6,4},{7,5},{8,9},{9,8},{10,11... | collective-permute-start | bytes 786440 | tf_op jit(solution)/shard_map/ppermute | solution.py:262
  37.0 5.8 %collective-permute-done.7.b_ref = f32[128,1024]{1,0:T(8,128)S(1)} collective-permute-done((f32[128,1024]{1,0:T(8,128)S(1)}, f32[128,1024]{1,0:T(8,128)S(1)}, u32[]{:S(2)}, u32[]{:S(2)}) %collective-permute-start.7) | collective-permute-done | bytes 524320 | tf_op jit(solution)/shard_map/ppermute | solution.py:262
  42.8 0.1 add.15.rest_0_.c_ref
  42.8 0.1 collective-permute-start.9
  42.9 1.1 %collective-permute-done.6.b_ref = f32[128,512]{1,0:T(8,128)S(1)} collective-permute-done((f32[128,512]{1,0:T(8,128)S(1)}, f32[128,512]{1,0:T(8,128)S(1)}, u32[]{:S(2)}, u32[]{:S(2)}) %collective-permute-start.6) | collective-permute-done | bytes 262176 | tf_op jit(solution)/shard_map/ppermute | solution.py:262
  44.1 2.7 %collective-permute-start.8 = (f32[128,512]{1,0:T(8,128)S(1)}, f32[128,512]{1,0:T(8,128)S(1)}, u32[]{:S(2)}, u32[]{:S(2)}) collective-permute-start(f32[128,512]{1,0:T(8,128)S(1)} %add.16.a_ref), channel_id=1, source_target_pairs={{0,2},{1,3},{2,0},{3,1},{4,5},{5,4},{6,7},{7,6},{8,10},{9,11},{10,... | collective-permute-start | bytes 786440 | tf_op jit(solution)/shard_map/ppermute | solution.py:262
  46.7 7.5 %collective-permute-done.8.b_ref = f32[128,512]{1,0:T(8,128)S(1)} collective-permute-done((f32[128,512]{1,0:T(8,128)S(1)}, f32[128,512]{1,0:T(8,128)S(1)}, u32[]{:S(2)}, u32[]{:S(2)}) %collective-permute-start.8) | collective-permute-done | bytes 262176 | tf_op jit(solution)/shard_map/ppermute | solution.py:262
  54.3 0.0 collective-permute-done.9.d_ref
  54.3 0.1 add_pairs.1
  54.4 0.1 collective-permute-start.10
  54.4 1.5 %charges_of_own_half.1 = (f32[128,512]{1,0:T(8,128)}, f32[128,2048]{1,0:T(8,128)}) custom-call(s32[1]{0:T(128)} %bitcast.core_ref, f32[128,512]{1,0:T(8,128)S(1)} %get-tuple-element.26.rhs_ref.erhs_ref, f32[4,128,128]{2,1,0:T(8,128)S(1)} %get-tuple-element.27.inv_ref.einv_ref, f32[128,512]{1,0:T(8,128)S(1)} %get-tuple-element.46.line_ref, ...), custom_call_target="tpu_custom_call" | custom-call | bytes 4290000 | tf_op jit(solution)/shard_map/charges_of_own_half/pallas_call | solution.py:214
  55.9 0.4 collective-permute-done.10.field_ref
  56.3 1.2 %charges_of_other_half.1 = f32[128,2048]{1,0:T(8,128)} custom-call(s32[1]{0:T(128)} %bitcast.core_ref, f32[128,2048]{1,0:T(8,128)S(1)} %get-tuple-element.28.rhs_ref.drhs_ref, f32[16,128,128]{2,1,0:T(8,128)S(1)} %get-tuple-element.29.inv_ref.dinv_ref, f32[128,1024]{1,0:T(8,128)S(1)} %collective-permute-done.10.field_ref, ...), custom_call_target="tpu_custom_call", output_to_operand_aliasing={{}: (4, {})} | custom-call | bytes 3300000 | tf_op jit(solution)/shard_map/charges_of_other_half/pallas_call | solution.py:214
  (2 shorter events, 0.1 us)
Async XLA Ops:
  4.7 2.9 %collective-permute-start.1 = (f32[128,1024]{1,0:T(8,128)S(1)}, f32[128,1024]{1,0:T(8,128)S(1)}, u32[]{:S(2)}, u32[]{:S(2)}) collective-permute-start(f32[128,1024]{1,0:T(8,128)S(1)} %get-tuple-element.39), channel_id=1, source_target_pairs={{0,4},{1,5},{2,6},{3,7},{4,0},{5,1},{6,2},{7,3},{8,12},{9,13},{10,... | collective-permute-start | bytes 1572872 | tf_op jit(solution)/shard_map/ppermute | solution.py:262
  7.7 9.7 %collective-permute-start.2 = (f32[128,1024]{1,0:T(8,128)S(1)}, f32[128,1024]{1,0:T(8,128)S(1)}, u32[]{:S(2)}, u32[]{:S(2)}) collective-permute-start(f32[128,1024]{1,0:T(8,128)S(1)} %add.11.a_ref), channel_id=1, source_target_pairs={{0,8},{1,9},{2,10},{3,11},{4,20},{5,21},{6,22},{7,23},{8,0},{9,1},... | collective-permute-start | bytes 1572872 | tf_op jit(solution)/shard_map/ppermute | solution.py:262
  10.3 9.3 %collective-permute-start = (f32[128,512]{1,0:T(8,128)S(1)}, f32[128,512]{1,0:T(8,128)S(1)}, u32[]{:S(2)}, u32[]{:S(2)}) collective-permute-start(f32[128,512]{1,0:T(8,128)S(1)} %get-tuple-element.37.rest_0_.a_ref), channel_id=1, source_target_pairs={{0,1},{1,0},{2,3},{3,2},{4,6},{5,7},{6,4},{7,5},{8,9},{9,8},{10,11... | collective-permute-start | bytes 786440 | tf_op jit(solution)/shard_map/ppermute | solution.py:262
  17.5 12.3 %collective-permute-start.4 = (f32[128,1024]{1,0:T(8,128)S(1)}, f32[128,1024]{1,0:T(8,128)S(1)}, u32[]{:S(2)}, u32[]{:S(2)}) collective-permute-start(f32[128,1024]{1,0:T(8,128)S(1)} %add.12.rest_0_.plane_ref), channel_id=1, source_target_pairs={{0,16},{1,17},{2,18},{3,19},{4,12},{5,13},{6,14},{7,15},{8,24},{9,... | collective-permute-start | bytes 1572872 | tf_op jit(solution)/shard_map/ppermute | solution.py:262
  19.7 10.2 %collective-permute-start.3 = (f32[128,512]{1,0:T(8,128)S(1)}, f32[128,512]{1,0:T(8,128)S(1)}, u32[]{:S(2)}, u32[]{:S(2)}) collective-permute-start(f32[128,512]{1,0:T(8,128)S(1)} %add.13.line_ref), channel_id=1, source_target_pairs={{0,2},{1,3},{2,0},{3,1},{4,5},{5,4},{6,7},{7,6},{8,10},{9,11},{10,... | collective-permute-start | bytes 786440 | tf_op jit(solution)/shard_map/ppermute | solution.py:262
  30.7 2.7 %collective-permute-start.5 = (f32[2,128,1024]{2,1,0:T(8,128)S(1)}, f32[2,128,1024]{2,1,0:T(8,128)S(1)}, u32[]{:S(2)}, u32[]{:S(2)}) collective-permute-start(f32[2,128,1024]{2,1,0:T(8,128)S(1)} %get-tuple-element.40.two_ref), channel_id=1, source_target_pairs={{0,4},{1,5},{2,6},{3,7},{4,0},{5,1},{6,2},{7,3},{8,12},{9,13},{10,... | collective-permute-start | bytes 3145736 | tf_op jit(solution)/shard_map/ppermute | solution.py:262
  33.5 9.2 %collective-permute-start.7 = (f32[128,1024]{1,0:T(8,128)S(1)}, f32[128,1024]{1,0:T(8,128)S(1)}, u32[]{:S(2)}, u32[]{:S(2)}) collective-permute-start(f32[128,1024]{1,0:T(8,128)S(1)} %add.14.a_ref), channel_id=1, source_target_pairs={{0,8},{1,9},{2,10},{3,11},{4,20},{5,21},{6,22},{7,23},{8,0},{9,1},... | collective-permute-start | bytes 1572872 | tf_op jit(solution)/shard_map/ppermute | solution.py:262
  36.2 7.8 %collective-permute-start.6 = (f32[128,512]{1,0:T(8,128)S(1)}, f32[128,512]{1,0:T(8,128)S(1)}, u32[]{:S(2)}, u32[]{:S(2)}) collective-permute-start(f32[128,512]{1,0:T(8,128)S(1)} %elec_field_of_other_half.1.a_ref), channel_id=1, source_target_pairs={{0,1},{1,0},{2,3},{3,2},{4,6},{5,7},{6,4},{7,5},{8,9},{9,8},{10,11... | collective-permute-start | bytes 786440 | tf_op jit(solution)/shard_map/ppermute | solution.py:262
  42.8 11.4 %collective-permute-start.9 = (f32[128,1024]{1,0:T(8,128)S(1)}, f32[128,1024]{1,0:T(8,128)S(1)}, u32[]{:S(2)}, u32[]{:S(2)}) collective-permute-start(f32[128,1024]{1,0:T(8,128)S(1)} %add.15.rest_0_.c_ref), channel_id=1, source_target_pairs={{0,16},{1,17},{2,18},{3,19},{4,12},{5,13},{6,14},{7,15},{8,24},{9,... | collective-permute-start | bytes 1572872 | tf_op jit(solution)/shard_map/ppermute | solution.py:262
  44.1 10.2 %collective-permute-start.8 = (f32[128,512]{1,0:T(8,128)S(1)}, f32[128,512]{1,0:T(8,128)S(1)}, u32[]{:S(2)}, u32[]{:S(2)}) collective-permute-start(f32[128,512]{1,0:T(8,128)S(1)} %add.16.a_ref), channel_id=1, source_target_pairs={{0,2},{1,3},{2,0},{3,1},{4,5},{5,4},{6,7},{7,6},{8,10},{9,11},{10,... | collective-permute-start | bytes 786440 | tf_op jit(solution)/shard_map/ppermute | solution.py:262
  54.4 2.0 %collective-permute-start.10 = (f32[128,1024]{1,0:T(8,128)S(1)}, f32[128,1024]{1,0:T(8,128)S(1)}, u32[]{:S(2)}, u32[]{:S(2)}) collective-permute-start(f32[128,1024]{1,0:T(8,128)S(1)} %get-tuple-element.47.plane_ref), channel_id=1, source_target_pairs={{0,4},{1,5},{2,6},{3,7},{4,0},{5,1},{6,2},{7,3},{8,12},{9,13},{10,... | collective-permute-start | bytes 1572872 | tf_op jit(solution)/shard_map/ppermute | solution.py:262

commit v4 on v3

--- a/solution.py
+++ b/solution.py
@@ -12,6 +12,7 @@
 SCREEN = 1.0
 LANES = 128
 CHUNK = 256
+PARTS = 2
 VMEM = pl.BlockSpec(memory_space=pltpu.VMEM)
 SMEM = pl.BlockSpec(memory_space=pltpu.SMEM)
 ANY = pl.BlockSpec(memory_space=pl.ANY)
@@ -154,60 +155,73 @@
     rest[-1][...] = a_ref[...] + b_ref[...]
 
 
-def add_pairs_kernel(a_ref, b_ref, c_ref, d_ref, ab_ref, cd_ref):
-    ab_ref[...] = a_ref[...] + b_ref[...]
-    cd_ref[...] = c_ref[...] + d_ref[...]
-
-
-def middle_kernel(couple, line_ref, line_got_ref, plane_ref, plane_got_ref, rhs_ref, inv_ref, high_ref, low_ref,
-                  two_ref, both_ref):
-    two_ref[0] = plane_ref[...] + plane_got_ref[...]
-    both = stacked(solve(inv_ref, rhs_ref[...] - (line_ref[...] + line_got_ref[...])))
+def fill(refs, value):
+    rows = refs[0].shape[0]
+    for at, ref in enumerate(refs):
+        ref[...] = value[at * rows : (at + 1) * rows]
+
+
+def fold_kernel(a_ref, b_ref, *refs):
+    fill(refs[-PARTS:], a_ref[...] + b_ref[...])
+
+
+def whole(refs):
+    return jnp.concatenate([ref[...] for ref in refs], axis=0)
+
+
+def join_kernel(*refs):
+    refs[-1][...] = whole(refs[:PARTS]) + whole(refs[PARTS : 2 * PARTS])
+
+
+def to_drop_kernel(couple, left_ref, right_ref, rhs_ref, inv_ref, high_ref, low_ref, send_ref, both_ref):
+    both = stacked(solve(inv_ref, rhs_ref[...] - (left_ref[...] + right_ref[...])))
     both_ref[...] = both
-    two_ref[1] = product(both, (high_ref[...], low_ref[...]), ROWS_IN) * couple
-
-
-def own_kernel(couple, core_ref, both_ref, rhs_ref, inv_ref, two_ref, high_ref, low_ref, keep_ref, elec_ref):
-    weights = high_ref[...], low_ref[...]
-    keep_ref[...] = product(both_ref[...], weights, ROWS_IN) * couple
-    charge = drop_charge(core_ref[0], rhs_ref, inv_ref, two_ref[0])
-    elec_ref[...] = product(stacked(charge), weights, ROWS_OUT)
-
-
-def plane_kernel(keep_ref, two_ref, out_ref):
-    out_ref[...] = keep_ref[...] + two_ref[1]
-
-
-def other_kernel(couple, core_ref, rhs_ref, inv_ref, two_ref, share_ref, high_ref, low_ref, elec_ref):
-    charge = drop_charge(1 - core_ref[0], rhs_ref, inv_ref, two_ref[0])
+    send_ref[...] = product(both, (high_ref[...], low_ref[...]), ROWS_IN) * couple
+
+
+def keep_kernel(couple, both_ref, high_ref, low_ref, keep_ref):
+    keep_ref[...] = product(both_ref[...], (high_ref[...], low_ref[...]), ROWS_IN) * couple
+
+
+def own_kernel(core_ref, rhs_ref, inv_ref, field_ref, high_ref, low_ref, elec_ref):
+    charge = drop_charge(core_ref[0], rhs_ref, inv_ref, field_ref[...])
+    elec_ref[...] = product(stacked(charge), (high_ref[...], low_ref[...]), ROWS_OUT)
+
+
+def other_kernel(couple, core_ref, rhs_ref, inv_ref, field_ref, share_ref, high_ref, low_ref, elec_ref):
+    charge = drop_charge(1 - core_ref[0], rhs_ref, inv_ref, field_ref[...])
     elec_ref[...] = (share_ref[...] + product(stacked(charge), (high_ref[...], low_ref[...]), ROWS_OUT)) * couple
 
 
-def charges_kernel(core_ref, erhs_ref, einv_ref, line_ref, drhs_ref, dinv_ref, plane_ref, elec_hbm, drop_hbm,
-                   elec, half, sems):
-    elec[...] = solve(einv_ref, erhs_ref[...] - line_ref[...])
-    elec_copy = pltpu.make_async_copy(elec, elec_hbm, sems.at[0])
-    elec_copy.start()
-    half[...] = drop_charge(core_ref[0], drhs_ref, dinv_ref, plane_ref[...])
-    drop_copy = pltpu.make_async_copy(half, drop_hbm.at[:, columns(core_ref[0], half.shape[1])], sems.at[1])
-    drop_copy.start()
-    elec_copy.wait()
-    drop_copy.wait()
-
-
-def rest_kernel(core_ref, rhs_ref, inv_ref, field_ref, _, drop_hbm, half, sems):
-    width = half.shape[1] // 2
-    blocks = width // LANES
+def charges_kernel(is_other, at, core_ref, rhs_ref, inv_ref, *refs):
+    out_ref = refs[-1]
+    rows, half = out_ref.shape
+    blocks = half // LANES
+    place = jnp.abs(core_ref[0] - is_other)
+    values = rhs_ref[at * rows : (at + 1) * rows, columns(place, half)] - whole(refs[:-1])
+    out_ref[...] = solve(inv_ref.at[pl.ds(place * blocks, blocks)], values)
+
+
+def last_kernel(core_ref, rhs_ref, inv_ref, own_first_ref, own_last_ref, other_first_ref, left_ref, right_ref, drop_hbm,
+                token_ref, other_last, sems):
+    token_ref[...] = jnp.zeros_like(token_ref)
+    rows, half = other_last.shape
+    own, other = columns(core_ref[0], half), columns(1 - core_ref[0], half)
     copies = []
-    for at in range(2):
-        place = (1 - core_ref[0]) * 2 + at
-        here = slice(at * width, (at + 1) * width)
-        values = rhs_ref[:, columns(place, width)] - field_ref[:, here]
-        half[:, here] = solve(inv_ref.at[pl.ds(place * blocks, blocks)], values)
-        copies.append(pltpu.make_async_copy(half.at[:, here], drop_hbm.at[:, columns(place, width)], sems.at[at]))
+    for at, (ref, part, cols) in enumerate(
+        ((own_first_ref, 0, own), (own_last_ref, 1, own), (other_first_ref, 0, other), (other_last, 1, other))
+    ):
+        if at == 3:
+            charges_kernel(1, 1, core_ref, rhs_ref, inv_ref, left_ref, right_ref, other_last)
+        place = drop_hbm.at[part * rows : (part + 1) * rows, cols]
+        copies.append(pltpu.make_async_copy(ref, place, sems.at[at]))
         copies[-1].start()
     for copy in copies:
         copy.wait()
+
+
+def elec_kernel(rhs_ref, inv_ref, left_ref, right_ref, after, out_ref):
+    out_ref[...] = solve(inv_ref, rhs_ref[...] - (left_ref[...] + right_ref[...]))
 
 
 def run(kernel, name, micros, operands, specs, outs, scratch=(), out_spec=VMEM, aliases=()):
@@ -230,6 +244,19 @@
     )[0]
 
 
+def run_last(core, drop_rhs, drop_inv, done, fields):
+    rows, half = done[0].shape
+    return pl.pallas_call(
+        last_kernel,
+        out_shape=[jax.ShapeDtypeStruct(drop_rhs.shape, jnp.float32), jax.ShapeDtypeStruct((8, LANES), jnp.float32)],
+        in_specs=[SMEM] + [VMEM] * 7,
+        out_specs=[HBM, VMEM],
+        scratch_shapes=[pltpu.VMEM((rows, half), jnp.float32), pltpu.SemaphoreType.DMA((4,))],
+        compiler_params=pltpu.CompilerParams(vmem_limit_bytes=32 * 2**20),
+        name="last_drop_charges",
+    )(core, drop_rhs, drop_inv, *done, *fields)
+
+
 def exchanges(elec_devices, drop_devices):
     def pairs(partner):
         out = []
@@ -261,13 +288,13 @@
     def swap(value, pairs):
         return lax.ppermute(value, ("elec", "drop"), pairs)
 
-    def sums(line, plane):
+    def steps(line, planes):
         for at in range(max(len(line_pairs), len(plane_pairs)) - 1):
-            line_got = swap(line, line_pairs[at]) if at < len(line_pairs) - 1 else jnp.zeros_like(line)
-            plane_got = swap(plane, plane_pairs[at]) if at < len(plane_pairs) - 1 else jnp.zeros_like(plane)
-            plane = add(plane, plane_got)
-            line = add(line, line_got, plane)
-        return line, swap(line, line_pairs[-1]), plane, swap(plane, plane_pairs[-1])
+            if at < len(line_pairs) - 1:
+                line = add(line, swap(line, line_pairs[at]))
+            if at < len(plane_pairs) - 1:
+                planes = [add(plane, swap(plane, plane_pairs[at])) for plane in planes]
+        return (line, swap(line, line_pairs[-1])), [(plane, swap(plane, plane_pairs[-1])) for plane in planes]
 
     def on_device(elec_pos, drop_vert, drop_conn, elec_rhs, drop_rhs, elec_inv, drop_inv):
         f32, bf16 = jnp.float32, jnp.bfloat16
@@ -296,51 +323,68 @@
             [VMEM] * 7,
             [((elec, half), bf16)] * 2 + [((rows, half), f32), ((rows, elec), f32)],
         )
-        parts = sums(line, add(keep, got, line))
-
-        two, both = run(
-            functools.partial(middle_kernel, couple), "elec_charges_to_drop_field", 0.8,
-            (*parts, elec_rhs, elec_inv, other_high, other_low),
-            [VMEM] * 8,
-            [((2, rows, half), f32), ((2 * rows, elec), bf16)],
-        )
-        two_got = swap(two, core_pairs)
-        keep, share = run(
-            functools.partial(own_kernel, couple), "fields_of_own_half", 1.5,
-            (core, both, drop_rhs, drop_inv, two, own_high, own_low),
-            [SMEM] + [VMEM] * 6,
-            [((rows, half), f32), ((rows, elec), f32)],
-        )
-        plane, = run(plane_kernel, "add", 0.1, (keep, two_got), [VMEM] * 2, [((rows, half), f32)])
+        part = rows // PARTS
+
+        def folded(left, right, *after):
+            return run(
+                fold_kernel, "add", 0.1, (left, right, *after), [VMEM] * 2 + [ANY] * len(after),
+                [((part, half), f32)] * PARTS,
+            )
+
+        line, planes = steps(line, folded(keep, got, line))
+
+        send, both = run(
+            functools.partial(to_drop_kernel, couple), "elec_charges_to_drop_field", 0.8,
+            (*line, elec_rhs, elec_inv, other_high, other_low),
+            [VMEM] * 6,
+            [((rows, half), f32), ((2 * rows, elec), bf16)],
+        )
+        got = swap(send, core_pairs)
+        field, = run(
+            join_kernel, "add", 0.1, [pair[at] for at in range(2) for pair in planes], [VMEM] * (2 * PARTS),
+            [((rows, half), f32)],
+        )
+        field_got = swap(field, core_pairs)
+        keep, = run(
+            functools.partial(keep_kernel, couple), "drop_field_of_own_half", 0.6,
+            (both, own_high, own_low), [VMEM] * 3, [((rows, half), f32)],
+        )
+        share, = run(
+            own_kernel, "elec_field_of_own_half", 1.0,
+            (core, drop_rhs, drop_inv, field, own_high, own_low),
+            [SMEM] + [VMEM] * 5,
+            [((rows, elec), f32)],
+        )
         line, = run(
             functools.partial(other_kernel, couple), "elec_field_of_other_half", 1.0,
-            (core, drop_rhs, drop_inv, two_got, share, other_high, other_low),
+            (core, drop_rhs, drop_inv, field_got, share, other_high, other_low),
             [SMEM] + [VMEM] * 6,
             [((rows, elec), f32)],
         )
-        parts = sums(line, plane)
-
-        line, plane = run(
-            add_pairs_kernel, "add_pairs", 0.1, parts, [VMEM] * 4, [((rows, elec), f32), ((rows, half), f32)]
-        )
-        plane_got = swap(plane, core_pairs)
-        outs = [((rows, elec), f32), ((rows, drop), f32)]
-        charge_elec, charge_drop = run(
-            charges_kernel, "charges_of_own_half", 1.3,
-            (core, elec_rhs, elec_inv, line, drop_rhs, drop_inv, plane),
-            [SMEM] + [VMEM] * 6,
-            outs,
-            [pltpu.VMEM((rows, elec), f32), pltpu.VMEM((rows, half), f32), pltpu.SemaphoreType.DMA((2,))],
-            out_spec=HBM,
-        )
-        charge_drop, = run(
-            rest_kernel, "charges_of_other_half", 1.0,
-            (core, drop_rhs, drop_inv, plane_got, charge_drop),
-            [SMEM] + [VMEM] * 3 + [HBM],
-            outs[1:],
-            [pltpu.VMEM((rows, half), f32), pltpu.SemaphoreType.DMA((2,))],
-            out_spec=HBM,
-            aliases={4: 0},
+        line, planes = steps(line, folded(keep, got))
+
+        def charges(is_other, at, fields):
+            return run(
+                functools.partial(charges_kernel, is_other, at), "drop_charges", 0.8,
+                (core, drop_rhs, drop_inv, *fields), [SMEM] + [VMEM] * (2 + len(fields)), [((part, half), f32)],
+            )[0]
+
+        mine, theirs = [], []
+        for at, (plane, plane_got) in enumerate(planes):
+            after = [charges(0, 0, mine[0])] if at else []
+            mine.append(
+                run(
+                    fold_kernel, "add", 0.1, (plane, plane_got, *after), [VMEM] * 2 + [ANY] * len(after),
+                    [((part // 2, half), f32)] * 2,
+                )
+            )
+            theirs.append([swap(value, core_pairs) for value in mine[at]])
+            done = after
+        done += [charges(0, 1, mine[1]), charges(1, 0, theirs[0])]
+        charge_drop, token = run_last(core, drop_rhs, drop_inv, done, theirs[1])
+        charge_elec, = run(
+            elec_kernel, "elec_charges", 1.0, (elec_rhs, elec_inv, *line, token), [VMEM] * 4 + [ANY],
+            [((rows, elec), f32)],
         )
         return (charge_elec, charge_drop)
 

time: 57.7 us -> 54.9 us (0.951)
  waiting for transfers between devices: 29.1 us -> 18.5 us
  starting transfers between devices: 14.6 us -> 21.5 us
  Pallas kernels: 13 us -> 14 us
    ppermute x11 -> x19, waiting for transfers between devices: 29.1 us -> 18.5 us  [swap(): return lax.ppermute(value, ('elec', 'drop'), pairs)]
    ppermute x11 -> x19, starting transfers between devices: 14.6 us -> 21.5 us  [swap(): return lax.ppermute(value, ('elec', 'drop'), pairs)]
    pallas_call x0 -> x1, Pallas kernels: none -> 1.19 us  [run_last(): pl.pallas_call(last_kernel, out_shape=[jax.ShapeDtypeStruct(drop_rhs.shap...]
    pallas_call x14 -> x21, Pallas kernels: 13 us -> 12.8 us  [run(): pl.pallas_call(kernel, out_shape=[jax.ShapeDtypeStruct(shape, dtype) for...]
  transfers between devices with their start and end apart: 11 -> 19, of which waited for: 7 -> 8; matrix products, arithmetic and copies ran while one was open for 0% -> 0% of each run, Pallas kernels for 12% -> 16%
where the time goes in v4:
time: 54.9 us; the launch traced here: 54.8 us
  starting transfers between devices  21.5 us (39%)
  waiting for transfers between devices  18.5 us (34%)
  Pallas kernels  14 us (26%)
  between operations  0.84 us (2%)
    ppermute x19, starting transfers between devices, swap(): return lax.ppermute(value, ('elec', 'drop'), pairs)  21.5 us
    ppermute x19, waiting for transfers between devices, swap(): return lax.ppermute(value, ('elec', 'drop'), pairs)  18.5 us
    pallas_call x21, Pallas kernels, run(): pl.pallas_call(kernel, out_shape=[jax.ShapeDtypeStruct(shape, dtype) for...  12.8 us
    pallas_call x1, Pallas kernels, run_last(): pl.pallas_call(last_kernel, out_shape=[jax.ShapeDtypeStruct(drop_rhs.shap...  1.19 us
  transfers between devices with their start and end apart: 19, of which 8 were waited for; matrix products, arithmetic and copies ran while one was open for 0% of the time, Pallas kernels for 16%

profile of v4, /device:TPU:0, one launch (start us, length us, event | category | flops | bytes accessed | tf_op | source)
XLA Modules:
  0.0 54.8 jit_solution(5688085982493699079)
XLA Ops:
  0.6 4.1 %coupling_other_half.1 = (bf16[512,1024]{1,0:T(8,128)(2,1)S(1)}, bf16[512,1024]{1,0:T(8,128)(2,1)S(1)}, f32[128,1024]{1,0:T(8,128)S(1)}, f32[3,512,128]{2,1,0:T(...) custom-call(s32[1]{0:T(128)} %bitcast.core_ref, ...), custom_call_target="tpu_custom_call" | custom-call | bytes 13200000 | tf_op jit(solution)/shard_map/coupling_other_half/pallas_call | solution.py:228
  4.7 0.5 collective-permute-start
  5.2 2.4 %coupling_own_half.1 = (bf16[512,1024]{1,0:T(8,128)(2,1)S(1)}, bf16[512,1024]{1,0:T(8,128)(2,1)S(1)}, f32[128,1024]{1,0:T(8,128)S(1)}, f32[128,512]{1,0:T(8,128)S(1)}) custom-call(f32[3,512,128]{2,1,0:T(8,128)S(1)} %get-tuple-element.34.wide_ref, f32[8,1024]{1,0:T(8,128)S(1)} %get-tuple-element.35.centre_ref, ...), custom_call_target="tpu_custom_call" | custom-call | bytes 6600000 | tf_op jit(solution)/shard_map/coupling_own_half/pallas_call | solution.py:228
  7.7 2.6 %collective-permute-start.8 = (f32[128,512]{1,0:T(8,128)S(1)}, f32[128,512]{1,0:T(8,128)S(1)}, u32[]{:S(2)}, u32[]{:S(2)}) collective-permute-start(f32[128,512]{1,0:T(8,128)S(1)} %get-tuple-element.43.refs_0_.a_ref), channel_id=1, source_target_pairs={{0,1},{1,0},{2,3},{3,2},{4,6},{5,7},{6,4},{7,5},{8,9},{9,8},{10,11... | collective-permute-start | bytes 786440 | tf_op jit(solution)/shard_map/ppermute | solution.py:289
  10.3 0.0 collective-permute-done.b_ref
  10.3 0.1 add.16
  10.4 1.6 %collective-permute-start.1 = (f32[64,1024]{1,0:T(8,128)S(1)}, f32[64,1024]{1,0:T(8,128)S(1)}, u32[]{:S(2)}, u32[]{:S(2)}) collective-permute-start(f32[64,1024]{1,0:T(8,128)S(1)} %get-tuple-element.44.a_ref), channel_id=1, source_target_pairs={{0,8},{1,9},{2,10},{3,11},{4,20},{5,21},{6,22},{7,23},{8,0},{9,1},... | collective-permute-start | bytes 786440 | tf_op jit(solution)/shard_map/ppermute | solution.py:289
  11.9 0.5 collective-permute-start.2
  12.5 4.6 %collective-permute-done.8.b_ref = f32[128,512]{1,0:T(8,128)S(1)} collective-permute-done((f32[128,512]{1,0:T(8,128)S(1)}, f32[128,512]{1,0:T(8,128)S(1)}, u32[]{:S(2)}, u32[]{:S(2)}) %collective-permute-start.8) | collective-permute-done | bytes 262176 | tf_op jit(solution)/shard_map/ppermute | solution.py:289
  17.1 2.9 %collective-permute-start.9 = (f32[128,512]{1,0:T(8,128)S(1)}, f32[128,512]{1,0:T(8,128)S(1)}, u32[]{:S(2)}, u32[]{:S(2)}) collective-permute-start(f32[128,512]{1,0:T(8,128)S(1)} %add.21.left_ref), channel_id=1, source_target_pairs={{0,2},{1,3},{2,0},{3,1},{4,5},{5,4},{6,7},{7,6},{8,10},{9,11},{10,... | collective-permute-start | bytes 786440 | tf_op jit(solution)/shard_map/ppermute | solution.py:289
  20.0 0.0 collective-permute-done.1.b_ref
  20.0 1.6 %collective-permute-start.3 = (f32[64,1024]{1,0:T(8,128)S(1)}, f32[64,1024]{1,0:T(8,128)S(1)}, u32[]{:S(2)}, u32[]{:S(2)}) collective-permute-start(f32[64,1024]{1,0:T(8,128)S(1)} %add.17.refs_0_), channel_id=1, source_target_pairs={{0,16},{1,17},{2,18},{3,19},{4,12},{5,13},{6,14},{7,15},{8,24},{9,... | collective-permute-start | bytes 786440 | tf_op jit(solution)/shard_map/ppermute | solution.py:289
  21.6 0.0 collective-permute-done.2.b_ref
  21.7 0.6 %collective-permute-start.4 = (f32[64,1024]{1,0:T(8,128)S(1)}, f32[64,1024]{1,0:T(8,128)S(1)}, u32[]{:S(2)}, u32[]{:S(2)}) collective-permute-start(f32[64,1024]{1,0:T(8,128)S(1)} %add.18.refs_1_), channel_id=1, source_target_pairs={{0,16},{1,17},{2,18},{3,19},{4,12},{5,13},{6,14},{7,15},{8,24},{9,... | collective-permute-start | bytes 786440 | tf_op jit(solution)/shard_map/ppermute | solution.py:289
  22.2 3.8 %collective-permute-done.9.right_ref = f32[128,512]{1,0:T(8,128)S(1)} collective-permute-done((f32[128,512]{1,0:T(8,128)S(1)}, f32[128,512]{1,0:T(8,128)S(1)}, u32[]{:S(2)}, u32[]{:S(2)}) %collective-permute-start.9) | collective-permute-done | bytes 262176 | tf_op jit(solution)/shard_map/ppermute | solution.py:289
  26.1 0.8 %elec_charges_to_drop_field.1 = (f32[128,1024]{1,0:T(8,128)S(1)}, bf16[256,512]{1,0:T(8,128)(2,1)S(1)}) custom-call(f32[128,512]{1,0:T(8,128)S(1)} %add.21.left_ref, f32[128,512]{1,0:T(8,128)S(1)} %collective-permute-done.9.right_ref, f32[128,512]{1,0:T(8,128)S(1)} %get-tuple-element.30.rhs_ref, f32[4,128,128]{2,1,0:T(8,128)S(1)} %get-tuple-element.31.inv_ref, ...), custom_call_target="tpu_custom_call" | custom-call | bytes 2640000 | tf_op jit(solution)/shard_map/elec_charges_to_drop_field/pallas_call | solution.py:228
  26.9 0.1 collective-permute-start.10
  26.9 0.0 collective-permute-done.3.refs_2_
  26.9 2.3 %collective-permute-done.4.refs_3_ = f32[64,1024]{1,0:T(8,128)S(1)} collective-permute-done((f32[64,1024]{1,0:T(8,128)S(1)}, f32[64,1024]{1,0:T(8,128)S(1)}, u32[]{:S(2)}, u32[]{:S(2)}) %collective-permute-start.4) | collective-permute-done | bytes 262176 | tf_op jit(solution)/shard_map/ppermute | solution.py:289
  29.3 0.1 add.19.field_ref
  29.3 0.1 collective-permute-start.5
  29.4 0.6 %drop_field_of_own_half.1.a_ref = f32[128,1024]{1,0:T(8,128)S(1)} custom-call(bf16[256,512]{1,0:T(8,128)(2,1)S(1)} %get-tuple-element.48.both_ref, bf16[512,1024]{1,0:T(8,128)(2,1)S(1)} %get-tuple-element.46.high_ref, bf16[512,1024]{1,0:T(8,128)(2,1)S(1)} %get-tuple-element.47.low_ref), custom_call_target="tpu_custom_call" | custom-call | bytes 1980000 | tf_op jit(solution)/shard_map/drop_field_of_own_half/pallas_call | solution.py:228
  30.0 0.0 collective-permute-done.10.b_ref
  30.0 0.1 add.22
  30.1 1.8 %collective-permute-start.11 = (f32[64,1024]{1,0:T(8,128)S(1)}, f32[64,1024]{1,0:T(8,128)S(1)}, u32[]{:S(2)}, u32[]{:S(2)}) collective-permute-start(f32[64,1024]{1,0:T(8,128)S(1)} %get-tuple-element.50.a_ref), channel_id=1, source_target_pairs={{0,8},{1,9},{2,10},{3,11},{4,20},{5,21},{6,22},{7,23},{8,0},{9,1},... | collective-permute-start | bytes 786440 | tf_op jit(solution)/shard_map/ppermute | solution.py:289
  31.9 0.3 collective-permute-start.13
  32.2 1.1 %elec_field_of_own_half.1.share_ref = f32[128,512]{1,0:T(8,128)S(1)} custom-call(s32[1]{0:T(128)} %bitcast.core_ref, f32[128,2048]{1,0:T(8,128)S(1)} %get-tuple-element.32.rhs_ref, f32[16,128,128]{2,1,0:T(8,128)S(1)} %get-tuple-element.33.inv_ref, f32[128,1024]{1,0:T(8,128)S(1)} %add.19.field_ref, bf16[512,1024]{1,0:T(8,128)(2,1)S(1)} %get-tuple-element.46.high_ref, ...), custom_call_target="tpu_custom_call" | custom-call | bytes 3300000 | tf_op jit(solution)/shard_map/elec_field_of_own_half/pallas_call | solution.py:228
  33.3 0.0 collective-permute-done.5.field_ref
  33.3 1.1 %elec_field_of_other_half.1.a_ref = f32[128,512]{1,0:T(8,128)S(1)} custom-call(s32[1]{0:T(128)} %bitcast.core_ref, f32[128,2048]{1,0:T(8,128)S(1)} %get-tuple-element.32.rhs_ref, f32[16,128,128]{2,1,0:T(8,128)S(1)} %get-tuple-element.33.inv_ref, f32[128,1024]{1,0:T(8,128)S(1)} %collective-permute-done.5.field_ref, ...), custom_call_target="tpu_custom_call" | custom-call | bytes 3300000 | tf_op jit(solution)/shard_map/elec_field_of_other_half/pallas_call | solution.py:228
  34.5 1.8 %collective-permute-start.6 = (f32[128,512]{1,0:T(8,128)S(1)}, f32[128,512]{1,0:T(8,128)S(1)}, u32[]{:S(2)}, u32[]{:S(2)}) collective-permute-start(f32[128,512]{1,0:T(8,128)S(1)} %elec_field_of_other_half.1.a_ref), channel_id=1, source_target_pairs={{0,1},{1,0},{2,3},{3,2},{4,6},{5,7},{6,4},{7,5},{8,9},{9,8},{10,11... | collective-permute-start | bytes 786440 | tf_op jit(solution)/shard_map/ppermute | solution.py:289
  36.3 0.3 collective-permute-done.11.b_ref
  36.6 1.9 %collective-permute-start.12 = (f32[64,1024]{1,0:T(8,128)S(1)}, f32[64,1024]{1,0:T(8,128)S(1)}, u32[]{:S(2)}, u32[]{:S(2)}) collective-permute-start(f32[64,1024]{1,0:T(8,128)S(1)} %add.23.a_ref), channel_id=1, source_target_pairs={{0,16},{1,17},{2,18},{3,19},{4,12},{5,13},{6,14},{7,15},{8,24},{9,... | collective-permute-start | bytes 786440 | tf_op jit(solution)/shard_map/ppermute | solution.py:289
  38.5 1.3 %collective-permute-done.13.b_ref = f32[64,1024]{1,0:T(8,128)S(1)} collective-permute-done((f32[64,1024]{1,0:T(8,128)S(1)}, f32[64,1024]{1,0:T(8,128)S(1)}, u32[]{:S(2)}, u32[]{:S(2)}) %collective-permute-start.13) | collective-permute-done | bytes 262176 | tf_op jit(solution)/shard_map/ppermute | solution.py:289
  39.8 2.2 %collective-permute-start.14 = (f32[64,1024]{1,0:T(8,128)S(1)}, f32[64,1024]{1,0:T(8,128)S(1)}, u32[]{:S(2)}, u32[]{:S(2)}) collective-permute-start(f32[64,1024]{1,0:T(8,128)S(1)} %add.25.a_ref), channel_id=1, source_target_pairs={{0,16},{1,17},{2,18},{3,19},{4,12},{5,13},{6,14},{7,15},{8,24},{9,... | collective-permute-start | bytes 786440 | tf_op jit(solution)/shard_map/ppermute | solution.py:289
  42.0 1.6 %collective-permute-done.6.b_ref = f32[128,512]{1,0:T(8,128)S(1)} collective-permute-done((f32[128,512]{1,0:T(8,128)S(1)}, f32[128,512]{1,0:T(8,128)S(1)}, u32[]{:S(2)}, u32[]{:S(2)}) %collective-permute-start.6) | collective-permute-done | bytes 262176 | tf_op jit(solution)/shard_map/ppermute | solution.py:289
  43.6 2.0 %collective-permute-start.7 = (f32[128,512]{1,0:T(8,128)S(1)}, f32[128,512]{1,0:T(8,128)S(1)}, u32[]{:S(2)}, u32[]{:S(2)}) collective-permute-start(f32[128,512]{1,0:T(8,128)S(1)} %add.20.left_ref), channel_id=1, source_target_pairs={{0,2},{1,3},{2,0},{3,1},{4,5},{5,4},{6,7},{7,6},{8,10},{9,11},{10,... | collective-permute-start | bytes 786440 | tf_op jit(solution)/shard_map/ppermute | solution.py:289
  45.6 0.0 collective-permute-done.12.b_ref
  45.7 0.1 collective-permute-start.15
  45.7 0.5 collective-permute-start.16
  46.2 0.4 drop_charges.3.refs_0_.own_first_ref
  46.7 0.0 collective-permute-done.14.b_ref
  46.7 0.1 collective-permute-start.17
  46.9 0.4 collective-permute-start.18
  47.3 0.4 drop_charges.4.own_last_ref
  47.7 0.0 collective-permute-done.15.refs_0_
  47.7 0.0 collective-permute-done.16.refs_1_
  47.8 0.4 drop_charges.5.other_first_ref
  48.2 0.0 collective-permute-done.17.left_ref
  48.2 0.1 collective-permute-done.18.right_ref
  48.3 1.2 %last_drop_charges.1 = (f32[128,2048]{1,0:T(8,128)}, f32[8,128]{1,0:T(8,128)S(1)}) custom-call(s32[1]{0:T(128)} %bitcast.core_ref, f32[128,2048]{1,0:T(8,128)S(1)} %get-tuple-element.32.rhs_ref, f32[16,128,128]{2,1,0:T(8,128)S(1)} %get-tuple-element.33.inv_ref, f32[64,1024]{1,0:T(8,128)S(1)} %drop_charges.3.refs_0_.own_first_ref, ...), custom_call_target="tpu_custom_call" | custom-call | tf_op jit(solution)/shard_map/last_drop_charges/pallas_call | solution.py:249
  49.5 4.3 %collective-permute-done.7.right_ref = f32[128,512]{1,0:T(8,128)S(1)} collective-permute-done((f32[128,512]{1,0:T(8,128)S(1)}, f32[128,512]{1,0:T(8,128)S(1)}, u32[]{:S(2)}, u32[]{:S(2)}) %collective-permute-start.7) | collective-permute-done | bytes 262176 | tf_op jit(solution)/shard_map/ppermute | solution.py:289
  53.8 1.0 %elec_charges.1 = f32[128,512]{1,0:T(8,128)} custom-call(f32[128,512]{1,0:T(8,128)S(1)} %get-tuple-element.30.rhs_ref, f32[4,128,128]{2,1,0:T(8,128)S(1)} %get-tuple-element.31.inv_ref, f32[128,512]{1,0:T(8,128)S(1)} %add.20.left_ref, f32[128,512]{1,0:T(8,128)S(1)} %collective-permute-done.7.right_ref, f32[8,128]{1,0:T(8,128)S(1)} %get-tuple-element.56.after), custom_call_target="tpu_custom_call" | custom-call | bytes 3300000 | tf_op jit(solution)/shard_map/elec_charges/pallas_call | solution.py:228
  (8 shorter events, 0.2 us)
Async XLA Ops:
  4.7 5.6 %collective-permute-start = (f32[128,1024]{1,0:T(8,128)S(1)}, f32[128,1024]{1,0:T(8,128)S(1)}, u32[]{:S(2)}, u32[]{:S(2)}) collective-permute-start(f32[128,1024]{1,0:T(8,128)S(1)} %get-tuple-element.42), channel_id=1, source_target_pairs={{0,4},{1,5},{2,6},{3,7},{4,0},{5,1},{6,2},{7,3},{8,12},{9,13},{10,... | collective-permute-start | bytes 1572872 | tf_op jit(solution)/shard_map/ppermute | solution.py:289
  7.7 9.4 %collective-permute-start.8 = (f32[128,512]{1,0:T(8,128)S(1)}, f32[128,512]{1,0:T(8,128)S(1)}, u32[]{:S(2)}, u32[]{:S(2)}) collective-permute-start(f32[128,512]{1,0:T(8,128)S(1)} %get-tuple-element.43.refs_0_.a_ref), channel_id=1, source_target_pairs={{0,1},{1,0},{2,3},{3,2},{4,6},{5,7},{6,4},{7,5},{8,9},{9,8},{10,11... | collective-permute-start | bytes 786440 | tf_op jit(solution)/shard_map/ppermute | solution.py:289
  10.4 9.6 %collective-permute-start.1 = (f32[64,1024]{1,0:T(8,128)S(1)}, f32[64,1024]{1,0:T(8,128)S(1)}, u32[]{:S(2)}, u32[]{:S(2)}) collective-permute-start(f32[64,1024]{1,0:T(8,128)S(1)} %get-tuple-element.44.a_ref), channel_id=1, source_target_pairs={{0,8},{1,9},{2,10},{3,11},{4,20},{5,21},{6,22},{7,23},{8,0},{9,1},... | collective-permute-start | bytes 786440 | tf_op jit(solution)/shard_map/ppermute | solution.py:289
  11.9 9.7 %collective-permute-start.2 = (f32[64,1024]{1,0:T(8,128)S(1)}, f32[64,1024]{1,0:T(8,128)S(1)}, u32[]{:S(2)}, u32[]{:S(2)}) collective-permute-start(f32[64,1024]{1,0:T(8,128)S(1)} %get-tuple-element.45.a_ref), channel_id=1, source_target_pairs={{0,8},{1,9},{2,10},{3,11},{4,20},{5,21},{6,22},{7,23},{8,0},{9,1},... | collective-permute-start | bytes 786440 | tf_op jit(solution)/shard_map/ppermute | solution.py:289
  17.1 9.0 %collective-permute-start.9 = (f32[128,512]{1,0:T(8,128)S(1)}, f32[128,512]{1,0:T(8,128)S(1)}, u32[]{:S(2)}, u32[]{:S(2)}) collective-permute-start(f32[128,512]{1,0:T(8,128)S(1)} %add.21.left_ref), channel_id=1, source_target_pairs={{0,2},{1,3},{2,0},{3,1},{4,5},{5,4},{6,7},{7,6},{8,10},{9,11},{10,... | collective-permute-start | bytes 786440 | tf_op jit(solution)/shard_map/ppermute | solution.py:289
  20.0 6.9 %collective-permute-start.3 = (f32[64,1024]{1,0:T(8,128)S(1)}, f32[64,1024]{1,0:T(8,128)S(1)}, u32[]{:S(2)}, u32[]{:S(2)}) collective-permute-start(f32[64,1024]{1,0:T(8,128)S(1)} %add.17.refs_0_), channel_id=1, source_target_pairs={{0,16},{1,17},{2,18},{3,19},{4,12},{5,13},{6,14},{7,15},{8,24},{9,... | collective-permute-start | bytes 786440 | tf_op jit(solution)/shard_map/ppermute | solution.py:289
  21.7 7.6 %collective-permute-start.4 = (f32[64,1024]{1,0:T(8,128)S(1)}, f32[64,1024]{1,0:T(8,128)S(1)}, u32[]{:S(2)}, u32[]{:S(2)}) collective-permute-start(f32[64,1024]{1,0:T(8,128)S(1)} %add.18.refs_1_), channel_id=1, source_target_pairs={{0,16},{1,17},{2,18},{3,19},{4,12},{5,13},{6,14},{7,15},{8,24},{9,... | collective-permute-start | bytes 786440 | tf_op jit(solution)/shard_map/ppermute | solution.py:289
  26.9 3.2 %collective-permute-start.10 = (f32[128,1024]{1,0:T(8,128)S(1)}, f32[128,1024]{1,0:T(8,128)S(1)}, u32[]{:S(2)}, u32[]{:S(2)}) collective-permute-start(f32[128,1024]{1,0:T(8,128)S(1)} %get-tuple-element.49), channel_id=1, source_target_pairs={{0,4},{1,5},{2,6},{3,7},{4,0},{5,1},{6,2},{7,3},{8,12},{9,13},{10,... | collective-permute-start | bytes 1572872 | tf_op jit(solution)/shard_map/ppermute | solution.py:289
  29.3 4.0 %collective-permute-start.5 = (f32[128,1024]{1,0:T(8,128)S(1)}, f32[128,1024]{1,0:T(8,128)S(1)}, u32[]{:S(2)}, u32[]{:S(2)}) collective-permute-start(f32[128,1024]{1,0:T(8,128)S(1)} %add.19.field_ref), channel_id=1, source_target_pairs={{0,4},{1,5},{2,6},{3,7},{4,0},{5,1},{6,2},{7,3},{8,12},{9,13},{10,... | collective-permute-start | bytes 1572872 | tf_op jit(solution)/shard_map/ppermute | solution.py:289
  30.1 6.4 %collective-permute-start.11 = (f32[64,1024]{1,0:T(8,128)S(1)}, f32[64,1024]{1,0:T(8,128)S(1)}, u32[]{:S(2)}, u32[]{:S(2)}) collective-permute-start(f32[64,1024]{1,0:T(8,128)S(1)} %get-tuple-element.50.a_ref), channel_id=1, source_target_pairs={{0,8},{1,9},{2,10},{3,11},{4,20},{5,21},{6,22},{7,23},{8,0},{9,1},... | collective-permute-start | bytes 786440 | tf_op jit(solution)/shard_map/ppermute | solution.py:289
  31.9 7.8 %collective-permute-start.13 = (f32[64,1024]{1,0:T(8,128)S(1)}, f32[64,1024]{1,0:T(8,128)S(1)}, u32[]{:S(2)}, u32[]{:S(2)}) collective-permute-start(f32[64,1024]{1,0:T(8,128)S(1)} %get-tuple-element.53.a_ref), channel_id=1, source_target_pairs={{0,8},{1,9},{2,10},{3,11},{4,20},{5,21},{6,22},{7,23},{8,0},{9,1},... | collective-permute-start | bytes 786440 | tf_op jit(solution)/shard_map/ppermute | solution.py:289
  34.5 9.1 %collective-permute-start.6 = (f32[128,512]{1,0:T(8,128)S(1)}, f32[128,512]{1,0:T(8,128)S(1)}, u32[]{:S(2)}, u32[]{:S(2)}) collective-permute-start(f32[128,512]{1,0:T(8,128)S(1)} %elec_field_of_other_half.1.a_ref), channel_id=1, source_target_pairs={{0,1},{1,0},{2,3},{3,2},{4,6},{5,7},{6,4},{7,5},{8,9},{9,8},{10,11... | collective-permute-start | bytes 786440 | tf_op jit(solution)/shard_map/ppermute | solution.py:289
  36.6 9.0 %collective-permute-start.12 = (f32[64,1024]{1,0:T(8,128)S(1)}, f32[64,1024]{1,0:T(8,128)S(1)}, u32[]{:S(2)}, u32[]{:S(2)}) collective-permute-start(f32[64,1024]{1,0:T(8,128)S(1)} %add.23.a_ref), channel_id=1, source_target_pairs={{0,16},{1,17},{2,18},{3,19},{4,12},{5,13},{6,14},{7,15},{8,24},{9,... | collective-permute-start | bytes 786440 | tf_op jit(solution)/shard_map/ppermute | solution.py:289
  39.8 6.9 %collective-permute-start.14 = (f32[64,1024]{1,0:T(8,128)S(1)}, f32[64,1024]{1,0:T(8,128)S(1)}, u32[]{:S(2)}, u32[]{:S(2)}) collective-permute-start(f32[64,1024]{1,0:T(8,128)S(1)} %add.25.a_ref), channel_id=1, source_target_pairs={{0,16},{1,17},{2,18},{3,19},{4,12},{5,13},{6,14},{7,15},{8,24},{9,... | collective-permute-start | bytes 786440 | tf_op jit(solution)/shard_map/ppermute | solution.py:289
  43.6 10.1 %collective-permute-start.7 = (f32[128,512]{1,0:T(8,128)S(1)}, f32[128,512]{1,0:T(8,128)S(1)}, u32[]{:S(2)}, u32[]{:S(2)}) collective-permute-start(f32[128,512]{1,0:T(8,128)S(1)} %add.20.left_ref), channel_id=1, source_target_pairs={{0,2},{1,3},{2,0},{3,1},{4,5},{5,4},{6,7},{7,6},{8,10},{9,11},{10,... | collective-permute-start | bytes 786440 | tf_op jit(solution)/shard_map/ppermute | solution.py:289
  45.7 2.1 %collective-permute-start.15 = (f32[32,1024]{1,0:T(8,128)S(1)}, f32[32,1024]{1,0:T(8,128)S(1)}, u32[]{:S(2)}, u32[]{:S(2)}) collective-permute-start(f32[32,1024]{1,0:T(8,128)S(1)} %get-tuple-element.51.refs_0_), channel_id=1, source_target_pairs={{0,4},{1,5},{2,6},{3,7},{4,0},{5,1},{6,2},{7,3},{8,12},{9,13},{10,... | collective-permute-start | bytes 393224 | tf_op jit(solution)/shard_map/ppermute | solution.py:289
  45.7 2.0 %collective-permute-start.16 = (f32[32,1024]{1,0:T(8,128)S(1)}, f32[32,1024]{1,0:T(8,128)S(1)}, u32[]{:S(2)}, u32[]{:S(2)}) collective-permute-start(f32[32,1024]{1,0:T(8,128)S(1)} %get-tuple-element.52.refs_1_), channel_id=1, source_target_pairs={{0,4},{1,5},{2,6},{3,7},{4,0},{5,1},{6,2},{7,3},{8,12},{9,13},{10,... | collective-permute-start | bytes 393224 | tf_op jit(solution)/shard_map/ppermute | solution.py:289
  46.7 1.5 %collective-permute-start.17 = (f32[32,1024]{1,0:T(8,128)S(1)}, f32[32,1024]{1,0:T(8,128)S(1)}, u32[]{:S(2)}, u32[]{:S(2)}) collective-permute-start(f32[32,1024]{1,0:T(8,128)S(1)} %get-tuple-element.54.refs_0_), channel_id=1, source_target_pairs={{0,4},{1,5},{2,6},{3,7},{4,0},{5,1},{6,2},{7,3},{8,12},{9,13},{10,... | collective-permute-start | bytes 393224 | tf_op jit(solution)/shard_map/ppermute | solution.py:289
  46.9 1.5 %collective-permute-start.18 = (f32[32,1024]{1,0:T(8,128)S(1)}, f32[32,1024]{1,0:T(8,128)S(1)}, u32[]{:S(2)}, u32[]{:S(2)}) collective-permute-start(f32[32,1024]{1,0:T(8,128)S(1)} %get-tuple-element.55.refs_1_), channel_id=1, source_target_pairs={{0,4},{1,5},{2,6},{3,7},{4,0},{5,1},{6,2},{7,3},{8,12},{9,13},{10,... | collective-permute-start | bytes 393224 | tf_op jit(solution)/shard_map/ppermute | solution.py:289

commit v5 on v4

--- a/solution.py
+++ b/solution.py
@@ -220,8 +220,15 @@
         copy.wait()
 
 
-def elec_kernel(rhs_ref, inv_ref, left_ref, right_ref, after, out_ref):
-    out_ref[...] = solve(inv_ref, rhs_ref[...] - (left_ref[...] + right_ref[...]))
+def elec_kernel(rhs_ref, inv_ref, left_ref, right_ref, after, out_hbm, charge, sems):
+    copies = []
+    for at in range(inv_ref.shape[0]):
+        cols = slice(at * LANES, (at + 1) * LANES)
+        charge[:, cols] = solve_block(inv_ref[at], rhs_ref[:, cols] - (left_ref[:, cols] + right_ref[:, cols]))
+        copies.append(pltpu.make_async_copy(charge.at[:, cols], out_hbm.at[:, cols], sems.at[at]))
+        copies[-1].start()
+    for copy in copies:
+        copy.wait()
 
 
 def run(kernel, name, micros, operands, specs, outs, scratch=(), out_spec=VMEM, aliases=()):
@@ -257,7 +264,7 @@
     )(core, drop_rhs, drop_inv, *done, *fields)
 
 
-def exchanges(elec_devices, drop_devices):
+def exchanges(elec_devices, drop_devices, far_core):
     def pairs(partner):
         out = []
         for elec in range(elec_devices):
@@ -276,19 +283,20 @@
         pairs(lambda e, d, s=s: (e ^ (1 << ordered(chip_bits, s, e & 1)), d)) for s in range(len(chip_bits))
     ]
     line = [
-        pairs(lambda e, d, s=s: (e, d ^ (1 << ordered(drop_bits, s, e & 1)))) for s in range(len(drop_bits))
+        pairs(lambda e, d, s=s: (e, d ^ (1 << ordered(drop_bits, s, far_core ^ 1 ^ (e & 1))))) for s in range(len(drop_bits))
     ]
-    return core, plane, line
+    return core, line, plane
 
 
 def solution(mesh):
     elec_devices, drop_devices = mesh.shape["elec"], mesh.shape["drop"]
-    core_pairs, plane_pairs, line_pairs = exchanges(elec_devices, drop_devices)
+    core_pairs, *first_pairs = exchanges(elec_devices, drop_devices, 0)
+    _, *second_pairs = exchanges(elec_devices, drop_devices, 1)
 
     def swap(value, pairs):
         return lax.ppermute(value, ("elec", "drop"), pairs)
 
-    def steps(line, planes):
+    def steps(line, planes, line_pairs, plane_pairs):
         for at in range(max(len(line_pairs), len(plane_pairs)) - 1):
             if at < len(line_pairs) - 1:
                 line = add(line, swap(line, line_pairs[at]))
@@ -331,7 +339,7 @@
                 [((part, half), f32)] * PARTS,
             )
 
-        line, planes = steps(line, folded(keep, got, line))
+        line, planes = steps(line, folded(keep, got, line), *first_pairs)
 
         send, both = run(
             functools.partial(to_drop_kernel, couple), "elec_charges_to_drop_field", 0.8,
@@ -340,15 +348,16 @@
             [((rows, half), f32), ((2 * rows, elec), bf16)],
         )
         got = swap(send, core_pairs)
-        field, = run(
-            join_kernel, "add", 0.1, [pair[at] for at in range(2) for pair in planes], [VMEM] * (2 * PARTS),
-            [((rows, half), f32)],
-        )
-        field_got = swap(field, core_pairs)
         keep, = run(
             functools.partial(keep_kernel, couple), "drop_field_of_own_half", 0.6,
             (both, own_high, own_low), [VMEM] * 3, [((rows, half), f32)],
         )
+        field, = run(
+            join_kernel, "add", 0.1, [pair[at] for at in range(2) for pair in planes] + [keep],
+            [VMEM] * (2 * PARTS) + [ANY],
+            [((rows, half), f32)],
+        )
+        field_got = swap(field, core_pairs)
         share, = run(
             own_kernel, "elec_field_of_own_half", 1.0,
             (core, drop_rhs, drop_inv, field, own_high, own_low),
@@ -361,7 +370,7 @@
             [SMEM] + [VMEM] * 6,
             [((rows, elec), f32)],
         )
-        line, planes = steps(line, folded(keep, got))
+        line, planes = steps(line, folded(keep, got), *second_pairs)
 
         def charges(is_other, at, fields):
             return run(
@@ -385,6 +394,8 @@
         charge_elec, = run(
             elec_kernel, "elec_charges", 1.0, (elec_rhs, elec_inv, *line, token), [VMEM] * 4 + [ANY],
             [((rows, elec), f32)],
+            [pltpu.VMEM((rows, elec), f32), pltpu.SemaphoreType.DMA((elec_inv.shape[0],))],
+            out_spec=HBM,
         )
         return (charge_elec, charge_drop)
 

time: 54.9 us -> 52 us (0.947); the launches traced: 54.8 us -> 51.1 us
  waiting for transfers between devices: 18.5 us -> 15 us
    ppermute x19, waiting for transfers between devices: 18.5 us -> 15 us  [swap(): return lax.ppermute(value, ('elec', 'drop'), pairs)]
  transfers between devices with their start and end apart: 19 -> 19, of which waited for: 8 -> 10; matrix products, arithmetic and copies ran while one was open for 0% -> 0% of each run, Pallas kernels for 16% -> 17%
where the time goes in v5:
time: 52 us; the launch traced here: 51.1 us
  starting transfers between devices  21.3 us (41%)
  waiting for transfers between devices  15 us (29%)
  Pallas kernels  14 us (27%)
  between operations  0.83 us (2%)
    ppermute x19, starting transfers between devices, swap(): return lax.ppermute(value, ('elec', 'drop'), pairs)  21.3 us
    ppermute x19, waiting for transfers between devices, swap(): return lax.ppermute(value, ('elec', 'drop'), pairs)  15 us
    pallas_call x21, Pallas kernels, run(): pl.pallas_call(kernel, out_shape=[jax.ShapeDtypeStruct(shape, dtype) for...  12.8 us
    pallas_call x1, Pallas kernels, run_last(): pl.pallas_call(last_kernel, out_shape=[jax.ShapeDtypeStruct(drop_rhs.shap...  1.19 us
  transfers between devices with their start and end apart: 19, of which 10 were waited for; matrix products, arithmetic and copies ran while one was open for 0% of the time, Pallas kernels for 17%

profile of v5, /device:TPU:0, one launch (start us, length us, event | category | flops | bytes accessed | tf_op | source)
XLA Modules:
  0.0 51.1 jit_solution(1699781558304791811)
XLA Ops:
  0.6 4.1 %coupling_other_half.1 = (bf16[512,1024]{1,0:T(8,128)(2,1)S(1)}, bf16[512,1024]{1,0:T(8,128)(2,1)S(1)}, f32[128,1024]{1,0:T(8,128)S(1)}, f32[3,512,128]{2,1,0:T(...) custom-call(s32[1]{0:T(128)} %bitcast.core_ref, ...), custom_call_target="tpu_custom_call" | custom-call | bytes 13200000 | tf_op jit(solution)/shard_map/coupling_other_half/pallas_call | solution.py:235
  4.7 0.5 %collective-permute-start = (f32[128,1024]{1,0:T(8,128)S(1)}, f32[128,1024]{1,0:T(8,128)S(1)}, u32[]{:S(2)}, u32[]{:S(2)}) collective-permute-start(f32[128,1024]{1,0:T(8,128)S(1)} %get-tuple-element.42), channel_id=1, source_target_pairs={{0,4},{1,5},{2,6},{3,7},{4,0},{5,1},{6,2},{7,3},{8,12},{9,13},{10,... | collective-permute-start | bytes 1572872 | tf_op jit(solution)/shard_map/ppermute | solution.py:297
  5.2 2.4 %coupling_own_half.1 = (bf16[512,1024]{1,0:T(8,128)(2,1)S(1)}, bf16[512,1024]{1,0:T(8,128)(2,1)S(1)}, f32[128,1024]{1,0:T(8,128)S(1)}, f32[128,512]{1,0:T(8,128)S(1)}) custom-call(f32[3,512,128]{2,1,0:T(8,128)S(1)} %get-tuple-element.34.wide_ref, f32[8,1024]{1,0:T(8,128)S(1)} %get-tuple-element.35.centre_ref, ...), custom_call_target="tpu_custom_call" | custom-call | bytes 6600000 | tf_op jit(solution)/shard_map/coupling_own_half/pallas_call | solution.py:235
  7.7 3.7 %collective-permute-start.5 = (f32[128,512]{1,0:T(8,128)S(1)}, f32[128,512]{1,0:T(8,128)S(1)}, u32[]{:S(2)}, u32[]{:S(2)}) collective-permute-start(f32[128,512]{1,0:T(8,128)S(1)} %get-tuple-element.43.refs_0_.a_ref), channel_id=1, source_target_pairs={{0,2},{1,3},{2,0},{3,1},{4,5},{5,4},{6,7},{7,6},{8,10},{9,11},{10,... | collective-permute-start | bytes 786440 | tf_op jit(solution)/shard_map/ppermute | solution.py:297
  11.3 0.0 collective-permute-done.b_ref
  11.3 0.1 add.16
  11.4 1.6 %collective-permute-start.1 = (f32[64,1024]{1,0:T(8,128)S(1)}, f32[64,1024]{1,0:T(8,128)S(1)}, u32[]{:S(2)}, u32[]{:S(2)}) collective-permute-start(f32[64,1024]{1,0:T(8,128)S(1)} %get-tuple-element.44.a_ref), channel_id=1, source_target_pairs={{0,8},{1,9},{2,10},{3,11},{4,20},{5,21},{6,22},{7,23},{8,0},{9,1},... | collective-permute-start | bytes 786440 | tf_op jit(solution)/shard_map/ppermute | solution.py:297
  12.9 0.5 %collective-permute-start.2 = (f32[64,1024]{1,0:T(8,128)S(1)}, f32[64,1024]{1,0:T(8,128)S(1)}, u32[]{:S(2)}, u32[]{:S(2)}) collective-permute-start(f32[64,1024]{1,0:T(8,128)S(1)} %get-tuple-element.45.a_ref), channel_id=1, source_target_pairs={{0,8},{1,9},{2,10},{3,11},{4,20},{5,21},{6,22},{7,23},{8,0},{9,1},... | collective-permute-start | bytes 786440 | tf_op jit(solution)/shard_map/ppermute | solution.py:297
  13.5 3.8 %collective-permute-done.5.b_ref = f32[128,512]{1,0:T(8,128)S(1)} collective-permute-done((f32[128,512]{1,0:T(8,128)S(1)}, f32[128,512]{1,0:T(8,128)S(1)}, u32[]{:S(2)}, u32[]{:S(2)}) %collective-permute-start.5) | collective-permute-done | bytes 262176 | tf_op jit(solution)/shard_map/ppermute | solution.py:297
  17.3 2.8 %collective-permute-start.6 = (f32[128,512]{1,0:T(8,128)S(1)}, f32[128,512]{1,0:T(8,128)S(1)}, u32[]{:S(2)}, u32[]{:S(2)}) collective-permute-start(f32[128,512]{1,0:T(8,128)S(1)} %add.19.left_ref), channel_id=1, source_target_pairs={{0,1},{1,0},{2,3},{3,2},{4,6},{5,7},{6,4},{7,5},{8,9},{9,8},{10,11... | collective-permute-start | bytes 786440 | tf_op jit(solution)/shard_map/ppermute | solution.py:297
  20.1 0.0 collective-permute-done.1.b_ref
  20.2 1.6 %collective-permute-start.3 = (f32[64,1024]{1,0:T(8,128)S(1)}, f32[64,1024]{1,0:T(8,128)S(1)}, u32[]{:S(2)}, u32[]{:S(2)}) collective-permute-start(f32[64,1024]{1,0:T(8,128)S(1)} %add.17.refs_0_), channel_id=1, source_target_pairs={{0,16},{1,17},{2,18},{3,19},{4,12},{5,13},{6,14},{7,15},{8,24},{9,... | collective-permute-start | bytes 786440 | tf_op jit(solution)/shard_map/ppermute | solution.py:297
  21.7 0.0 collective-permute-done.2.b_ref
  21.8 0.6 %collective-permute-start.4 = (f32[64,1024]{1,0:T(8,128)S(1)}, f32[64,1024]{1,0:T(8,128)S(1)}, u32[]{:S(2)}, u32[]{:S(2)}) collective-permute-start(f32[64,1024]{1,0:T(8,128)S(1)} %add.18.refs_1_), channel_id=1, source_target_pairs={{0,16},{1,17},{2,18},{3,19},{4,12},{5,13},{6,14},{7,15},{8,24},{9,... | collective-permute-start | bytes 786440 | tf_op jit(solution)/shard_map/ppermute | solution.py:297
  22.3 4.9 %collective-permute-done.6.right_ref = f32[128,512]{1,0:T(8,128)S(1)} collective-permute-done((f32[128,512]{1,0:T(8,128)S(1)}, f32[128,512]{1,0:T(8,128)S(1)}, u32[]{:S(2)}, u32[]{:S(2)}) %collective-permute-start.6) | collective-permute-done | bytes 262176 | tf_op jit(solution)/shard_map/ppermute | solution.py:297
  27.2 0.8 %elec_charges_to_drop_field.1 = (f32[128,1024]{1,0:T(8,128)S(1)}, bf16[256,512]{1,0:T(8,128)(2,1)S(1)}) custom-call(f32[128,512]{1,0:T(8,128)S(1)} %add.19.left_ref, f32[128,512]{1,0:T(8,128)S(1)} %collective-permute-done.6.right_ref, f32[128,512]{1,0:T(8,128)S(1)} %get-tuple-element.30.rhs_ref, f32[4,128,128]{2,1,0:T(8,128)S(1)} %get-tuple-element.31.inv_ref, ...), custom_call_target="tpu_custom_call" | custom-call | bytes 2640000 | tf_op jit(solution)/shard_map/elec_charges_to_drop_field/pallas_call | solution.py:235
  28.0 0.1 collective-permute-start.10
  28.1 0.6 %drop_field_of_own_half.1.refs_4_.a_ref = f32[128,1024]{1,0:T(8,128)S(1)} custom-call(bf16[256,512]{1,0:T(8,128)(2,1)S(1)} %get-tuple-element.46.both_ref, bf16[512,1024]{1,0:T(8,128)(2,1)S(1)} %get-tuple-element.47.high_ref, bf16[512,1024]{1,0:T(8,128)(2,1)S(1)} %get-tuple-element.48.low_ref), custom_call_target="tpu_custom_call" | custom-call | bytes 1980000 | tf_op jit(solution)/shard_map/drop_field_of_own_half/pallas_call | solution.py:235
  28.7 0.0 collective-permute-done.3.refs_2_
  28.7 0.7 %collective-permute-done.4.refs_3_ = f32[64,1024]{1,0:T(8,128)S(1)} collective-permute-done((f32[64,1024]{1,0:T(8,128)S(1)}, f32[64,1024]{1,0:T(8,128)S(1)}, u32[]{:S(2)}, u32[]{:S(2)}) %collective-permute-start.4) | collective-permute-done | bytes 262176 | tf_op jit(solution)/shard_map/ppermute | solution.py:297
  29.4 0.1 add.20.field_ref
  29.5 0.1 collective-permute-start.7
  29.5 0.4 collective-permute-done.10.b_ref
  30.0 0.1 add.22
  30.0 1.5 %collective-permute-start.11 = (f32[64,1024]{1,0:T(8,128)S(1)}, f32[64,1024]{1,0:T(8,128)S(1)}, u32[]{:S(2)}, u32[]{:S(2)}) collective-permute-start(f32[64,1024]{1,0:T(8,128)S(1)} %get-tuple-element.50.a_ref), channel_id=1, source_target_pairs={{0,8},{1,9},{2,10},{3,11},{4,20},{5,21},{6,22},{7,23},{8,0},{9,1},... | collective-permute-start | bytes 786440 | tf_op jit(solution)/shard_map/ppermute | solution.py:297
  31.6 0.5 %collective-permute-start.13 = (f32[64,1024]{1,0:T(8,128)S(1)}, f32[64,1024]{1,0:T(8,128)S(1)}, u32[]{:S(2)}, u32[]{:S(2)}) collective-permute-start(f32[64,1024]{1,0:T(8,128)S(1)} %get-tuple-element.53.a_ref), channel_id=1, source_target_pairs={{0,8},{1,9},{2,10},{3,11},{4,20},{5,21},{6,22},{7,23},{8,0},{9,1},... | collective-permute-start | bytes 786440 | tf_op jit(solution)/shard_map/ppermute | solution.py:297
  32.1 1.1 %elec_field_of_own_half.1.share_ref = f32[128,512]{1,0:T(8,128)S(1)} custom-call(s32[1]{0:T(128)} %bitcast.core_ref, f32[128,2048]{1,0:T(8,128)S(1)} %get-tuple-element.32.rhs_ref, f32[16,128,128]{2,1,0:T(8,128)S(1)} %get-tuple-element.33.inv_ref, f32[128,1024]{1,0:T(8,128)S(1)} %add.20.field_ref, bf16[512,1024]{1,0:T(8,128)(2,1)S(1)} %get-tuple-element.47.high_ref, ...), custom_call_target="tpu_custom_call" | custom-call | bytes 3300000 | tf_op jit(solution)/shard_map/elec_field_of_own_half/pallas_call | solution.py:235
  33.2 0.0 collective-permute-done.7.field_ref
  33.3 1.1 %elec_field_of_other_half.1.a_ref = f32[128,512]{1,0:T(8,128)S(1)} custom-call(s32[1]{0:T(128)} %bitcast.core_ref, f32[128,2048]{1,0:T(8,128)S(1)} %get-tuple-element.32.rhs_ref, f32[16,128,128]{2,1,0:T(8,128)S(1)} %get-tuple-element.33.inv_ref, f32[128,1024]{1,0:T(8,128)S(1)} %collective-permute-done.7.field_ref, ...), custom_call_target="tpu_custom_call" | custom-call | bytes 3300000 | tf_op jit(solution)/shard_map/elec_field_of_other_half/pallas_call | solution.py:235
  34.4 1.1 %collective-permute-start.8 = (f32[128,512]{1,0:T(8,128)S(1)}, f32[128,512]{1,0:T(8,128)S(1)}, u32[]{:S(2)}, u32[]{:S(2)}) collective-permute-start(f32[128,512]{1,0:T(8,128)S(1)} %elec_field_of_other_half.1.a_ref), channel_id=1, source_target_pairs={{0,1},{1,0},{2,3},{3,2},{4,6},{5,7},{6,4},{7,5},{8,9},{9,8},{10,11... | collective-permute-start | bytes 786440 | tf_op jit(solution)/shard_map/ppermute | solution.py:297
  35.5 1.0 %collective-permute-done.11.b_ref = f32[64,1024]{1,0:T(8,128)S(1)} collective-permute-done((f32[64,1024]{1,0:T(8,128)S(1)}, f32[64,1024]{1,0:T(8,128)S(1)}, u32[]{:S(2)}, u32[]{:S(2)}) %collective-permute-start.11) | collective-permute-done | bytes 262176 | tf_op jit(solution)/shard_map/ppermute | solution.py:297
  36.5 1.6 %collective-permute-start.12 = (f32[64,1024]{1,0:T(8,128)S(1)}, f32[64,1024]{1,0:T(8,128)S(1)}, u32[]{:S(2)}, u32[]{:S(2)}) collective-permute-start(f32[64,1024]{1,0:T(8,128)S(1)} %add.23.a_ref), channel_id=1, source_target_pairs={{0,16},{1,17},{2,18},{3,19},{4,12},{5,13},{6,14},{7,15},{8,24},{9,... | collective-permute-start | bytes 786440 | tf_op jit(solution)/shard_map/ppermute | solution.py:297
  38.1 1.2 %collective-permute-done.13.b_ref = f32[64,1024]{1,0:T(8,128)S(1)} collective-permute-done((f32[64,1024]{1,0:T(8,128)S(1)}, f32[64,1024]{1,0:T(8,128)S(1)}, u32[]{:S(2)}, u32[]{:S(2)}) %collective-permute-start.13) | collective-permute-done | bytes 262176 | tf_op jit(solution)/shard_map/ppermute | solution.py:297
  39.3 1.6 %collective-permute-start.14 = (f32[64,1024]{1,0:T(8,128)S(1)}, f32[64,1024]{1,0:T(8,128)S(1)}, u32[]{:S(2)}, u32[]{:S(2)}) collective-permute-start(f32[64,1024]{1,0:T(8,128)S(1)} %add.25.a_ref), channel_id=1, source_target_pairs={{0,16},{1,17},{2,18},{3,19},{4,12},{5,13},{6,14},{7,15},{8,24},{9,... | collective-permute-start | bytes 786440 | tf_op jit(solution)/shard_map/ppermute | solution.py:297
  40.9 0.9 %collective-permute-done.8.b_ref = f32[128,512]{1,0:T(8,128)S(1)} collective-permute-done((f32[128,512]{1,0:T(8,128)S(1)}, f32[128,512]{1,0:T(8,128)S(1)}, u32[]{:S(2)}, u32[]{:S(2)}) %collective-permute-start.8) | collective-permute-done | bytes 262176 | tf_op jit(solution)/shard_map/ppermute | solution.py:297
  41.8 2.6 %collective-permute-start.9 = (f32[128,512]{1,0:T(8,128)S(1)}, f32[128,512]{1,0:T(8,128)S(1)}, u32[]{:S(2)}, u32[]{:S(2)}) collective-permute-start(f32[128,512]{1,0:T(8,128)S(1)} %add.21.left_ref), channel_id=1, source_target_pairs={{0,2},{1,3},{2,0},{3,1},{4,5},{5,4},{6,7},{7,6},{8,10},{9,11},{10,... | collective-permute-start | bytes 786440 | tf_op jit(solution)/shard_map/ppermute | solution.py:297
  44.4 0.0 collective-permute-done.12.b_ref
  44.4 0.1 collective-permute-start.15
  44.5 0.5 collective-permute-start.16
  45.0 0.4 drop_charges.3.refs_0_.own_first_ref
  45.4 0.3 collective-permute-done.14.b_ref
  45.8 0.1 collective-permute-start.17
  45.8 0.5 collective-permute-start.18
  46.3 0.4 drop_charges.4.own_last_ref
  46.8 0.0 collective-permute-done.15.refs_0_
  46.8 0.0 collective-permute-done.16.refs_1_
  46.8 0.4 drop_charges.5.other_first_ref
  47.2 0.0 collective-permute-done.17.left_ref
  47.3 0.1 collective-permute-done.18.right_ref
  47.4 1.2 %last_drop_charges.1 = (f32[128,2048]{1,0:T(8,128)}, f32[8,128]{1,0:T(8,128)S(1)}) custom-call(s32[1]{0:T(128)} %bitcast.core_ref, f32[128,2048]{1,0:T(8,128)S(1)} %get-tuple-element.32.rhs_ref, f32[16,128,128]{2,1,0:T(8,128)S(1)} %get-tuple-element.33.inv_ref, f32[64,1024]{1,0:T(8,128)S(1)} %drop_charges.3.refs_0_.own_first_ref, ...), custom_call_target="tpu_custom_call" | custom-call | tf_op jit(solution)/shard_map/last_drop_charges/pallas_call | solution.py:256
  48.6 1.6 %collective-permute-done.9.right_ref = f32[128,512]{1,0:T(8,128)S(1)} collective-permute-done((f32[128,512]{1,0:T(8,128)S(1)}, f32[128,512]{1,0:T(8,128)S(1)}, u32[]{:S(2)}, u32[]{:S(2)}) %collective-permute-start.9) | collective-permute-done | bytes 262176 | tf_op jit(solution)/shard_map/ppermute | solution.py:297
  50.1 1.0 %elec_charges.1 = f32[128,512]{1,0:T(8,128)} custom-call(f32[128,512]{1,0:T(8,128)S(1)} %get-tuple-element.30.rhs_ref, f32[4,128,128]{2,1,0:T(8,128)S(1)} %get-tuple-element.31.inv_ref, f32[128,512]{1,0:T(8,128)S(1)} %add.21.left_ref, f32[128,512]{1,0:T(8,128)S(1)} %collective-permute-done.9.right_ref, f32[8,128]{1,0:T(8,128)S(1)} %get-tuple-element.56.after), custom_call_target="tpu_custom_call" | custom-call | bytes 3300000 | tf_op jit(solution)/shard_map/elec_charges/pallas_call | solution.py:235
  (8 shorter events, 0.2 us)
Async XLA Ops:
  4.7 6.6 %collective-permute-start = (f32[128,1024]{1,0:T(8,128)S(1)}, f32[128,1024]{1,0:T(8,128)S(1)}, u32[]{:S(2)}, u32[]{:S(2)}) collective-permute-start(f32[128,1024]{1,0:T(8,128)S(1)} %get-tuple-element.42), channel_id=1, source_target_pairs={{0,4},{1,5},{2,6},{3,7},{4,0},{5,1},{6,2},{7,3},{8,12},{9,13},{10,... | collective-permute-start | bytes 1572872 | tf_op jit(solution)/shard_map/ppermute | solution.py:297
  7.7 9.7 %collective-permute-start.5 = (f32[128,512]{1,0:T(8,128)S(1)}, f32[128,512]{1,0:T(8,128)S(1)}, u32[]{:S(2)}, u32[]{:S(2)}) collective-permute-start(f32[128,512]{1,0:T(8,128)S(1)} %get-tuple-element.43.refs_0_.a_ref), channel_id=1, source_target_pairs={{0,2},{1,3},{2,0},{3,1},{4,5},{5,4},{6,7},{7,6},{8,10},{9,11},{10,... | collective-permute-start | bytes 786440 | tf_op jit(solution)/shard_map/ppermute | solution.py:297
  11.4 8.7 %collective-permute-start.1 = (f32[64,1024]{1,0:T(8,128)S(1)}, f32[64,1024]{1,0:T(8,128)S(1)}, u32[]{:S(2)}, u32[]{:S(2)}) collective-permute-start(f32[64,1024]{1,0:T(8,128)S(1)} %get-tuple-element.44.a_ref), channel_id=1, source_target_pairs={{0,8},{1,9},{2,10},{3,11},{4,20},{5,21},{6,22},{7,23},{8,0},{9,1},... | collective-permute-start | bytes 786440 | tf_op jit(solution)/shard_map/ppermute | solution.py:297
  12.9 8.8 %collective-permute-start.2 = (f32[64,1024]{1,0:T(8,128)S(1)}, f32[64,1024]{1,0:T(8,128)S(1)}, u32[]{:S(2)}, u32[]{:S(2)}) collective-permute-start(f32[64,1024]{1,0:T(8,128)S(1)} %get-tuple-element.45.a_ref), channel_id=1, source_target_pairs={{0,8},{1,9},{2,10},{3,11},{4,20},{5,21},{6,22},{7,23},{8,0},{9,1},... | collective-permute-start | bytes 786440 | tf_op jit(solution)/shard_map/ppermute | solution.py:297
  17.3 9.9 %collective-permute-start.6 = (f32[128,512]{1,0:T(8,128)S(1)}, f32[128,512]{1,0:T(8,128)S(1)}, u32[]{:S(2)}, u32[]{:S(2)}) collective-permute-start(f32[128,512]{1,0:T(8,128)S(1)} %add.19.left_ref), channel_id=1, source_target_pairs={{0,1},{1,0},{2,3},{3,2},{4,6},{5,7},{6,4},{7,5},{8,9},{9,8},{10,11... | collective-permute-start | bytes 786440 | tf_op jit(solution)/shard_map/ppermute | solution.py:297
  20.2 8.5 %collective-permute-start.3 = (f32[64,1024]{1,0:T(8,128)S(1)}, f32[64,1024]{1,0:T(8,128)S(1)}, u32[]{:S(2)}, u32[]{:S(2)}) collective-permute-start(f32[64,1024]{1,0:T(8,128)S(1)} %add.17.refs_0_), channel_id=1, source_target_pairs={{0,16},{1,17},{2,18},{3,19},{4,12},{5,13},{6,14},{7,15},{8,24},{9,... | collective-permute-start | bytes 786440 | tf_op jit(solution)/shard_map/ppermute | solution.py:297
  21.8 7.6 %collective-permute-start.4 = (f32[64,1024]{1,0:T(8,128)S(1)}, f32[64,1024]{1,0:T(8,128)S(1)}, u32[]{:S(2)}, u32[]{:S(2)}) collective-permute-start(f32[64,1024]{1,0:T(8,128)S(1)} %add.18.refs_1_), channel_id=1, source_target_pairs={{0,16},{1,17},{2,18},{3,19},{4,12},{5,13},{6,14},{7,15},{8,24},{9,... | collective-permute-start | bytes 786440 | tf_op jit(solution)/shard_map/ppermute | solution.py:297
  28.0 2.0 %collective-permute-start.10 = (f32[128,1024]{1,0:T(8,128)S(1)}, f32[128,1024]{1,0:T(8,128)S(1)}, u32[]{:S(2)}, u32[]{:S(2)}) collective-permute-start(f32[128,1024]{1,0:T(8,128)S(1)} %get-tuple-element.49), channel_id=1, source_target_pairs={{0,4},{1,5},{2,6},{3,7},{4,0},{5,1},{6,2},{7,3},{8,12},{9,13},{10,... | collective-permute-start | bytes 1572872 | tf_op jit(solution)/shard_map/ppermute | solution.py:297
  29.5 3.8 %collective-permute-start.7 = (f32[128,1024]{1,0:T(8,128)S(1)}, f32[128,1024]{1,0:T(8,128)S(1)}, u32[]{:S(2)}, u32[]{:S(2)}) collective-permute-start(f32[128,1024]{1,0:T(8,128)S(1)} %add.20.field_ref), channel_id=1, source_target_pairs={{0,4},{1,5},{2,6},{3,7},{4,0},{5,1},{6,2},{7,3},{8,12},{9,13},{10,... | collective-permute-start | bytes 1572872 | tf_op jit(solution)/shard_map/ppermute | solution.py:297
  30.0 6.4 %collective-permute-start.11 = (f32[64,1024]{1,0:T(8,128)S(1)}, f32[64,1024]{1,0:T(8,128)S(1)}, u32[]{:S(2)}, u32[]{:S(2)}) collective-permute-start(f32[64,1024]{1,0:T(8,128)S(1)} %get-tuple-element.50.a_ref), channel_id=1, source_target_pairs={{0,8},{1,9},{2,10},{3,11},{4,20},{5,21},{6,22},{7,23},{8,0},{9,1},... | collective-permute-start | bytes 786440 | tf_op jit(solution)/shard_map/ppermute | solution.py:297
  31.6 7.7 %collective-permute-start.13 = (f32[64,1024]{1,0:T(8,128)S(1)}, f32[64,1024]{1,0:T(8,128)S(1)}, u32[]{:S(2)}, u32[]{:S(2)}) collective-permute-start(f32[64,1024]{1,0:T(8,128)S(1)} %get-tuple-element.53.a_ref), channel_id=1, source_target_pairs={{0,8},{1,9},{2,10},{3,11},{4,20},{5,21},{6,22},{7,23},{8,0},{9,1},... | collective-permute-start | bytes 786440 | tf_op jit(solution)/shard_map/ppermute | solution.py:297
  34.4 7.4 %collective-permute-start.8 = (f32[128,512]{1,0:T(8,128)S(1)}, f32[128,512]{1,0:T(8,128)S(1)}, u32[]{:S(2)}, u32[]{:S(2)}) collective-permute-start(f32[128,512]{1,0:T(8,128)S(1)} %elec_field_of_other_half.1.a_ref), channel_id=1, source_target_pairs={{0,1},{1,0},{2,3},{3,2},{4,6},{5,7},{6,4},{7,5},{8,9},{9,8},{10,11... | collective-permute-start | bytes 786440 | tf_op jit(solution)/shard_map/ppermute | solution.py:297
  36.5 7.9 %collective-permute-start.12 = (f32[64,1024]{1,0:T(8,128)S(1)}, f32[64,1024]{1,0:T(8,128)S(1)}, u32[]{:S(2)}, u32[]{:S(2)}) collective-permute-start(f32[64,1024]{1,0:T(8,128)S(1)} %add.23.a_ref), channel_id=1, source_target_pairs={{0,16},{1,17},{2,18},{3,19},{4,12},{5,13},{6,14},{7,15},{8,24},{9,... | collective-permute-start | bytes 786440 | tf_op jit(solution)/shard_map/ppermute | solution.py:297
  39.3 6.4 %collective-permute-start.14 = (f32[64,1024]{1,0:T(8,128)S(1)}, f32[64,1024]{1,0:T(8,128)S(1)}, u32[]{:S(2)}, u32[]{:S(2)}) collective-permute-start(f32[64,1024]{1,0:T(8,128)S(1)} %add.25.a_ref), channel_id=1, source_target_pairs={{0,16},{1,17},{2,18},{3,19},{4,12},{5,13},{6,14},{7,15},{8,24},{9,... | collective-permute-start | bytes 786440 | tf_op jit(solution)/shard_map/ppermute | solution.py:297
  41.8 8.4 %collective-permute-start.9 = (f32[128,512]{1,0:T(8,128)S(1)}, f32[128,512]{1,0:T(8,128)S(1)}, u32[]{:S(2)}, u32[]{:S(2)}) collective-permute-start(f32[128,512]{1,0:T(8,128)S(1)} %add.21.left_ref), channel_id=1, source_target_pairs={{0,2},{1,3},{2,0},{3,1},{4,5},{5,4},{6,7},{7,6},{8,10},{9,11},{10,... | collective-permute-start | bytes 786440 | tf_op jit(solution)/shard_map/ppermute | solution.py:297
  44.4 2.4 %collective-permute-start.15 = (f32[32,1024]{1,0:T(8,128)S(1)}, f32[32,1024]{1,0:T(8,128)S(1)}, u32[]{:S(2)}, u32[]{:S(2)}) collective-permute-start(f32[32,1024]{1,0:T(8,128)S(1)} %get-tuple-element.51.refs_0_), channel_id=1, source_target_pairs={{0,4},{1,5},{2,6},{3,7},{4,0},{5,1},{6,2},{7,3},{8,12},{9,13},{10,... | collective-permute-start | bytes 393224 | tf_op jit(solution)/shard_map/ppermute | solution.py:297
  44.5 2.3 %collective-permute-start.16 = (f32[32,1024]{1,0:T(8,128)S(1)}, f32[32,1024]{1,0:T(8,128)S(1)}, u32[]{:S(2)}, u32[]{:S(2)}) collective-permute-start(f32[32,1024]{1,0:T(8,128)S(1)} %get-tuple-element.52.refs_1_), channel_id=1, source_target_pairs={{0,4},{1,5},{2,6},{3,7},{4,0},{5,1},{6,2},{7,3},{8,12},{9,13},{10,... | collective-permute-start | bytes 393224 | tf_op jit(solution)/shard_map/ppermute | solution.py:297
  45.8 1.5 %collective-permute-start.17 = (f32[32,1024]{1,0:T(8,128)S(1)}, f32[32,1024]{1,0:T(8,128)S(1)}, u32[]{:S(2)}, u32[]{:S(2)}) collective-permute-start(f32[32,1024]{1,0:T(8,128)S(1)} %get-tuple-element.54.refs_0_), channel_id=1, source_target_pairs={{0,4},{1,5},{2,6},{3,7},{4,0},{5,1},{6,2},{7,3},{8,12},{9,13},{10,... | collective-permute-start | bytes 393224 | tf_op jit(solution)/shard_map/ppermute | solution.py:297
  45.8 1.5 %collective-permute-start.18 = (f32[32,1024]{1,0:T(8,128)S(1)}, f32[32,1024]{1,0:T(8,128)S(1)}, u32[]{:S(2)}, u32[]{:S(2)}) collective-permute-start(f32[32,1024]{1,0:T(8,128)S(1)} %get-tuple-element.55.refs_1_), channel_id=1, source_target_pairs={{0,4},{1,5},{2,6},{3,7},{4,0},{5,1},{6,2},{7,3},{8,12},{9,13},{10,... | collective-permute-start | bytes 393224 | tf_op jit(solution)/shard_map/ppermute | solution.py:297

commit v6 on v5

--- a/solution.py
+++ b/solution.py
@@ -169,8 +169,9 @@
     return jnp.concatenate([ref[...] for ref in refs], axis=0)
 
 
-def join_kernel(*refs):
-    refs[-1][...] = whole(refs[:PARTS]) + whole(refs[PARTS : 2 * PARTS])
+def drop_kernel(core_ref, rhs_ref, inv_ref, *refs):
+    field = whole(refs[:PARTS]) + whole(refs[PARTS : 2 * PARTS])
+    refs[-1][...] = drop_charge(core_ref[0], rhs_ref, inv_ref, field)
 
 
 def to_drop_kernel(couple, left_ref, right_ref, rhs_ref, inv_ref, high_ref, low_ref, send_ref, both_ref):
@@ -183,14 +184,13 @@
     keep_ref[...] = product(both_ref[...], (high_ref[...], low_ref[...]), ROWS_IN) * couple
 
 
-def own_kernel(core_ref, rhs_ref, inv_ref, field_ref, high_ref, low_ref, elec_ref):
-    charge = drop_charge(core_ref[0], rhs_ref, inv_ref, field_ref[...])
-    elec_ref[...] = product(stacked(charge), (high_ref[...], low_ref[...]), ROWS_OUT)
-
-
-def other_kernel(couple, core_ref, rhs_ref, inv_ref, field_ref, share_ref, high_ref, low_ref, elec_ref):
-    charge = drop_charge(1 - core_ref[0], rhs_ref, inv_ref, field_ref[...])
-    elec_ref[...] = (share_ref[...] + product(stacked(charge), (high_ref[...], low_ref[...]), ROWS_OUT)) * couple
+def own_kernel(charge_ref, high_ref, low_ref, elec_ref):
+    elec_ref[...] = product(stacked(charge_ref[...]), (high_ref[...], low_ref[...]), ROWS_OUT)
+
+
+def other_kernel(couple, charge_ref, share_ref, high_ref, low_ref, elec_ref):
+    field = product(stacked(charge_ref[...]), (high_ref[...], low_ref[...]), ROWS_OUT)
+    elec_ref[...] = (share_ref[...] + field) * couple
 
 
 def charges_kernel(is_other, at, core_ref, rhs_ref, inv_ref, *refs):
@@ -290,8 +290,8 @@
 
 def solution(mesh):
     elec_devices, drop_devices = mesh.shape["elec"], mesh.shape["drop"]
-    core_pairs, *first_pairs = exchanges(elec_devices, drop_devices, 0)
-    _, *second_pairs = exchanges(elec_devices, drop_devices, 1)
+    core_pairs, *first_pairs = exchanges(elec_devices, drop_devices, 1)
+    _, *second_pairs = exchanges(elec_devices, drop_devices, 0)
 
     def swap(value, pairs):
         return lax.ppermute(value, ("elec", "drop"), pairs)
@@ -352,22 +352,20 @@
             functools.partial(keep_kernel, couple), "drop_field_of_own_half", 0.6,
             (both, own_high, own_low), [VMEM] * 3, [((rows, half), f32)],
         )
-        field, = run(
-            join_kernel, "add", 0.1, [pair[at] for at in range(2) for pair in planes] + [keep],
-            [VMEM] * (2 * PARTS) + [ANY],
+        charge, = run(
+            drop_kernel, "drop_charges_of_own_half", 0.4,
+            (core, drop_rhs, drop_inv, *(pair[at] for at in range(2) for pair in planes), keep),
+            [SMEM] + [VMEM] * (2 + 2 * PARTS) + [ANY],
             [((rows, half), f32)],
         )
-        field_got = swap(field, core_pairs)
+        charge_got = swap(charge, core_pairs)
         share, = run(
-            own_kernel, "elec_field_of_own_half", 1.0,
-            (core, drop_rhs, drop_inv, field, own_high, own_low),
-            [SMEM] + [VMEM] * 5,
-            [((rows, elec), f32)],
+            own_kernel, "elec_field_of_own_half", 0.8, (charge, own_high, own_low), [VMEM] * 3, [((rows, elec), f32)]
         )
         line, = run(
-            functools.partial(other_kernel, couple), "elec_field_of_other_half", 1.0,
-            (core, drop_rhs, drop_inv, field_got, share, other_high, other_low),
-            [SMEM] + [VMEM] * 6,
+            functools.partial(other_kernel, couple), "elec_field_of_other_half", 0.8,
+            (charge_got, share, other_high, other_low),
+            [VMEM] * 4,
             [((rows, elec), f32)],
         )
         line, planes = steps(line, folded(keep, got), *second_pairs)

time: 52 us -> 51.6 us (level); the launches traced: 51.1 us -> 51.4 us
  waiting for transfers between devices: 15 us -> 15.6 us
    ppermute x19, waiting for transfers between devices: 15 us -> 15.6 us  [swap(): return lax.ppermute(value, ('elec', 'drop'), pairs)]
  transfers between devices with their start and end apart: 19 -> 19, of which waited for: 10 -> 9; matrix products, arithmetic and copies ran while one was open for 0% -> 0% of each run, Pallas kernels for 17% -> 17%
where the time goes in v6:
time: 51.6 us; the launch traced here: 51.4 us
  starting transfers between devices  21.3 us (41%)
  waiting for transfers between devices  15.6 us (30%)
  Pallas kernels  13.6 us (26%)
  between operations  0.85 us (2%)
    ppermute x19, starting transfers between devices, swap(): return lax.ppermute(value, ('elec', 'drop'), pairs)  21.3 us
    ppermute x19, waiting for transfers between devices, swap(): return lax.ppermute(value, ('elec', 'drop'), pairs)  15.6 us
    pallas_call x21, Pallas kernels, run(): pl.pallas_call(kernel, out_shape=[jax.ShapeDtypeStruct(shape, dtype) for...  12.4 us
    pallas_call x1, Pallas kernels, run_last(): pl.pallas_call(last_kernel, out_shape=[jax.ShapeDtypeStruct(drop_rhs.shap...  1.18 us
  transfers between devices with their start and end apart: 19, of which 9 were waited for; matrix products, arithmetic and copies ran while one was open for 0% of the time, Pallas kernels for 17%

profile of v6, /device:TPU:0, one launch (start us, length us, event | category | flops | bytes accessed | tf_op | source)
XLA Modules:
  0.0 51.4 jit_solution(12104239406326010012)
XLA Ops:
  0.6 4.1 %coupling_other_half.1 = (bf16[512,1024]{1,0:T(8,128)(2,1)S(1)}, bf16[512,1024]{1,0:T(8,128)(2,1)S(1)}, f32[128,1024]{1,0:T(8,128)S(1)}, f32[3,512,128]{2,1,0:T(...) custom-call(s32[1]{0:T(128)} %bitcast.core_ref, ...), custom_call_target="tpu_custom_call" | custom-call | bytes 13200000 | tf_op jit(solution)/shard_map/coupling_other_half/pallas_call | solution.py:235
  4.7 0.5 collective-permute-start
  5.2 2.4 %coupling_own_half.1 = (bf16[512,1024]{1,0:T(8,128)(2,1)S(1)}, bf16[512,1024]{1,0:T(8,128)(2,1)S(1)}, f32[128,1024]{1,0:T(8,128)S(1)}, f32[128,512]{1,0:T(8,128)S(1)}) custom-call(f32[3,512,128]{2,1,0:T(8,128)S(1)} %get-tuple-element.34.wide_ref, f32[8,1024]{1,0:T(8,128)S(1)} %get-tuple-element.35.centre_ref, ...), custom_call_target="tpu_custom_call" | custom-call | bytes 6600000 | tf_op jit(solution)/shard_map/coupling_own_half/pallas_call | solution.py:235
  7.6 2.7 %collective-permute-start.5 = (f32[128,512]{1,0:T(8,128)S(1)}, f32[128,512]{1,0:T(8,128)S(1)}, u32[]{:S(2)}, u32[]{:S(2)}) collective-permute-start(f32[128,512]{1,0:T(8,128)S(1)} %get-tuple-element.43.refs_0_.a_ref), channel_id=1, source_target_pairs={{0,1},{1,0},{2,3},{3,2},{4,6},{5,7},{6,4},{7,5},{8,9},{9,8},{10,11... | collective-permute-start | bytes 786440 | tf_op jit(solution)/shard_map/ppermute | solution.py:297
  10.3 0.0 collective-permute-done.b_ref
  10.3 0.1 add.15
  10.4 1.6 %collective-permute-start.1 = (f32[64,1024]{1,0:T(8,128)S(1)}, f32[64,1024]{1,0:T(8,128)S(1)}, u32[]{:S(2)}, u32[]{:S(2)}) collective-permute-start(f32[64,1024]{1,0:T(8,128)S(1)} %get-tuple-element.44.a_ref), channel_id=1, source_target_pairs={{0,8},{1,9},{2,10},{3,11},{4,20},{5,21},{6,22},{7,23},{8,0},{9,1},... | collective-permute-start | bytes 786440 | tf_op jit(solution)/shard_map/ppermute | solution.py:297
  11.9 0.5 %collective-permute-start.2 = (f32[64,1024]{1,0:T(8,128)S(1)}, f32[64,1024]{1,0:T(8,128)S(1)}, u32[]{:S(2)}, u32[]{:S(2)}) collective-permute-start(f32[64,1024]{1,0:T(8,128)S(1)} %get-tuple-element.45.a_ref), channel_id=1, source_target_pairs={{0,8},{1,9},{2,10},{3,11},{4,20},{5,21},{6,22},{7,23},{8,0},{9,1},... | collective-permute-start | bytes 786440 | tf_op jit(solution)/shard_map/ppermute | solution.py:297
  12.5 4.6 %collective-permute-done.5.b_ref = f32[128,512]{1,0:T(8,128)S(1)} collective-permute-done((f32[128,512]{1,0:T(8,128)S(1)}, f32[128,512]{1,0:T(8,128)S(1)}, u32[]{:S(2)}, u32[]{:S(2)}) %collective-permute-start.5) | collective-permute-done | bytes 262176 | tf_op jit(solution)/shard_map/ppermute | solution.py:297
  17.1 2.9 %collective-permute-start.6 = (f32[128,512]{1,0:T(8,128)S(1)}, f32[128,512]{1,0:T(8,128)S(1)}, u32[]{:S(2)}, u32[]{:S(2)}) collective-permute-start(f32[128,512]{1,0:T(8,128)S(1)} %add.18.left_ref), channel_id=1, source_target_pairs={{0,2},{1,3},{2,0},{3,1},{4,5},{5,4},{6,7},{7,6},{8,10},{9,11},{10,... | collective-permute-start | bytes 786440 | tf_op jit(solution)/shard_map/ppermute | solution.py:297
  20.0 0.0 collective-permute-done.1.b_ref
  20.0 1.6 %collective-permute-start.3 = (f32[64,1024]{1,0:T(8,128)S(1)}, f32[64,1024]{1,0:T(8,128)S(1)}, u32[]{:S(2)}, u32[]{:S(2)}) collective-permute-start(f32[64,1024]{1,0:T(8,128)S(1)} %add.16.refs_0_), channel_id=1, source_target_pairs={{0,16},{1,17},{2,18},{3,19},{4,12},{5,13},{6,14},{7,15},{8,24},{9,... | collective-permute-start | bytes 786440 | tf_op jit(solution)/shard_map/ppermute | solution.py:297
  21.6 0.0 collective-permute-done.2.b_ref
  21.7 0.6 %collective-permute-start.4 = (f32[64,1024]{1,0:T(8,128)S(1)}, f32[64,1024]{1,0:T(8,128)S(1)}, u32[]{:S(2)}, u32[]{:S(2)}) collective-permute-start(f32[64,1024]{1,0:T(8,128)S(1)} %add.17.refs_1_), channel_id=1, source_target_pairs={{0,16},{1,17},{2,18},{3,19},{4,12},{5,13},{6,14},{7,15},{8,24},{9,... | collective-permute-start | bytes 786440 | tf_op jit(solution)/shard_map/ppermute | solution.py:297
  22.2 3.8 %collective-permute-done.6.right_ref = f32[128,512]{1,0:T(8,128)S(1)} collective-permute-done((f32[128,512]{1,0:T(8,128)S(1)}, f32[128,512]{1,0:T(8,128)S(1)}, u32[]{:S(2)}, u32[]{:S(2)}) %collective-permute-start.6) | collective-permute-done | bytes 262176 | tf_op jit(solution)/shard_map/ppermute | solution.py:297
  26.1 0.8 %elec_charges_to_drop_field.1 = (f32[128,1024]{1,0:T(8,128)S(1)}, bf16[256,512]{1,0:T(8,128)(2,1)S(1)}) custom-call(f32[128,512]{1,0:T(8,128)S(1)} %add.18.left_ref, f32[128,512]{1,0:T(8,128)S(1)} %collective-permute-done.6.right_ref, f32[128,512]{1,0:T(8,128)S(1)} %get-tuple-element.30.rhs_ref, f32[4,128,128]{2,1,0:T(8,128)S(1)} %get-tuple-element.31.inv_ref, ...), custom_call_target="tpu_custom_call" | custom-call | bytes 2640000 | tf_op jit(solution)/shard_map/elec_charges_to_drop_field/pallas_call | solution.py:235
  26.8 0.1 collective-permute-start.10
  26.9 0.6 %drop_field_of_own_half.1.refs_4_.a_ref = f32[128,1024]{1,0:T(8,128)S(1)} custom-call(bf16[256,512]{1,0:T(8,128)(2,1)S(1)} %get-tuple-element.46.both_ref, bf16[512,1024]{1,0:T(8,128)(2,1)S(1)} %get-tuple-element.47.high_ref, bf16[512,1024]{1,0:T(8,128)(2,1)S(1)} %get-tuple-element.48.low_ref), custom_call_target="tpu_custom_call" | custom-call | bytes 1980000 | tf_op jit(solution)/shard_map/drop_field_of_own_half/pallas_call | solution.py:235
  27.5 0.0 collective-permute-done.3.refs_2_
  27.5 1.8 %collective-permute-done.4.refs_3_ = f32[64,1024]{1,0:T(8,128)S(1)} collective-permute-done((f32[64,1024]{1,0:T(8,128)S(1)}, f32[64,1024]{1,0:T(8,128)S(1)}, u32[]{:S(2)}, u32[]{:S(2)}) %collective-permute-start.4) | collective-permute-done | bytes 262176 | tf_op jit(solution)/shard_map/ppermute | solution.py:297
  29.3 0.5 drop_charges_of_own_half.1.charge_ref
  29.8 0.1 collective-permute-start.7
  29.9 0.0 collective-permute-done.10.b_ref
  29.9 0.1 add.20
  29.9 2.0 %collective-permute-start.11 = (f32[64,1024]{1,0:T(8,128)S(1)}, f32[64,1024]{1,0:T(8,128)S(1)}, u32[]{:S(2)}, u32[]{:S(2)}) collective-permute-start(f32[64,1024]{1,0:T(8,128)S(1)} %get-tuple-element.50.a_ref), channel_id=1, source_target_pairs={{0,8},{1,9},{2,10},{3,11},{4,20},{5,21},{6,22},{7,23},{8,0},{9,1},... | collective-permute-start | bytes 786440 | tf_op jit(solution)/shard_map/ppermute | solution.py:297
  31.9 0.1 collective-permute-start.13
  32.0 0.7 %elec_field_of_own_half.1.share_ref = f32[128,512]{1,0:T(8,128)S(1)} custom-call(f32[128,1024]{1,0:T(8,128)S(1)} %drop_charges_of_own_half.1.charge_ref, bf16[512,1024]{1,0:T(8,128)(2,1)S(1)} %get-tuple-element.47.high_ref, bf16[512,1024]{1,0:T(8,128)(2,1)S(1)} %get-tuple-element.48.low_ref), custom_call_target="tpu_custom_call" | custom-call | bytes 2640000 | tf_op jit(solution)/shard_map/elec_field_of_own_half/pallas_call | solution.py:235
  32.8 0.0 collective-permute-done.7.charge_ref
  32.8 0.8 %elec_field_of_other_half.1.a_ref = f32[128,512]{1,0:T(8,128)S(1)} custom-call(f32[128,1024]{1,0:T(8,128)S(1)} %collective-permute-done.7.charge_ref, f32[128,512]{1,0:T(8,128)S(1)} %elec_field_of_own_half.1.share_ref, bf16[512,1024]{1,0:T(8,128)(2,1)S(1)} %get-tuple-element.39.ohigh_ref.high_ref, bf16[512,1024]{1,0:T(8,128)(2,1)S(1)} %get-tuple-element.40.olow_ref.low_ref), custom_call_target="tpu_custom_call" | custom-call | bytes 2640000 | tf_op jit(solution)/shard_map/elec_field_of_other_half/pallas_call | solution.py:235
  33.6 1.4 %collective-permute-start.8 = (f32[128,512]{1,0:T(8,128)S(1)}, f32[128,512]{1,0:T(8,128)S(1)}, u32[]{:S(2)}, u32[]{:S(2)}) collective-permute-start(f32[128,512]{1,0:T(8,128)S(1)} %elec_field_of_other_half.1.a_ref), channel_id=1, source_target_pairs={{0,2},{1,3},{2,0},{3,1},{4,5},{5,4},{6,7},{7,6},{8,10},{9,11},{10,... | collective-permute-start | bytes 786440 | tf_op jit(solution)/shard_map/ppermute | solution.py:297
  35.0 1.4 %collective-permute-done.11.b_ref = f32[64,1024]{1,0:T(8,128)S(1)} collective-permute-done((f32[64,1024]{1,0:T(8,128)S(1)}, f32[64,1024]{1,0:T(8,128)S(1)}, u32[]{:S(2)}, u32[]{:S(2)}) %collective-permute-start.11) | collective-permute-done | bytes 262176 | tf_op jit(solution)/shard_map/ppermute | solution.py:297
  36.4 2.0 %collective-permute-start.12 = (f32[64,1024]{1,0:T(8,128)S(1)}, f32[64,1024]{1,0:T(8,128)S(1)}, u32[]{:S(2)}, u32[]{:S(2)}) collective-permute-start(f32[64,1024]{1,0:T(8,128)S(1)} %add.21.a_ref), channel_id=1, source_target_pairs={{0,16},{1,17},{2,18},{3,19},{4,12},{5,13},{6,14},{7,15},{8,24},{9,... | collective-permute-start | bytes 786440 | tf_op jit(solution)/shard_map/ppermute | solution.py:297
  38.4 1.2 %collective-permute-done.13.b_ref = f32[64,1024]{1,0:T(8,128)S(1)} collective-permute-done((f32[64,1024]{1,0:T(8,128)S(1)}, f32[64,1024]{1,0:T(8,128)S(1)}, u32[]{:S(2)}, u32[]{:S(2)}) %collective-permute-start.13) | collective-permute-done | bytes 262176 | tf_op jit(solution)/shard_map/ppermute | solution.py:297
  39.6 2.4 %collective-permute-start.14 = (f32[64,1024]{1,0:T(8,128)S(1)}, f32[64,1024]{1,0:T(8,128)S(1)}, u32[]{:S(2)}, u32[]{:S(2)}) collective-permute-start(f32[64,1024]{1,0:T(8,128)S(1)} %add.23.a_ref), channel_id=1, source_target_pairs={{0,16},{1,17},{2,18},{3,19},{4,12},{5,13},{6,14},{7,15},{8,24},{9,... | collective-permute-start | bytes 786440 | tf_op jit(solution)/shard_map/ppermute | solution.py:297
  42.0 0.6 %collective-permute-done.8.b_ref = f32[128,512]{1,0:T(8,128)S(1)} collective-permute-done((f32[128,512]{1,0:T(8,128)S(1)}, f32[128,512]{1,0:T(8,128)S(1)}, u32[]{:S(2)}, u32[]{:S(2)}) %collective-permute-start.8) | collective-permute-done | bytes 262176 | tf_op jit(solution)/shard_map/ppermute | solution.py:297
  42.6 1.8 %collective-permute-start.9 = (f32[128,512]{1,0:T(8,128)S(1)}, f32[128,512]{1,0:T(8,128)S(1)}, u32[]{:S(2)}, u32[]{:S(2)}) collective-permute-start(f32[128,512]{1,0:T(8,128)S(1)} %add.19.left_ref), channel_id=1, source_target_pairs={{0,1},{1,0},{2,3},{3,2},{4,6},{5,7},{6,4},{7,5},{8,9},{9,8},{10,11... | collective-permute-start | bytes 786440 | tf_op jit(solution)/shard_map/ppermute | solution.py:297
  44.4 0.0 collective-permute-done.12.b_ref
  44.4 0.1 collective-permute-start.15
  44.5 0.5 collective-permute-start.16
  45.0 0.4 drop_charges.3.refs_0_.own_first_ref
  45.5 0.9 %collective-permute-done.14.b_ref = f32[64,1024]{1,0:T(8,128)S(1)} collective-permute-done((f32[64,1024]{1,0:T(8,128)S(1)}, f32[64,1024]{1,0:T(8,128)S(1)}, u32[]{:S(2)}, u32[]{:S(2)}) %collective-permute-start.14) | collective-permute-done | bytes 262176 | tf_op jit(solution)/shard_map/ppermute | solution.py:297
  46.4 0.1 collective-permute-start.17
  46.5 0.5 collective-permute-start.18
  47.0 0.4 drop_charges.4.own_last_ref
  47.4 0.0 collective-permute-done.15.refs_0_
  47.4 0.0 collective-permute-done.16.refs_1_
  47.4 0.4 drop_charges.5.other_first_ref
  47.9 0.0 collective-permute-done.17.left_ref
  47.9 0.1 collective-permute-done.18.right_ref
  48.0 1.2 %last_drop_charges.1 = (f32[128,2048]{1,0:T(8,128)}, f32[8,128]{1,0:T(8,128)S(1)}) custom-call(s32[1]{0:T(128)} %bitcast.core_ref, f32[128,2048]{1,0:T(8,128)S(1)} %get-tuple-element.32.rhs_ref, f32[16,128,128]{2,1,0:T(8,128)S(1)} %get-tuple-element.33.inv_ref, f32[64,1024]{1,0:T(8,128)S(1)} %drop_charges.3.refs_0_.own_first_ref, ...), custom_call_target="tpu_custom_call" | custom-call | tf_op jit(solution)/shard_map/last_drop_charges/pallas_call | solution.py:256
  49.2 1.2 %collective-permute-done.9.right_ref = f32[128,512]{1,0:T(8,128)S(1)} collective-permute-done((f32[128,512]{1,0:T(8,128)S(1)}, f32[128,512]{1,0:T(8,128)S(1)}, u32[]{:S(2)}, u32[]{:S(2)}) %collective-permute-start.9) | collective-permute-done | bytes 262176 | tf_op jit(solution)/shard_map/ppermute | solution.py:297
  50.4 1.0 %elec_charges.1 = f32[128,512]{1,0:T(8,128)} custom-call(f32[128,512]{1,0:T(8,128)S(1)} %get-tuple-element.30.rhs_ref, f32[4,128,128]{2,1,0:T(8,128)S(1)} %get-tuple-element.31.inv_ref, f32[128,512]{1,0:T(8,128)S(1)} %add.19.left_ref, f32[128,512]{1,0:T(8,128)S(1)} %collective-permute-done.9.right_ref, f32[8,128]{1,0:T(8,128)S(1)} %get-tuple-element.56.after), custom_call_target="tpu_custom_call" | custom-call | bytes 3300000 | tf_op jit(solution)/shard_map/elec_charges/pallas_call | solution.py:235
  (8 shorter events, 0.2 us)
Async XLA Ops:
  4.7 5.6 %collective-permute-start = (f32[128,1024]{1,0:T(8,128)S(1)}, f32[128,1024]{1,0:T(8,128)S(1)}, u32[]{:S(2)}, u32[]{:S(2)}) collective-permute-start(f32[128,1024]{1,0:T(8,128)S(1)} %get-tuple-element.42), channel_id=1, source_target_pairs={{0,4},{1,5},{2,6},{3,7},{4,0},{5,1},{6,2},{7,3},{8,12},{9,13},{10,... | collective-permute-start | bytes 1572872 | tf_op jit(solution)/shard_map/ppermute | solution.py:297
  7.6 9.4 %collective-permute-start.5 = (f32[128,512]{1,0:T(8,128)S(1)}, f32[128,512]{1,0:T(8,128)S(1)}, u32[]{:S(2)}, u32[]{:S(2)}) collective-permute-start(f32[128,512]{1,0:T(8,128)S(1)} %get-tuple-element.43.refs_0_.a_ref), channel_id=1, source_target_pairs={{0,1},{1,0},{2,3},{3,2},{4,6},{5,7},{6,4},{7,5},{8,9},{9,8},{10,11... | collective-permute-start | bytes 786440 | tf_op jit(solution)/shard_map/ppermute | solution.py:297
  10.4 9.6 %collective-permute-start.1 = (f32[64,1024]{1,0:T(8,128)S(1)}, f32[64,1024]{1,0:T(8,128)S(1)}, u32[]{:S(2)}, u32[]{:S(2)}) collective-permute-start(f32[64,1024]{1,0:T(8,128)S(1)} %get-tuple-element.44.a_ref), channel_id=1, source_target_pairs={{0,8},{1,9},{2,10},{3,11},{4,20},{5,21},{6,22},{7,23},{8,0},{9,1},... | collective-permute-start | bytes 786440 | tf_op jit(solution)/shard_map/ppermute | solution.py:297
  11.9 9.7 %collective-permute-start.2 = (f32[64,1024]{1,0:T(8,128)S(1)}, f32[64,1024]{1,0:T(8,128)S(1)}, u32[]{:S(2)}, u32[]{:S(2)}) collective-permute-start(f32[64,1024]{1,0:T(8,128)S(1)} %get-tuple-element.45.a_ref), channel_id=1, source_target_pairs={{0,8},{1,9},{2,10},{3,11},{4,20},{5,21},{6,22},{7,23},{8,0},{9,1},... | collective-permute-start | bytes 786440 | tf_op jit(solution)/shard_map/ppermute | solution.py:297
  17.1 9.0 %collective-permute-start.6 = (f32[128,512]{1,0:T(8,128)S(1)}, f32[128,512]{1,0:T(8,128)S(1)}, u32[]{:S(2)}, u32[]{:S(2)}) collective-permute-start(f32[128,512]{1,0:T(8,128)S(1)} %add.18.left_ref), channel_id=1, source_target_pairs={{0,2},{1,3},{2,0},{3,1},{4,5},{5,4},{6,7},{7,6},{8,10},{9,11},{10,... | collective-permute-start | bytes 786440 | tf_op jit(solution)/shard_map/ppermute | solution.py:297
  20.0 7.5 %collective-permute-start.3 = (f32[64,1024]{1,0:T(8,128)S(1)}, f32[64,1024]{1,0:T(8,128)S(1)}, u32[]{:S(2)}, u32[]{:S(2)}) collective-permute-start(f32[64,1024]{1,0:T(8,128)S(1)} %add.16.refs_0_), channel_id=1, source_target_pairs={{0,16},{1,17},{2,18},{3,19},{4,12},{5,13},{6,14},{7,15},{8,24},{9,... | collective-permute-start | bytes 786440 | tf_op jit(solution)/shard_map/ppermute | solution.py:297
  21.7 7.6 %collective-permute-start.4 = (f32[64,1024]{1,0:T(8,128)S(1)}, f32[64,1024]{1,0:T(8,128)S(1)}, u32[]{:S(2)}, u32[]{:S(2)}) collective-permute-start(f32[64,1024]{1,0:T(8,128)S(1)} %add.17.refs_1_), channel_id=1, source_target_pairs={{0,16},{1,17},{2,18},{3,19},{4,12},{5,13},{6,14},{7,15},{8,24},{9,... | collective-permute-start | bytes 786440 | tf_op jit(solution)/shard_map/ppermute | solution.py:297
  26.8 3.0 %collective-permute-start.10 = (f32[128,1024]{1,0:T(8,128)S(1)}, f32[128,1024]{1,0:T(8,128)S(1)}, u32[]{:S(2)}, u32[]{:S(2)}) collective-permute-start(f32[128,1024]{1,0:T(8,128)S(1)} %get-tuple-element.49), channel_id=1, source_target_pairs={{0,4},{1,5},{2,6},{3,7},{4,0},{5,1},{6,2},{7,3},{8,12},{9,13},{10,... | collective-permute-start | bytes 1572872 | tf_op jit(solution)/shard_map/ppermute | solution.py:297
  29.8 3.0 %collective-permute-start.7 = (f32[128,1024]{1,0:T(8,128)S(1)}, f32[128,1024]{1,0:T(8,128)S(1)}, u32[]{:S(2)}, u32[]{:S(2)}) collective-permute-start(f32[128,1024]{1,0:T(8,128)S(1)} %drop_charges_of_own_half.1.charge_ref), channel_id=1, source_target_pairs={{0,4},{1,5},{2,6},{3,7},{4,0},{5,1},{6,2},{7,3},{8,12},{9,13},{10,... | collective-permute-start | bytes 1572872 | tf_op jit(solution)/shard_map/ppermute | solution.py:297
  29.9 6.4 %collective-permute-start.11 = (f32[64,1024]{1,0:T(8,128)S(1)}, f32[64,1024]{1,0:T(8,128)S(1)}, u32[]{:S(2)}, u32[]{:S(2)}) collective-permute-start(f32[64,1024]{1,0:T(8,128)S(1)} %get-tuple-element.50.a_ref), channel_id=1, source_target_pairs={{0,8},{1,9},{2,10},{3,11},{4,20},{5,21},{6,22},{7,23},{8,0},{9,1},... | collective-permute-start | bytes 786440 | tf_op jit(solution)/shard_map/ppermute | solution.py:297
  31.9 7.6 %collective-permute-start.13 = (f32[64,1024]{1,0:T(8,128)S(1)}, f32[64,1024]{1,0:T(8,128)S(1)}, u32[]{:S(2)}, u32[]{:S(2)}) collective-permute-start(f32[64,1024]{1,0:T(8,128)S(1)} %get-tuple-element.53.a_ref), channel_id=1, source_target_pairs={{0,8},{1,9},{2,10},{3,11},{4,20},{5,21},{6,22},{7,23},{8,0},{9,1},... | collective-permute-start | bytes 786440 | tf_op jit(solution)/shard_map/ppermute | solution.py:297
  33.6 9.0 %collective-permute-start.8 = (f32[128,512]{1,0:T(8,128)S(1)}, f32[128,512]{1,0:T(8,128)S(1)}, u32[]{:S(2)}, u32[]{:S(2)}) collective-permute-start(f32[128,512]{1,0:T(8,128)S(1)} %elec_field_of_other_half.1.a_ref), channel_id=1, source_target_pairs={{0,2},{1,3},{2,0},{3,1},{4,5},{5,4},{6,7},{7,6},{8,10},{9,11},{10,... | collective-permute-start | bytes 786440 | tf_op jit(solution)/shard_map/ppermute | solution.py:297
  36.4 8.0 %collective-permute-start.12 = (f32[64,1024]{1,0:T(8,128)S(1)}, f32[64,1024]{1,0:T(8,128)S(1)}, u32[]{:S(2)}, u32[]{:S(2)}) collective-permute-start(f32[64,1024]{1,0:T(8,128)S(1)} %add.21.a_ref), channel_id=1, source_target_pairs={{0,16},{1,17},{2,18},{3,19},{4,12},{5,13},{6,14},{7,15},{8,24},{9,... | collective-permute-start | bytes 786440 | tf_op jit(solution)/shard_map/ppermute | solution.py:297
  39.6 6.7 %collective-permute-start.14 = (f32[64,1024]{1,0:T(8,128)S(1)}, f32[64,1024]{1,0:T(8,128)S(1)}, u32[]{:S(2)}, u32[]{:S(2)}) collective-permute-start(f32[64,1024]{1,0:T(8,128)S(1)} %add.23.a_ref), channel_id=1, source_target_pairs={{0,16},{1,17},{2,18},{3,19},{4,12},{5,13},{6,14},{7,15},{8,24},{9,... | collective-permute-start | bytes 786440 | tf_op jit(solution)/shard_map/ppermute | solution.py:297
  42.6 7.8 %collective-permute-start.9 = (f32[128,512]{1,0:T(8,128)S(1)}, f32[128,512]{1,0:T(8,128)S(1)}, u32[]{:S(2)}, u32[]{:S(2)}) collective-permute-start(f32[128,512]{1,0:T(8,128)S(1)} %add.19.left_ref), channel_id=1, source_target_pairs={{0,1},{1,0},{2,3},{3,2},{4,6},{5,7},{6,4},{7,5},{8,9},{9,8},{10,11... | collective-permute-start | bytes 786440 | tf_op jit(solution)/shard_map/ppermute | solution.py:297
  44.4 3.0 %collective-permute-start.15 = (f32[32,1024]{1,0:T(8,128)S(1)}, f32[32,1024]{1,0:T(8,128)S(1)}, u32[]{:S(2)}, u32[]{:S(2)}) collective-permute-start(f32[32,1024]{1,0:T(8,128)S(1)} %get-tuple-element.51.refs_0_), channel_id=1, source_target_pairs={{0,4},{1,5},{2,6},{3,7},{4,0},{5,1},{6,2},{7,3},{8,12},{9,13},{10,... | collective-permute-start | bytes 393224 | tf_op jit(solution)/shard_map/ppermute | solution.py:297
  44.5 2.9 %collective-permute-start.16 = (f32[32,1024]{1,0:T(8,128)S(1)}, f32[32,1024]{1,0:T(8,128)S(1)}, u32[]{:S(2)}, u32[]{:S(2)}) collective-permute-start(f32[32,1024]{1,0:T(8,128)S(1)} %get-tuple-element.52.refs_1_), channel_id=1, source_target_pairs={{0,4},{1,5},{2,6},{3,7},{4,0},{5,1},{6,2},{7,3},{8,12},{9,13},{10,... | collective-permute-start | bytes 393224 | tf_op jit(solution)/shard_map/ppermute | solution.py:297
  46.4 1.5 %collective-permute-start.17 = (f32[32,1024]{1,0:T(8,128)S(1)}, f32[32,1024]{1,0:T(8,128)S(1)}, u32[]{:S(2)}, u32[]{:S(2)}) collective-permute-start(f32[32,1024]{1,0:T(8,128)S(1)} %get-tuple-element.54.refs_0_), channel_id=1, source_target_pairs={{0,4},{1,5},{2,6},{3,7},{4,0},{5,1},{6,2},{7,3},{8,12},{9,13},{10,... | collective-permute-start | bytes 393224 | tf_op jit(solution)/shard_map/ppermute | solution.py:297
  46.5 1.5 %collective-permute-start.18 = (f32[32,1024]{1,0:T(8,128)S(1)}, f32[32,1024]{1,0:T(8,128)S(1)}, u32[]{:S(2)}, u32[]{:S(2)}) collective-permute-start(f32[32,1024]{1,0:T(8,128)S(1)} %get-tuple-element.55.refs_1_), channel_id=1, source_target_pairs={{0,4},{1,5},{2,6},{3,7},{4,0},{5,1},{6,2},{7,3},{8,12},{9,13},{10,... | collective-permute-start | bytes 393224 | tf_op jit(solution)/shard_map/ppermute | solution.py:297

commit v7 on v6

--- a/solution.py
+++ b/solution.py
@@ -132,14 +132,13 @@
             out_ref[:, cols] = stacked(solve(dinv.at[pl.ds(block, CHUNK // LANES)], drhs[:, here]))
 
 
-def second_kernel(couple, wide_ref, centre_ref, both_ref, own_ref, other_ref, ohigh_ref, olow_ref,
-                  high_ref, low_ref, keep_ref, elec_ref):
+def second_kernel(couple, wide_ref, centre_ref, own_ref, other_ref, ohigh_ref, olow_ref,
+                  high_ref, low_ref, elec_ref):
     total = jnp.zeros(elec_ref.shape, jnp.float32)
     for start in range(0, high_ref.shape[1], CHUNK):
         cols = slice(start, start + CHUNK)
         weights = coupling_chunk(wide_ref, centre_ref, start)
         high_ref[:, cols], low_ref[:, cols] = weights
-        keep_ref[:, cols] = product(both_ref[...], weights, ROWS_IN) * couple
         total = total + product(other_ref[:, cols], (ohigh_ref[:, cols], olow_ref[:, cols]), ROWS_OUT)
         total = total + product(own_ref[:, cols], weights, ROWS_OUT)
     elec_ref[...] = total * couple
@@ -221,12 +220,16 @@
 
 
 def elec_kernel(rhs_ref, inv_ref, left_ref, right_ref, after, out_hbm, charge, sems):
+    both = stacked(rhs_ref[...] - (left_ref[...] + right_ref[...]))
     copies = []
-    for at in range(inv_ref.shape[0]):
+    blocks = inv_ref.shape[0]
+    for at in range(blocks):
         cols = slice(at * LANES, (at + 1) * LANES)
-        charge[:, cols] = solve_block(inv_ref[at], rhs_ref[:, cols] - (left_ref[:, cols] + right_ref[:, cols]))
-        copies.append(pltpu.make_async_copy(charge.at[:, cols], out_hbm.at[:, cols], sems.at[at]))
-        copies[-1].start()
+        charge[:, cols] = product(both[:, cols], split(inv_ref[at]), ROWS_OUT)
+        if at % 2:
+            two = slice((at - 1) * LANES, (at + 1) * LANES)
+            copies.append(pltpu.make_async_copy(charge.at[:, two], out_hbm.at[:, two], sems.at[at]))
+            copies[-1].start()
     for copy in copies:
         copy.wait()
 
@@ -325,11 +328,15 @@
             + [pltpu.VMEM((8, drop), f32), pltpu.SemaphoreType.DMA((7,))],
         )
         got = swap(send, core_pairs)
-        own_high, own_low, keep, line = run(
+        own_high, own_low, line = run(
             functools.partial(second_kernel, couple), "coupling_own_half", 2.0,
-            (wide, centre, both, own_charge, other_charge, other_high, other_low),
-            [VMEM] * 7,
-            [((elec, half), bf16)] * 2 + [((rows, half), f32), ((rows, elec), f32)],
+            (wide, centre, own_charge, other_charge, other_high, other_low),
+            [VMEM] * 6,
+            [((elec, half), bf16)] * 2 + [((rows, elec), f32)],
+        )
+        keep, = run(
+            functools.partial(keep_kernel, couple), "drop_field_of_own_half", 0.6,
+            (both, own_high, own_low), [VMEM] * 3, [((rows, half), f32)],
         )
         part = rows // PARTS
 

time: 51.6 us -> 51.3 us (level)
  waiting for transfers between devices: 15.6 us -> 15 us
    ppermute x19, waiting for transfers between devices: 15.6 us -> 15 us  [swap(): return lax.ppermute(value, ('elec', 'drop'), pairs)]
    pallas_call x21 -> x22, Pallas kernels: 12.4 us -> 12.8 us  [run(): pl.pallas_call(kernel, out_shape=[jax.ShapeDtypeStruct(shape, dtype) for...]
where the time goes in v7:
time: 51.3 us; the launch traced here: 51.2 us
  starting transfers between devices  21.3 us (42%)
  waiting for transfers between devices  15 us (29%)
  Pallas kernels  14 us (27%)
  between operations  0.86 us (2%)
    ppermute x19, starting transfers between devices, swap(): return lax.ppermute(value, ('elec', 'drop'), pairs)  21.3 us
    ppermute x19, waiting for transfers between devices, swap(): return lax.ppermute(value, ('elec', 'drop'), pairs)  15 us
    pallas_call x22, Pallas kernels, run(): pl.pallas_call(kernel, out_shape=[jax.ShapeDtypeStruct(shape, dtype) for...  12.8 us
    pallas_call x1, Pallas kernels, run_last(): pl.pallas_call(last_kernel, out_shape=[jax.ShapeDtypeStruct(drop_rhs.shap...  1.19 us
  transfers between devices with their start and end apart: 19, of which 9 were waited for; matrix products, arithmetic and copies ran while one was open for 0% of the time, Pallas kernels for 17%

profile of v7, /device:TPU:0, one launch (start us, length us, event | category | flops | bytes accessed | tf_op | source)
XLA Modules:
  0.0 51.2 jit_solution(7382678133087439761)
XLA Ops:
  0.6 4.1 %coupling_other_half.1 = (bf16[512,1024]{1,0:T(8,128)(2,1)S(1)}, bf16[512,1024]{1,0:T(8,128)(2,1)S(1)}, f32[128,1024]{1,0:T(8,128)S(1)}, f32[3,512,128]{2,1,0:T(...) custom-call(s32[1]{0:T(128)} %bitcast.core_ref, ...), custom_call_target="tpu_custom_call" | custom-call | bytes 13200000 | tf_op jit(solution)/shard_map/coupling_other_half/pallas_call | solution.py:238
  4.7 0.5 %collective-permute-start = (f32[128,1024]{1,0:T(8,128)S(1)}, f32[128,1024]{1,0:T(8,128)S(1)}, u32[]{:S(2)}, u32[]{:S(2)}) collective-permute-start(f32[128,1024]{1,0:T(8,128)S(1)} %get-tuple-element.42), channel_id=1, source_target_pairs={{0,4},{1,5},{2,6},{3,7},{4,0},{5,1},{6,2},{7,3},{8,12},{9,13},{10,... | collective-permute-start | bytes 1572872 | tf_op jit(solution)/shard_map/ppermute | solution.py:300
  5.2 2.1 %coupling_own_half.1 = (bf16[512,1024]{1,0:T(8,128)(2,1)S(1)}, bf16[512,1024]{1,0:T(8,128)(2,1)S(1)}, f32[128,512]{1,0:T(8,128)S(1)}) custom-call(f32[3,512,128]{2,1,0:T(8,128)S(1)} %get-tuple-element.34.wide_ref, f32[8,1024]{1,0:T(8,128)S(1)} %get-tuple-element.35.centre_ref, bf16[256,1024]{1,0:T(8,128)(2,1)S(1)} %get-tuple-element.36.own_ref, ...), custom_call_target="tpu_custom_call" | custom-call | bytes 6600000 | tf_op jit(solution)/shard_map/coupling_own_half/pallas_call | solution.py:238
  7.4 2.7 %collective-permute-start.5 = (f32[128,512]{1,0:T(8,128)S(1)}, f32[128,512]{1,0:T(8,128)S(1)}, u32[]{:S(2)}, u32[]{:S(2)}) collective-permute-start(f32[128,512]{1,0:T(8,128)S(1)} %get-tuple-element.43.refs_0_.a_ref), channel_id=1, source_target_pairs={{0,1},{1,0},{2,3},{3,2},{4,6},{5,7},{6,4},{7,5},{8,9},{9,8},{10,11... | collective-permute-start | bytes 786440 | tf_op jit(solution)/shard_map/ppermute | solution.py:300
  10.0 0.6 %drop_field_of_own_half.2.a_ref = f32[128,1024]{1,0:T(8,128)S(1)} custom-call(bf16[256,512]{1,0:T(8,128)(2,1)S(1)} %get-tuple-element.33.both_ref, bf16[512,1024]{1,0:T(8,128)(2,1)S(1)} %get-tuple-element.40.high_ref, bf16[512,1024]{1,0:T(8,128)(2,1)S(1)} %get-tuple-element.41.low_ref), custom_call_target="tpu_custom_call" | custom-call | bytes 1980000 | tf_op jit(solution)/shard_map/drop_field_of_own_half/pallas_call | solution.py:238
  10.6 0.0 collective-permute-done.b_ref
  10.6 0.1 add.15
  10.7 1.6 %collective-permute-start.1 = (f32[64,1024]{1,0:T(8,128)S(1)}, f32[64,1024]{1,0:T(8,128)S(1)}, u32[]{:S(2)}, u32[]{:S(2)}) collective-permute-start(f32[64,1024]{1,0:T(8,128)S(1)} %get-tuple-element.44.a_ref), channel_id=1, source_target_pairs={{0,8},{1,9},{2,10},{3,11},{4,20},{5,21},{6,22},{7,23},{8,0},{9,1},... | collective-permute-start | bytes 786440 | tf_op jit(solution)/shard_map/ppermute | solution.py:300
  12.2 0.5 %collective-permute-start.2 = (f32[64,1024]{1,0:T(8,128)S(1)}, f32[64,1024]{1,0:T(8,128)S(1)}, u32[]{:S(2)}, u32[]{:S(2)}) collective-permute-start(f32[64,1024]{1,0:T(8,128)S(1)} %get-tuple-element.45.a_ref), channel_id=1, source_target_pairs={{0,8},{1,9},{2,10},{3,11},{4,20},{5,21},{6,22},{7,23},{8,0},{9,1},... | collective-permute-start | bytes 786440 | tf_op jit(solution)/shard_map/ppermute | solution.py:300
  12.8 4.0 %collective-permute-done.5.b_ref = f32[128,512]{1,0:T(8,128)S(1)} collective-permute-done((f32[128,512]{1,0:T(8,128)S(1)}, f32[128,512]{1,0:T(8,128)S(1)}, u32[]{:S(2)}, u32[]{:S(2)}) %collective-permute-start.5) | collective-permute-done | bytes 262176 | tf_op jit(solution)/shard_map/ppermute | solution.py:300
  16.9 2.9 %collective-permute-start.6 = (f32[128,512]{1,0:T(8,128)S(1)}, f32[128,512]{1,0:T(8,128)S(1)}, u32[]{:S(2)}, u32[]{:S(2)}) collective-permute-start(f32[128,512]{1,0:T(8,128)S(1)} %add.18.left_ref), channel_id=1, source_target_pairs={{0,2},{1,3},{2,0},{3,1},{4,5},{5,4},{6,7},{7,6},{8,10},{9,11},{10,... | collective-permute-start | bytes 786440 | tf_op jit(solution)/shard_map/ppermute | solution.py:300
  19.7 0.0 collective-permute-done.1.b_ref
  19.8 1.6 %collective-permute-start.3 = (f32[64,1024]{1,0:T(8,128)S(1)}, f32[64,1024]{1,0:T(8,128)S(1)}, u32[]{:S(2)}, u32[]{:S(2)}) collective-permute-start(f32[64,1024]{1,0:T(8,128)S(1)} %add.16.refs_0_), channel_id=1, source_target_pairs={{0,16},{1,17},{2,18},{3,19},{4,12},{5,13},{6,14},{7,15},{8,24},{9,... | collective-permute-start | bytes 786440 | tf_op jit(solution)/shard_map/ppermute | solution.py:300
  21.3 0.0 collective-permute-done.2.b_ref
  21.4 0.6 %collective-permute-start.4 = (f32[64,1024]{1,0:T(8,128)S(1)}, f32[64,1024]{1,0:T(8,128)S(1)}, u32[]{:S(2)}, u32[]{:S(2)}) collective-permute-start(f32[64,1024]{1,0:T(8,128)S(1)} %add.17.refs_1_), channel_id=1, source_target_pairs={{0,16},{1,17},{2,18},{3,19},{4,12},{5,13},{6,14},{7,15},{8,24},{9,... | collective-permute-start | bytes 786440 | tf_op jit(solution)/shard_map/ppermute | solution.py:300
  22.0 3.9 %collective-permute-done.6.right_ref = f32[128,512]{1,0:T(8,128)S(1)} collective-permute-done((f32[128,512]{1,0:T(8,128)S(1)}, f32[128,512]{1,0:T(8,128)S(1)}, u32[]{:S(2)}, u32[]{:S(2)}) %collective-permute-start.6) | collective-permute-done | bytes 262176 | tf_op jit(solution)/shard_map/ppermute | solution.py:300
  25.8 0.8 %elec_charges_to_drop_field.1 = (f32[128,1024]{1,0:T(8,128)S(1)}, bf16[256,512]{1,0:T(8,128)(2,1)S(1)}) custom-call(f32[128,512]{1,0:T(8,128)S(1)} %add.18.left_ref, f32[128,512]{1,0:T(8,128)S(1)} %collective-permute-done.6.right_ref, f32[128,512]{1,0:T(8,128)S(1)} %get-tuple-element.29.rhs_ref, f32[4,128,128]{2,1,0:T(8,128)S(1)} %get-tuple-element.30.inv_ref, ...), custom_call_target="tpu_custom_call" | custom-call | bytes 2640000 | tf_op jit(solution)/shard_map/elec_charges_to_drop_field/pallas_call | solution.py:238
  26.6 0.1 collective-permute-start.10
  26.7 0.6 %drop_field_of_own_half.3.refs_4_.a_ref = f32[128,1024]{1,0:T(8,128)S(1)} custom-call(bf16[256,512]{1,0:T(8,128)(2,1)S(1)} %get-tuple-element.46.both_ref, bf16[512,1024]{1,0:T(8,128)(2,1)S(1)} %get-tuple-element.40.high_ref, bf16[512,1024]{1,0:T(8,128)(2,1)S(1)} %get-tuple-element.41.low_ref), custom_call_target="tpu_custom_call" | custom-call | bytes 1980000 | tf_op jit(solution)/shard_map/drop_field_of_own_half/pallas_call | solution.py:238
  27.3 0.0 collective-permute-done.3.refs_2_
  27.3 1.7 %collective-permute-done.4.refs_3_ = f32[64,1024]{1,0:T(8,128)S(1)} collective-permute-done((f32[64,1024]{1,0:T(8,128)S(1)}, f32[64,1024]{1,0:T(8,128)S(1)}, u32[]{:S(2)}, u32[]{:S(2)}) %collective-permute-start.4) | collective-permute-done | bytes 262176 | tf_op jit(solution)/shard_map/ppermute | solution.py:300
  29.0 0.5 drop_charges_of_own_half.1.charge_ref
  29.5 0.1 collective-permute-start.7
  29.6 0.0 collective-permute-done.10.b_ref
  29.6 0.1 add.20
  29.7 2.0 %collective-permute-start.11 = (f32[64,1024]{1,0:T(8,128)S(1)}, f32[64,1024]{1,0:T(8,128)S(1)}, u32[]{:S(2)}, u32[]{:S(2)}) collective-permute-start(f32[64,1024]{1,0:T(8,128)S(1)} %get-tuple-element.48.a_ref), channel_id=1, source_target_pairs={{0,8},{1,9},{2,10},{3,11},{4,20},{5,21},{6,22},{7,23},{8,0},{9,1},... | collective-permute-start | bytes 786440 | tf_op jit(solution)/shard_map/ppermute | solution.py:300
  31.7 0.1 collective-permute-start.13
  31.7 0.8 %elec_field_of_own_half.1.share_ref = f32[128,512]{1,0:T(8,128)S(1)} custom-call(f32[128,1024]{1,0:T(8,128)S(1)} %drop_charges_of_own_half.1.charge_ref, bf16[512,1024]{1,0:T(8,128)(2,1)S(1)} %get-tuple-element.40.high_ref, bf16[512,1024]{1,0:T(8,128)(2,1)S(1)} %get-tuple-element.41.low_ref), custom_call_target="tpu_custom_call" | custom-call | bytes 2640000 | tf_op jit(solution)/shard_map/elec_field_of_own_half/pallas_call | solution.py:238
  32.5 0.0 collective-permute-done.7.charge_ref
  32.5 0.8 %elec_field_of_other_half.1.a_ref = f32[128,512]{1,0:T(8,128)S(1)} custom-call(f32[128,1024]{1,0:T(8,128)S(1)} %collective-permute-done.7.charge_ref, f32[128,512]{1,0:T(8,128)S(1)} %elec_field_of_own_half.1.share_ref, bf16[512,1024]{1,0:T(8,128)(2,1)S(1)} %get-tuple-element.38.ohigh_ref.high_ref, bf16[512,1024]{1,0:T(8,128)(2,1)S(1)} %get-tuple-element.39.olow_ref.low_ref), custom_call_target="tpu_custom_call" | custom-call | bytes 2640000 | tf_op jit(solution)/shard_map/elec_field_of_other_half/pallas_call | solution.py:238
  33.3 1.5 %collective-permute-start.8 = (f32[128,512]{1,0:T(8,128)S(1)}, f32[128,512]{1,0:T(8,128)S(1)}, u32[]{:S(2)}, u32[]{:S(2)}) collective-permute-start(f32[128,512]{1,0:T(8,128)S(1)} %elec_field_of_other_half.1.a_ref), channel_id=1, source_target_pairs={{0,2},{1,3},{2,0},{3,1},{4,5},{5,4},{6,7},{7,6},{8,10},{9,11},{10,... | collective-permute-start | bytes 786440 | tf_op jit(solution)/shard_map/ppermute | solution.py:300
  34.7 1.4 %collective-permute-done.11.b_ref = f32[64,1024]{1,0:T(8,128)S(1)} collective-permute-done((f32[64,1024]{1,0:T(8,128)S(1)}, f32[64,1024]{1,0:T(8,128)S(1)}, u32[]{:S(2)}, u32[]{:S(2)}) %collective-permute-start.11) | collective-permute-done | bytes 262176 | tf_op jit(solution)/shard_map/ppermute | solution.py:300
  36.1 2.0 %collective-permute-start.12 = (f32[64,1024]{1,0:T(8,128)S(1)}, f32[64,1024]{1,0:T(8,128)S(1)}, u32[]{:S(2)}, u32[]{:S(2)}) collective-permute-start(f32[64,1024]{1,0:T(8,128)S(1)} %add.21.a_ref), channel_id=1, source_target_pairs={{0,16},{1,17},{2,18},{3,19},{4,12},{5,13},{6,14},{7,15},{8,24},{9,... | collective-permute-start | bytes 786440 | tf_op jit(solution)/shard_map/ppermute | solution.py:300
  38.2 1.2 %collective-permute-done.13.b_ref = f32[64,1024]{1,0:T(8,128)S(1)} collective-permute-done((f32[64,1024]{1,0:T(8,128)S(1)}, f32[64,1024]{1,0:T(8,128)S(1)}, u32[]{:S(2)}, u32[]{:S(2)}) %collective-permute-start.13) | collective-permute-done | bytes 262176 | tf_op jit(solution)/shard_map/ppermute | solution.py:300
  39.4 2.4 %collective-permute-start.14 = (f32[64,1024]{1,0:T(8,128)S(1)}, f32[64,1024]{1,0:T(8,128)S(1)}, u32[]{:S(2)}, u32[]{:S(2)}) collective-permute-start(f32[64,1024]{1,0:T(8,128)S(1)} %add.23.a_ref), channel_id=1, source_target_pairs={{0,16},{1,17},{2,18},{3,19},{4,12},{5,13},{6,14},{7,15},{8,24},{9,... | collective-permute-start | bytes 786440 | tf_op jit(solution)/shard_map/ppermute | solution.py:300
  41.7 0.6 %collective-permute-done.8.b_ref = f32[128,512]{1,0:T(8,128)S(1)} collective-permute-done((f32[128,512]{1,0:T(8,128)S(1)}, f32[128,512]{1,0:T(8,128)S(1)}, u32[]{:S(2)}, u32[]{:S(2)}) %collective-permute-start.8) | collective-permute-done | bytes 262176 | tf_op jit(solution)/shard_map/ppermute | solution.py:300
  42.3 1.8 %collective-permute-start.9 = (f32[128,512]{1,0:T(8,128)S(1)}, f32[128,512]{1,0:T(8,128)S(1)}, u32[]{:S(2)}, u32[]{:S(2)}) collective-permute-start(f32[128,512]{1,0:T(8,128)S(1)} %add.19.left_ref), channel_id=1, source_target_pairs={{0,1},{1,0},{2,3},{3,2},{4,6},{5,7},{6,4},{7,5},{8,9},{9,8},{10,11... | collective-permute-start | bytes 786440 | tf_op jit(solution)/shard_map/ppermute | solution.py:300
  44.1 0.0 collective-permute-done.12.b_ref
  44.2 0.1 collective-permute-start.15
  44.3 0.5 collective-permute-start.16
  44.7 0.4 drop_charges.3.refs_0_.own_first_ref
  45.2 0.9 %collective-permute-done.14.b_ref = f32[64,1024]{1,0:T(8,128)S(1)} collective-permute-done((f32[64,1024]{1,0:T(8,128)S(1)}, f32[64,1024]{1,0:T(8,128)S(1)}, u32[]{:S(2)}, u32[]{:S(2)}) %collective-permute-start.14) | collective-permute-done | bytes 262176 | tf_op jit(solution)/shard_map/ppermute | solution.py:300
  46.1 0.1 collective-permute-start.17
  46.2 0.5 collective-permute-start.18
  46.7 0.4 drop_charges.4.own_last_ref
  47.1 0.0 collective-permute-done.15.refs_0_
  47.2 0.0 collective-permute-done.16.refs_1_
  47.2 0.4 drop_charges.5.other_first_ref
  47.6 0.0 collective-permute-done.17.left_ref
  47.6 0.1 collective-permute-done.18.right_ref
  47.7 1.2 %last_drop_charges.1 = (f32[128,2048]{1,0:T(8,128)}, f32[8,128]{1,0:T(8,128)S(1)}) custom-call(s32[1]{0:T(128)} %bitcast.core_ref, f32[128,2048]{1,0:T(8,128)S(1)} %get-tuple-element.31.rhs_ref, f32[16,128,128]{2,1,0:T(8,128)S(1)} %get-tuple-element.32.inv_ref, f32[64,1024]{1,0:T(8,128)S(1)} %drop_charges.3.refs_0_.own_first_ref, ...), custom_call_target="tpu_custom_call" | custom-call | tf_op jit(solution)/shard_map/last_drop_charges/pallas_call | solution.py:259
  48.9 1.3 %collective-permute-done.9.right_ref = f32[128,512]{1,0:T(8,128)S(1)} collective-permute-done((f32[128,512]{1,0:T(8,128)S(1)}, f32[128,512]{1,0:T(8,128)S(1)}, u32[]{:S(2)}, u32[]{:S(2)}) %collective-permute-start.9) | collective-permute-done | bytes 262176 | tf_op jit(solution)/shard_map/ppermute | solution.py:300
  50.2 1.0 %elec_charges.1 = f32[128,512]{1,0:T(8,128)} custom-call(f32[128,512]{1,0:T(8,128)S(1)} %get-tuple-element.29.rhs_ref, f32[4,128,128]{2,1,0:T(8,128)S(1)} %get-tuple-element.30.inv_ref, f32[128,512]{1,0:T(8,128)S(1)} %add.19.left_ref, f32[128,512]{1,0:T(8,128)S(1)} %collective-permute-done.9.right_ref, f32[8,128]{1,0:T(8,128)S(1)} %get-tuple-element.54.after), custom_call_target="tpu_custom_call" | custom-call | bytes 3300000 | tf_op jit(solution)/shard_map/elec_charges/pallas_call | solution.py:238
  (8 shorter events, 0.2 us)
Async XLA Ops:
  4.7 5.9 %collective-permute-start = (f32[128,1024]{1,0:T(8,128)S(1)}, f32[128,1024]{1,0:T(8,128)S(1)}, u32[]{:S(2)}, u32[]{:S(2)}) collective-permute-start(f32[128,1024]{1,0:T(8,128)S(1)} %get-tuple-element.42), channel_id=1, source_target_pairs={{0,4},{1,5},{2,6},{3,7},{4,0},{5,1},{6,2},{7,3},{8,12},{9,13},{10,... | collective-permute-start | bytes 1572872 | tf_op jit(solution)/shard_map/ppermute | solution.py:300
  7.4 9.5 %collective-permute-start.5 = (f32[128,512]{1,0:T(8,128)S(1)}, f32[128,512]{1,0:T(8,128)S(1)}, u32[]{:S(2)}, u32[]{:S(2)}) collective-permute-start(f32[128,512]{1,0:T(8,128)S(1)} %get-tuple-element.43.refs_0_.a_ref), channel_id=1, source_target_pairs={{0,1},{1,0},{2,3},{3,2},{4,6},{5,7},{6,4},{7,5},{8,9},{9,8},{10,11... | collective-permute-start | bytes 786440 | tf_op jit(solution)/shard_map/ppermute | solution.py:300
  10.7 9.0 %collective-permute-start.1 = (f32[64,1024]{1,0:T(8,128)S(1)}, f32[64,1024]{1,0:T(8,128)S(1)}, u32[]{:S(2)}, u32[]{:S(2)}) collective-permute-start(f32[64,1024]{1,0:T(8,128)S(1)} %get-tuple-element.44.a_ref), channel_id=1, source_target_pairs={{0,8},{1,9},{2,10},{3,11},{4,20},{5,21},{6,22},{7,23},{8,0},{9,1},... | collective-permute-start | bytes 786440 | tf_op jit(solution)/shard_map/ppermute | solution.py:300
  12.2 9.1 %collective-permute-start.2 = (f32[64,1024]{1,0:T(8,128)S(1)}, f32[64,1024]{1,0:T(8,128)S(1)}, u32[]{:S(2)}, u32[]{:S(2)}) collective-permute-start(f32[64,1024]{1,0:T(8,128)S(1)} %get-tuple-element.45.a_ref), channel_id=1, source_target_pairs={{0,8},{1,9},{2,10},{3,11},{4,20},{5,21},{6,22},{7,23},{8,0},{9,1},... | collective-permute-start | bytes 786440 | tf_op jit(solution)/shard_map/ppermute | solution.py:300
  16.9 9.0 %collective-permute-start.6 = (f32[128,512]{1,0:T(8,128)S(1)}, f32[128,512]{1,0:T(8,128)S(1)}, u32[]{:S(2)}, u32[]{:S(2)}) collective-permute-start(f32[128,512]{1,0:T(8,128)S(1)} %add.18.left_ref), channel_id=1, source_target_pairs={{0,2},{1,3},{2,0},{3,1},{4,5},{5,4},{6,7},{7,6},{8,10},{9,11},{10,... | collective-permute-start | bytes 786440 | tf_op jit(solution)/shard_map/ppermute | solution.py:300
  19.8 7.5 %collective-permute-start.3 = (f32[64,1024]{1,0:T(8,128)S(1)}, f32[64,1024]{1,0:T(8,128)S(1)}, u32[]{:S(2)}, u32[]{:S(2)}) collective-permute-start(f32[64,1024]{1,0:T(8,128)S(1)} %add.16.refs_0_), channel_id=1, source_target_pairs={{0,16},{1,17},{2,18},{3,19},{4,12},{5,13},{6,14},{7,15},{8,24},{9,... | collective-permute-start | bytes 786440 | tf_op jit(solution)/shard_map/ppermute | solution.py:300
  21.4 7.6 %collective-permute-start.4 = (f32[64,1024]{1,0:T(8,128)S(1)}, f32[64,1024]{1,0:T(8,128)S(1)}, u32[]{:S(2)}, u32[]{:S(2)}) collective-permute-start(f32[64,1024]{1,0:T(8,128)S(1)} %add.17.refs_1_), channel_id=1, source_target_pairs={{0,16},{1,17},{2,18},{3,19},{4,12},{5,13},{6,14},{7,15},{8,24},{9,... | collective-permute-start | bytes 786440 | tf_op jit(solution)/shard_map/ppermute | solution.py:300
  26.6 3.0 %collective-permute-start.10 = (f32[128,1024]{1,0:T(8,128)S(1)}, f32[128,1024]{1,0:T(8,128)S(1)}, u32[]{:S(2)}, u32[]{:S(2)}) collective-permute-start(f32[128,1024]{1,0:T(8,128)S(1)} %get-tuple-element.47), channel_id=1, source_target_pairs={{0,4},{1,5},{2,6},{3,7},{4,0},{5,1},{6,2},{7,3},{8,12},{9,13},{10,... | collective-permute-start | bytes 1572872 | tf_op jit(solution)/shard_map/ppermute | solution.py:300
  29.5 3.0 %collective-permute-start.7 = (f32[128,1024]{1,0:T(8,128)S(1)}, f32[128,1024]{1,0:T(8,128)S(1)}, u32[]{:S(2)}, u32[]{:S(2)}) collective-permute-start(f32[128,1024]{1,0:T(8,128)S(1)} %drop_charges_of_own_half.1.charge_ref), channel_id=1, source_target_pairs={{0,4},{1,5},{2,6},{3,7},{4,0},{5,1},{6,2},{7,3},{8,12},{9,13},{10,... | collective-permute-start | bytes 1572872 | tf_op jit(solution)/shard_map/ppermute | solution.py:300
  29.7 6.4 %collective-permute-start.11 = (f32[64,1024]{1,0:T(8,128)S(1)}, f32[64,1024]{1,0:T(8,128)S(1)}, u32[]{:S(2)}, u32[]{:S(2)}) collective-permute-start(f32[64,1024]{1,0:T(8,128)S(1)} %get-tuple-element.48.a_ref), channel_id=1, source_target_pairs={{0,8},{1,9},{2,10},{3,11},{4,20},{5,21},{6,22},{7,23},{8,0},{9,1},... | collective-permute-start | bytes 786440 | tf_op jit(solution)/shard_map/ppermute | solution.py:300
  31.7 7.7 %collective-permute-start.13 = (f32[64,1024]{1,0:T(8,128)S(1)}, f32[64,1024]{1,0:T(8,128)S(1)}, u32[]{:S(2)}, u32[]{:S(2)}) collective-permute-start(f32[64,1024]{1,0:T(8,128)S(1)} %get-tuple-element.51.a_ref), channel_id=1, source_target_pairs={{0,8},{1,9},{2,10},{3,11},{4,20},{5,21},{6,22},{7,23},{8,0},{9,1},... | collective-permute-start | bytes 786440 | tf_op jit(solution)/shard_map/ppermute | solution.py:300
  33.3 9.0 %collective-permute-start.8 = (f32[128,512]{1,0:T(8,128)S(1)}, f32[128,512]{1,0:T(8,128)S(1)}, u32[]{:S(2)}, u32[]{:S(2)}) collective-permute-start(f32[128,512]{1,0:T(8,128)S(1)} %elec_field_of_other_half.1.a_ref), channel_id=1, source_target_pairs={{0,2},{1,3},{2,0},{3,1},{4,5},{5,4},{6,7},{7,6},{8,10},{9,11},{10,... | collective-permute-start | bytes 786440 | tf_op jit(solution)/shard_map/ppermute | solution.py:300
  36.1 8.0 %collective-permute-start.12 = (f32[64,1024]{1,0:T(8,128)S(1)}, f32[64,1024]{1,0:T(8,128)S(1)}, u32[]{:S(2)}, u32[]{:S(2)}) collective-permute-start(f32[64,1024]{1,0:T(8,128)S(1)} %add.21.a_ref), channel_id=1, source_target_pairs={{0,16},{1,17},{2,18},{3,19},{4,12},{5,13},{6,14},{7,15},{8,24},{9,... | collective-permute-start | bytes 786440 | tf_op jit(solution)/shard_map/ppermute | solution.py:300
  39.4 6.7 %collective-permute-start.14 = (f32[64,1024]{1,0:T(8,128)S(1)}, f32[64,1024]{1,0:T(8,128)S(1)}, u32[]{:S(2)}, u32[]{:S(2)}) collective-permute-start(f32[64,1024]{1,0:T(8,128)S(1)} %add.23.a_ref), channel_id=1, source_target_pairs={{0,16},{1,17},{2,18},{3,19},{4,12},{5,13},{6,14},{7,15},{8,24},{9,... | collective-permute-start | bytes 786440 | tf_op jit(solution)/shard_map/ppermute | solution.py:300
  42.3 7.8 %collective-permute-start.9 = (f32[128,512]{1,0:T(8,128)S(1)}, f32[128,512]{1,0:T(8,128)S(1)}, u32[]{:S(2)}, u32[]{:S(2)}) collective-permute-start(f32[128,512]{1,0:T(8,128)S(1)} %add.19.left_ref), channel_id=1, source_target_pairs={{0,1},{1,0},{2,3},{3,2},{4,6},{5,7},{6,4},{7,5},{8,9},{9,8},{10,11... | collective-permute-start | bytes 786440 | tf_op jit(solution)/shard_map/ppermute | solution.py:300
  44.2 3.0 %collective-permute-start.15 = (f32[32,1024]{1,0:T(8,128)S(1)}, f32[32,1024]{1,0:T(8,128)S(1)}, u32[]{:S(2)}, u32[]{:S(2)}) collective-permute-start(f32[32,1024]{1,0:T(8,128)S(1)} %get-tuple-element.49.refs_0_), channel_id=1, source_target_pairs={{0,4},{1,5},{2,6},{3,7},{4,0},{5,1},{6,2},{7,3},{8,12},{9,13},{10,... | collective-permute-start | bytes 393224 | tf_op jit(solution)/shard_map/ppermute | solution.py:300
  44.3 2.9 %collective-permute-start.16 = (f32[32,1024]{1,0:T(8,128)S(1)}, f32[32,1024]{1,0:T(8,128)S(1)}, u32[]{:S(2)}, u32[]{:S(2)}) collective-permute-start(f32[32,1024]{1,0:T(8,128)S(1)} %get-tuple-element.50.refs_1_), channel_id=1, source_target_pairs={{0,4},{1,5},{2,6},{3,7},{4,0},{5,1},{6,2},{7,3},{8,12},{9,13},{10,... | collective-permute-start | bytes 393224 | tf_op jit(solution)/shard_map/ppermute | solution.py:300
  46.1 1.5 %collective-permute-start.17 = (f32[32,1024]{1,0:T(8,128)S(1)}, f32[32,1024]{1,0:T(8,128)S(1)}, u32[]{:S(2)}, u32[]{:S(2)}) collective-permute-start(f32[32,1024]{1,0:T(8,128)S(1)} %get-tuple-element.52.refs_0_), channel_id=1, source_target_pairs={{0,4},{1,5},{2,6},{3,7},{4,0},{5,1},{6,2},{7,3},{8,12},{9,13},{10,... | collective-permute-start | bytes 393224 | tf_op jit(solution)/shard_map/ppermute | solution.py:300
  46.2 1.5 %collective-permute-start.18 = (f32[32,1024]{1,0:T(8,128)S(1)}, f32[32,1024]{1,0:T(8,128)S(1)}, u32[]{:S(2)}, u32[]{:S(2)}) collective-permute-start(f32[32,1024]{1,0:T(8,128)S(1)} %get-tuple-element.53.refs_1_), channel_id=1, source_target_pairs={{0,4},{1,5},{2,6},{3,7},{4,0},{5,1},{6,2},{7,3},{8,12},{9,13},{10,... | collective-permute-start | bytes 393224 | tf_op jit(solution)/shard_map/ppermute | solution.py:300
